TPU v7x, 128 devices: a whole 4x4x4 slice. The times are simulated.
128 devices in a mesh: orb: 32 (over z_hi, x, y), slab: 4 (over z_lo, core).
Axes of the slice: x: 4, y: 4, z: 4 (z_hi: 2, z_lo: 2; z = z_hi * 2 + z_lo), core: 2. Of those that a mesh axis runs over, the one named last changes fastest.
Arguments:
- orbitals: float32 [32, 2, 128, 32, 128], P('orb', None, None, 'slab'), may hold values from -7 to 7, as said below
- potential: float32 [128, 32, 128], P(None, 'slab'), may hold values from 0 to 2
- occupation: float32 [32], P('orb'), may hold values from 0.5 to 2
- e_field: float32 [3, 128, 32, 128], P(None, 'orb', 'slab'), may hold values from -3 to 3
- a_field: float32 [3, 128, 32, 128], P(None, 'orb', 'slab'), may hold values from -1.8 to 1.8
Outputs:
- orbitals_next: float32 [32, 2, 128, 32, 128], P('orb', None, None, 'slab')
- electric_field: float32 [3, 128, 32, 128], P(None, 'orb', 'slab')
- vector_potential: float32 [3, 128, 32, 128], P(None, 'orb', 'slab')
Inputs may be any that keep to these rules, and one draw needn't show every extreme that they name: `orbitals`: real and imaginary parts of each orbital at each cell.
All inputs are finite; a program needn't handle non-finite values.
Results may differ from a plain program's by a relative error of at most 0.0003.
Values sent between devices are 32-bit elements; how exact they have to be, the bound alone decides.
No kernel may reach another device: no remote copies, remote signals or barrier semaphores. Data moves between devices by JAX's collectives and lax.ppermute only.
A program may use at most 64 MiB of HBM per device.

v0:
```python
import functools

import jax
import jax.numpy as jnp
from jax import lax
from jax.experimental import pallas as pl
from jax.experimental.pallas import tpu as pltpu
from jax.sharding import PartitionSpec as P

TERMS = 4
STEPS = 2
TIME_STEP = 0.3
WAVE_STEP = 0.5
EPSILON = 1e-06

NX = 128
NY = 128
NZ = 32
ORBS = 32
SLABS = 4
CELLS = NX * NY * NZ
DEPTH = NZ // SLABS
ROWS = NX // ORBS
HALO = TERMS + 1
MARGIN = TERMS
WIDE = DEPTH + 2 * HALO
PAD = 8
XP = NX + 2 * PAD
PACK = 3 * DEPTH * ROWS
CHUNK = 32
F32 = jnp.float32

CORE_PAIRS = [(0, 1), (1, 0), (2, 3), (3, 2)]
CHIP_PAIRS = [(1, 2), (2, 1)]


def vmem():
    return pl.BlockSpec(memory_space=pltpu.VMEM)


def smem():
    return pl.BlockSpec(memory_space=pltpu.SMEM)


def call(body, outs, ins, scratch=(), flops=1000000, limit=40):
    shapes = [jax.ShapeDtypeStruct(s, F32) for s in outs]
    size = sum(4 * s.size for s in shapes)
    return pl.pallas_call(
        body,
        out_shape=shapes,
        in_specs=ins,
        out_specs=[vmem()] * len(outs),
        scratch_shapes=list(scratch),
        compiler_params=pltpu.CompilerParams(vmem_limit_bytes=limit * 1024 * 1024),
        cost_estimate=pl.CostEstimate(flops=flops, bytes_accessed=2 * size, transcendentals=0),
    )


def core_index():
    return lax.rem(lax.axis_index("slab"), 2)


def lane_shifts(value):
    lane = lax.broadcasted_iota(jnp.int32, value.shape, value.ndim - 1)
    plus = jnp.where(lane == NY - 1, 0.0, pltpu.roll(value, NY - 1, value.ndim - 1))
    minus = jnp.where(lane == 0, 0.0, pltpu.roll(value, 1, value.ndim - 1))
    return plus, minus


def half_rows(shape):
    return lax.broadcasted_iota(jnp.int32, shape, len(shape) - 2) % 8 < 4


def prepare_body(orb_ref, pot_ref, wide_ref, weight_ref, core_ref, chip_ref):
    core = core_index()
    for z in range(DEPTH):
        for part in range(2):
            wide_ref[z + 1, part, PAD : PAD + NX, :] = orb_ref[part, pl.ds(z, NX, stride=DEPTH), :]
        weight_ref[z] = 2.0 * pot_ref[pl.ds(z, NX, stride=DEPTH), :] + 6.0
    to_core = 1 + (1 - core) * (DEPTH - HALO)
    to_chip = 1 + core * (DEPTH - HALO)
    for i in range(HALO):
        for part in range(2):
            core_ref[2 * i + part] = wide_ref[to_core + i, part, PAD : PAD + NX, :]
            chip_ref[2 * i + part] = wide_ref[to_chip + i, part, PAD : PAD + NX, :]
    for i in range(MARGIN):
        core_ref[2 * HALO + i] = weight_ref[(1 - core) * (DEPTH - MARGIN) + i]
        chip_ref[2 * HALO + i] = weight_ref[core * (DEPTH - MARGIN) + i]


def prepare(orbitals, potential):
    planes = 2 * HALO + MARGIN
    return call(
        prepare_body,
        [(DEPTH + 2, 2, XP, NY), (DEPTH, NX, NY), (planes, NX, NY), (planes, NX, NY)],
        [vmem(), vmem()],
    )(orbitals.reshape(2, NX * DEPTH, NY), potential.reshape(NX * DEPTH, NY))


def rims_body(wide_ref, core_ref, chip_ref):
    core = core_index()
    to_core = 1 + (1 - core) * (DEPTH - HALO)
    to_chip = 1 + core * (DEPTH - HALO)
    for i in range(HALO):
        for part in range(2):
            core_ref[2 * i + part] = wide_ref[to_core + i, part, PAD : PAD + NX, :]
            chip_ref[2 * i + part] = wide_ref[to_chip + i, part, PAD : PAD + NX, :]


def rims(wide):
    return call(rims_body, [(2 * HALO, NX, NY)] * 2, [vmem()])(wide)


def spread_body(a_ref, e_ref, copies_ref, a_rows_ref, e_rows_ref):
    for comp in range(3):
        for z in range(DEPTH):
            rows = pl.ds((comp * DEPTH + z) * ROWS, ROWS)
            a_rows_ref[rows, :] = a_ref[comp, pl.ds(z, ROWS, stride=DEPTH), :]
            e_rows_ref[rows, :] = e_ref[comp, pl.ds(z, ROWS, stride=DEPTH), :]
    value = a_rows_ref[...]
    for i in range(ORBS):
        copies_ref[i] = value


def spread(a_field, e_field):
    flat = (3, ROWS * DEPTH, NY)
    return call(spread_body, [(ORBS, PACK, NY), (PACK, NY), (PACK, NY)], [vmem(), vmem()])(
        a_field.reshape(flat), e_field.reshape(flat)
    )


def assemble_body(got_ref, field_ref, core_ref, chip_ref):
    core = core_index()
    low = half_rows((ORBS // 2, 8, NY))
    for comp in range(3):
        for pair in range(DEPTH // 2):
            rows = pl.ds((comp * DEPTH + 2 * pair) * ROWS, 8)
            first = got_ref[:, 0, rows, :]
            second = got_ref[:, 1, rows, :]
            even = jnp.where(low, first, pltpu.roll(second, 4, 1))
            odd = jnp.where(low, pltpu.roll(first, 4, 1), second)
            field_ref[2 * pair, comp] = even.reshape(NX, NY)
            field_ref[2 * pair + 1, comp] = odd.reshape(NX, NY)
    for i in range(MARGIN):
        for comp in range(3):
            core_ref[i, comp] = field_ref[(1 - core) * (DEPTH - MARGIN) + i, comp]
            chip_ref[i, comp] = field_ref[core * (DEPTH - MARGIN) + i, comp]


def assemble(got):
    return call(
        assemble_body,
        [(DEPTH, 3, NX, NY), (MARGIN, 3, NX, NY), (MARGIN, 3, NX, NY)],
        [vmem()],
    )(got.reshape(ORBS // 2, 2, PACK, NY))


def propagate_body(
    scale_ref, wide_ref, hcore_ref, hchip_ref, weight_ref, vcore_ref, vchip_ref, field_ref, acore_ref, achip_ref,
    out_ref, norm_ref, ping_ref, pong_ref, w_ref, a_ref,
):
    core = core_index()
    scale = scale_ref[0:1, :]
    edge = jnp.zeros((PAD, NY), F32)

    def clear(ref, count):
        @pl.loop(0, count)
        def _(j):
            for part in range(2):
                ref[j, part, 0:PAD, :] = edge
                ref[j, part, PAD + NX : XP, :] = edge

    clear(ping_ref, WIDE)
    clear(pong_ref, WIDE)
    clear(out_ref, DEPTH + 2)

    def put_field(j, plane, base):
        total = base
        for comp in range(3):
            value = plane[comp]
            a_ref[j, comp] = value
            total = total + value * value
        w_ref[j] = total

    @pl.loop(0, DEPTH)
    def _(z):
        for part in range(2):
            ping_ref[z + HALO, part, PAD : PAD + NX, :] = wide_ref[z + 1, part, PAD : PAD + NX, :] * scale
        put_field(z + MARGIN, field_ref[z], weight_ref[z])

    def put_halo(start, width, orb_ref, pot_ref, fld_ref):
        @pl.loop(0, HALO)
        def _(i):
            for part in range(2):
                ping_ref[start * (DEPTH + HALO) + i, part, PAD : PAD + NX, :] = orb_ref[2 * i + part] * scale

        @pl.loop(0, MARGIN)
        def _(i):
            put_field(start * (DEPTH + MARGIN) + i, fld_ref[i], pot_ref[i])

    @pl.when(core == 1)
    def _():
        put_halo(0, 0, hcore_ref, vcore_ref, acore_ref)
        put_halo(1, 0, hchip_ref, vchip_ref, achip_ref)

    @pl.when(core == 0)
    def _():
        put_halo(1, 0, hcore_ref, vcore_ref, acore_ref)
        put_halo(0, 0, hchip_ref, vchip_ref, achip_ref)

    slab = lax.axis_index("slab")
    source, target = ping_ref, pong_ref
    norm_ref[...] = jnp.zeros((8, NY), F32)
    for order in range(1, TERMS + 1):

        @pl.loop(order, WIDE - order)
        def _(j, order=order, source=source, target=target):
            depth = slab * DEPTH + j - HALO
            inside = jnp.where((depth >= 0) & (depth < NZ), 1.0, 0.0).astype(F32)
            factor = inside * (0.5 * TIME_STEP / order)
            own = j - HALO + 1
            squares = jnp.zeros((8, NY), F32)
            for r in range(0, NX, CHUNK):
                here = pl.ds(PAD + r, CHUNK)
                centre, total, drift = [], [], []
                fields = [a_ref[j - 1, comp, r : r + CHUNK, :] for comp in range(3)]
                for part in range(2):
                    mid = source[j, part, here, :]
                    xp = source[j, part, pl.ds(PAD + r + 1, CHUNK), :]
                    xm = source[j, part, pl.ds(PAD + r - 1, CHUNK), :]
                    zp = source[j + 1, part, here, :]
                    zm = source[j - 1, part, here, :]
                    yp, ym = lane_shifts(mid)
                    centre.append(mid)
                    total.append((xp + xm) + (yp + ym) + (zp + zm))
                    drift.append(fields[0] * (xp - xm) + fields[1] * (yp - ym) + fields[2] * (zp - zm))
                weight = w_ref[j - 1, r : r + CHUNK, :]
                real_h = weight * centre[0] - total[0] + drift[1]
                imag_h = weight * centre[1] - total[1] - drift[0]
                new = (factor * imag_h, -factor * real_h)
                if order < TERMS:
                    for part in range(2):
                        target[j, part, here, :] = new[part]
                if order == 1:

                    @pl.when((own >= 0) & (own < DEPTH + 2))
                    def _():
                        for part in range(2):
                            out_ref[own, part, here, :] = centre[part] + new[part]
                elif order < TERMS:

                    @pl.when((own >= 0) & (own < DEPTH + 2))
                    def _():
                        for part in range(2):
                            out_ref[own, part, here, :] += new[part]
                else:
                    for part in range(2):
                        moved = out_ref[own, part, here, :] + new[part]
                        out_ref[own, part, here, :] = moved
                        squares = squares + (moved * moved).reshape(CHUNK // 8, 8, NY).sum(0)
            if order == TERMS:

                @pl.when((own >= 1) & (own < DEPTH + 1))
                def _():
                    norm_ref[...] += squares

        source, target = target, source


def propagate(scale, wide, hcore, hchip, weight, vcore, vchip, field, acore, achip):
    return call(
        propagate_body,
        [(DEPTH + 2, 2, XP, NY), (8, NY)],
        [vmem()] * 10,
        [
            pltpu.VMEM((WIDE, 2, XP, NY), F32),
            pltpu.VMEM((WIDE, 2, XP, NY), F32),
            pltpu.VMEM((DEPTH + 2 * MARGIN, NX, NY), F32),
            pltpu.VMEM((DEPTH + 2 * MARGIN, 3, NX, NY), F32),
        ],
        flops=60000000,
    )(scale, wide, hcore, hchip, weight, vcore, vchip, field, acore, achip)


def current_body(wide_ref, field_ref, flow_ref):
    low = half_rows((CHUNK // 8, 8, NY))

    @pl.loop(0, DEPTH // 2)
    def _(pair):
        for r in range(0, NX, CHUNK):
            both = []
            for z in range(2):
                j = 2 * pair + z + 1
                here = pl.ds(PAD + r, CHUNK)
                mids, grads = [], []
                for part in range(2):
                    mid = wide_ref[j, part, here, :]
                    yp, ym = lane_shifts(mid)
                    mids.append(mid)
                    grads.append(
                        (
                            wide_ref[j, part, pl.ds(PAD + r + 1, CHUNK), :]
                            - wide_ref[j, part, pl.ds(PAD + r - 1, CHUNK), :],
                            yp - ym,
                            wide_ref[j + 1, part, here, :] - wide_ref[j - 1, part, here, :],
                        )
                    )
                u, w = mids
                density = u * u + w * w
                both.append(
                    [
                        0.5 * (u * grads[1][comp] - w * grads[0][comp])
                        + field_ref[j - 1, comp, r : r + CHUNK, :] * density
                        for comp in range(3)
                    ]
                )
            tiles = pl.ds(r // 8, CHUNK // 8)
            for comp in range(3):
                even = both[0][comp].reshape(CHUNK // 8, 8, NY)
                odd = both[1][comp].reshape(CHUNK // 8, 8, NY)
                rows = pl.ds(pl.multiple_of((comp * DEPTH + 2 * pair) * ROWS, 8), 8)
                flow_ref[tiles, 0, rows, :] = jnp.where(low, even, pltpu.roll(odd, 4, 1))
                flow_ref[tiles, 1, rows, :] = jnp.where(low, pltpu.roll(even, 4, 1), odd)


def current(wide, field):
    return call(current_body, [(ORBS // 2, 2, PACK, NY)], [vmem(), vmem()], flops=10000000)(wide, field)[0]


def weigh_body(occ_ref, n0_ref, n1_ref, n2_ref, n3_ref, flow_ref, out_ref, scale_ref):
    sums = (n0_ref[...] + n1_ref[...]) + (n2_ref[...] + n3_ref[...])
    norm = jnp.sum(jnp.sum(sums, axis=1, keepdims=True), axis=0, keepdims=True)
    mean = norm * (1.0 / CELLS) + EPSILON
    scale = 1.0 / jnp.sqrt(mean)
    scale_ref[...] = jnp.broadcast_to(scale, (8, NY))
    weight = jnp.broadcast_to(scale * scale * (occ_ref[0] * (1.0 / ORBS)), (1, NY))

    @pl.loop(0, ORBS // 2)
    def _(i):
        for side in range(2):
            out_ref[i, side] = flow_ref[i, side] * weight


def weigh(occupation, norms, flow):
    return call(
        weigh_body, [(ORBS // 2, 2, PACK, NY), (8, NY)], [smem()] + [vmem()] * 5, flops=500000
    )(occupation, *norms, flow)


def curl_body(field_ref, acore_ref, achip_ref, out_ref):
    core = core_index()
    owner = lax.axis_index("orb")
    tile = owner // 2
    odd = lax.rem(owner, 2)
    row = lax.broadcasted_iota(jnp.int32, (8, NY), 0)
    keep = ((owner > 0) | (row != 0)) & ((owner < ORBS - 1) | (row != ROWS + 1))
    starts = [pl.multiple_of(8 * jnp.clip(tile + k, 0, NX // 8 - 1), 8) for k in (-1, 0, 1)]

    def window(load):
        before, middle, after = [load(pl.ds(s, 8)) for s in starts]
        first = jnp.where(odd == 1, middle, before)
        second = jnp.where(odd == 1, after, middle)
        shift_first = jnp.where(odd == 1, pltpu.roll(first, 5, 0), pltpu.roll(first, 1, 0))
        shift_second = jnp.where(odd == 1, pltpu.roll(second, 5, 0), pltpu.roll(second, 1, 0))
        split = jnp.where(odd == 1, 5, 1)
        return jnp.where(keep, jnp.where(row < split, shift_first, shift_second), 0.0)

    def x_plus(v):
        return pltpu.roll(v, 7, 0)

    def x_minus(v):
        return pltpu.roll(v, 1, 0)

    planes = []
    for z in range(-1, DEPTH + 1):
        comps = []
        for comp in range(3):
            if z < 0:
                value = jnp.where(
                    core == 1,
                    window(lambda r: acore_ref[MARGIN - 1, comp, r, :]),
                    window(lambda r: achip_ref[MARGIN - 1, comp, r, :]),
                )
            elif z < DEPTH:
                value = window(lambda r: field_ref[z, comp, r, :])
            else:
                value = jnp.where(
                    core == 0,
                    window(lambda r: acore_ref[0, comp, r, :]),
                    window(lambda r: achip_ref[0, comp, r, :]),
                )
            comps.append(value)
        planes.append(comps)
    for z in range(DEPTH):
        ax, ay, az = planes[z + 1]
        axm, aym, azm = planes[z]
        axp, ayp, azp = planes[z + 2]
        ax_up, ax_dn = lane_shifts(ax)
        ay_dn = lane_shifts(ay)[1]
        az_up, az_dn = lane_shifts(az)
        dy_ay = ay - ay_dn
        dx_ax = ax - x_minus(ax)
        inner_x = dy_ay + (az - azm)
        inner_y = dx_ax + (az - azm)
        inner_z = dx_ax + dy_ay
        up_inner_z = (axp - x_minus(axp)) + (ayp - lane_shifts(ayp)[1])
        out_x = (x_plus(inner_x) - inner_x) - (ax_up + ax_dn + axp + axm - 4.0 * ax)
        out_y = (lane_shifts(inner_y)[0] - inner_y) - (x_plus(ay) + x_minus(ay) + ayp + aym - 4.0 * ay)
        out_z = (up_inner_z - inner_z) - (x_plus(az) + x_minus(az) + az_up + az_dn - 4.0 * az)
        for comp, value in enumerate((out_x, out_y, out_z)):
            out_ref[pl.ds((comp * DEPTH + z) * ROWS, ROWS), :] = pltpu.roll(value, 7, 0)[0:ROWS]


def double_curl(field, acore, achip):
    return call(curl_body, [(PACK, NY)], [vmem()] * 3, flops=1000000)(field, acore, achip)[0]


def update_body(last, got_ref, curl_ref, e_ref, a_ref, *outs):
    total = got_ref[0]
    for i in range(1, ORBS):
        total = total + got_ref[i]
    e_new = e_ref[...] + WAVE_STEP * (curl_ref[...] - total)
    a_new = a_ref[...] - WAVE_STEP * e_new
    if last:
        for ref, value in zip(outs, (e_new, a_new)):
            for comp in range(3):
                for z in range(DEPTH):
                    start = (comp * DEPTH + z) * ROWS
                    ref[comp, pl.ds(z, ROWS, stride=DEPTH), :] = value[start : start + ROWS]
    else:
        copies_ref, a_out_ref, e_out_ref = outs
        a_out_ref[...] = a_new
        e_out_ref[...] = e_new
        for i in range(ORBS):
            copies_ref[i] = a_new


def update(last, got, curl, e_rows, a_rows):
    if last:
        outs = [(3, ROWS * DEPTH, NY)] * 2
    else:
        outs = [(ORBS, PACK, NY), (PACK, NY), (PACK, NY)]
    return call(functools.partial(update_body, last), outs, [vmem()] * 4, flops=500000)(got, curl, e_rows, a_rows)


def finish_body(scale_ref, wide_ref, out_ref):
    scale = scale_ref[0:1, :]
    for z in range(DEPTH):
        for part in range(2):
            out_ref[part, pl.ds(z, NX, stride=DEPTH), :] = wide_ref[z + 1, part, PAD : PAD + NX, :] * scale


def finish(scale, wide):
    return call(finish_body, [(2, NX * DEPTH, NY)], [vmem()] * 2)(scale, wide)[0]


def everyone(copies):
    return lax.all_to_all(copies, "orb", 0, 0, tiled=True)


def per_device(orbitals, potential, occupation, e_field, a_field):
    copies, a_rows, e_rows = spread(a_field, e_field)
    got = everyone(copies)
    wide, weight, core_send, chip_send = prepare(orbitals, potential)
    hcore = lax.ppermute(core_send, "slab", CORE_PAIRS)
    hchip = lax.ppermute(chip_send, "slab", CHIP_PAIRS)
    vcore, vchip = hcore[2 * HALO :], hchip[2 * HALO :]
    scale = jnp.ones((8, NY), F32)
    for step in range(STEPS):
        last = step == STEPS - 1
        field, acore_send, achip_send = assemble(got)
        acore = lax.ppermute(acore_send, "slab", CORE_PAIRS)
        achip = lax.ppermute(achip_send, "slab", CHIP_PAIRS)
        wide, norm = propagate(scale, wide, hcore, hchip, weight, vcore, vchip, field, acore, achip)
        norms = [norm] + [lax.ppermute(norm, "slab", [(i, i ^ k) for i in range(SLABS)]) for k in (1, 2, 3)]
        flow = current(wide, field)
        flow, scale = weigh(occupation, norms, flow)
        flows = everyone(flow.reshape(ORBS, PACK, NY))
        curl = double_curl(field, acore, achip)
        if not last:
            core_send, chip_send = rims(wide)
            hcore = lax.ppermute(core_send, "slab", CORE_PAIRS)
            hchip = lax.ppermute(chip_send, "slab", CHIP_PAIRS)
            copies, a_rows, e_rows = update(last, flows, curl, e_rows, a_rows)
            got = everyone(copies)
        else:
            e_new, a_new = update(last, flows, curl, e_rows, a_rows)
            orbitals = finish(scale, wide)
    return (
        orbitals.reshape(1, 2, NX, DEPTH, NY),
        e_new.reshape(3, ROWS, DEPTH, NY),
        a_new.reshape(3, ROWS, DEPTH, NY),
    )


def solution(mesh):
    return jax.shard_map(
        per_device,
        mesh=mesh,
        in_specs=(
            P("orb", None, None, "slab", None),
            P(None, "slab", None),
            P("orb"),
            P(None, "orb", "slab", None),
            P(None, "orb", "slab", None),
        ),
        out_specs=(
            P("orb", None, None, "slab", None),
            P(None, "orb", "slab", None),
            P(None, "orb", "slab", None),
        ),
        check_vma=False,
    )
```

profile of v0, /device:TPU:0, one launch (start us, length us, event | category | flops | bytes accessed | tf_op | source)
XLA Modules:
  0.0 213.8 jit_solution(4121337872415510027)
XLA Ops:
  0.6 0.8 copy-done.21
  1.4 0.8 copy-done.22
  2.2 1.3 shard_map.77
  3.5 10.9 %all-to-all-start = ((f32[32,96,128]{2,1,0:T(8,128)}), f32[32,96,128]{2,1,0:T(8,128)S(1)}, u32[]{:S(2)}, u32[]{:S(2)}) async-start(f32[32,96,128]{2,1,0:T(8,128)} %get-tuple-element.35), calls=%async_computation | async-start | bytes 3145728 | tf_op jit(solution)/shard_map/all_to_all | solution.py:458
  14.4 1.7 shard_map.76
  16.1 0.8 copy-done.12
  16.9 1.1 copy-done.17
  18.1 0.0 collective-permute-start
  18.1 1.6 collective-permute-start.1
  19.7 18.2 %all-to-all-done = f32[32,96,128]{2,1,0:T(8,128)S(1)} async-done(((f32[32,96,128]{2,1,0:T(8,128)}), f32[32,96,128]{2,1,0:T(8,128)S(1)}, u32[]{:S(2)}, u32[]{:S(2)}) %all-to-all-start) | async-done | bytes 1572896 | tf_op jit(solution)/shard_map/all_to_all | solution.py:458
  37.9 0.3 shard_map.78
  38.2 0.1 collective-permute-start.2
  38.3 0.8 collective-permute-start.3
  39.2 1.0 slice.8.vcore_ref
  40.2 0.0 collective-permute-done.1.hchip_ref
  40.2 1.0 slice.9.vchip_ref
  41.2 0.0 collective-permute-done.2.acore_ref
  41.2 0.0 copy-start.6
  41.2 19.9 %shard_map.79 = (f32[10,2,144,128]{3,2,1,0:T(8,128)S(1)}, f32[8,128]{1,0:T(8,128)S(1)}) custom-call(f32[8,128]{1,0:T(8,128)S(1)} %broadcast_in_dim.3.scale_ref, f32[10,2,144,128]{3,2,1,0:T(8,128)S(1)} %copy-done.18, f32[14,128,128]{2,1,0:T(8,128)} %collective-permute-done.hcore_ref, f32[14,128,128]{2,1,0:T(8,128)} %collective-permute-done.1.hchip_ref, ...), custom_call_target="tpu_custom_call" | custom-call | flops 60000000 | bytes 2957312 | tf_op jit(solution)/shard_map/pallas_call | solution.py:271
  61.2 11.0 %collective-permute-start.4 = (f32[8,128]{1,0:T(8,128)S(1)}, f32[8,128]{1,0:T(8,128)S(1)}, u32[]{:S(2)}, u32[]{:S(2)}) collective-permute-start(f32[8,128]{1,0:T(8,128)S(1)} %get-tuple-element.39.n0_ref), channel_id=1, source_target_pairs={{0,1},{1,0},{2,3},{3,2},{4,5},{5,4},{6,7},{7,6},{8,9},{9,8},{10,11... | collective-permute-start | bytes 12296 | tf_op jit(solution)/shard_map/ppermute | solution.py:475
  72.1 1.3 collective-permute-start.5
  73.4 0.2 collective-permute-start.6
  74.2 0.9 shard_map.80.flow_ref
  75.1 0.6 collective-permute-done.5.n2_ref
  75.7 0.7 collective-permute-done.6.n3_ref
  76.5 0.2 shard_map.81
  76.7 0.0 copy-start.23
  76.7 1.1 copy-done.16
  77.9 8.4 %all-to-all-start.1 = ((f32[32,96,128]{2,1,0:T(8,128)}), f32[32,96,128]{2,1,0:T(8,128)}, u32[]{:S(2)}, u32[]{:S(2)}) async-start(f32[32,96,128]{2,1,0:T(8,128)} %bitcast.14), calls=%async_computation.1 | async-start | bytes 3145728 | tf_op jit(solution)/shard_map/all_to_all | solution.py:458
  86.3 0.0 copy-start.7
  86.3 1.1 copy-done.7
  87.4 1.1 copy-done.9
  88.5 0.1 shard_map.83.curl_ref
  88.7 21.3 %all-to-all-done.1.got_ref = f32[32,96,128]{2,1,0:T(8,128)} async-done(((f32[32,96,128]{2,1,0:T(8,128)}), f32[32,96,128]{2,1,0:T(8,128)}, u32[]{:S(2)}, u32[]{:S(2)}) %all-to-all-start.1) | async-done | bytes 1572896 | tf_op jit(solution)/shard_map/all_to_all | solution.py:458
  110.0 1.6 shard_map.84
  111.7 29.0 %all_to_all.20 = f32[32,96,128]{2,1,0:T(8,128)S(1)} all-to-all(f32[32,96,128]{2,1,0:T(8,128)S(1)} %get-tuple-element.47), channel_id=1, replica_groups=mesh['orb'=32,'slab'=4] {'orb'}, dimensions={0} | all-to-all | bytes 3145728 | tf_op jit(solution)/shard_map/all_to_all | solution.py:458
  140.6 0.3 shard_map.85
  140.9 0.7 collective-permute-start.10
  141.7 2.1 collective-permute-start.9
  143.8 0.1 shard_map.82
  143.8 0.1 collective-permute-start.7
  144.0 0.7 collective-permute-start.8
  144.7 2.0 collective-permute-done.7.hcore_ref
  146.6 0.0 collective-permute-done.8.hchip_ref
  146.6 0.0 collective-permute-done.10.achip_ref
  146.6 0.0 collective-permute-done.9.acore_ref
  146.6 0.0 copy-start.4
  146.7 17.9 %shard_map.86 = (f32[10,2,144,128]{3,2,1,0:T(8,128)S(1)}, f32[8,128]{1,0:T(8,128)S(1)}) custom-call(f32[8,128]{1,0:T(8,128)S(1)} %copy-done.24, f32[10,2,144,128]{3,2,1,0:T(8,128)S(1)} %get-tuple-element.40.wide_ref, f32[10,128,128]{2,1,0:T(8,128)S(1)} %collective-permute-done.7.hcore_ref, f32[10,128,128]{2,1,0:T(8,128)S(1)} %collective-permute-done.8.hchip_ref, ...), custom_call_target="tpu_custom_call" | custom-call | flops 60000000 | bytes 2957312 | tf_op jit(solution)/shard_map/pallas_call | solution.py:271
  164.6 13.8 %collective-permute-start.11 = (f32[8,128]{1,0:T(8,128)S(1)}, f32[8,128]{1,0:T(8,128)S(1)}, u32[]{:S(2)}, u32[]{:S(2)}) collective-permute-start(f32[8,128]{1,0:T(8,128)S(1)} %get-tuple-element.51.n0_ref), channel_id=1, source_target_pairs={{0,1},{1,0},{2,3},{3,2},{4,5},{5,4},{6,7},{7,6},{8,9},{9,8},{10,11... | collective-permute-start | bytes 12296 | tf_op jit(solution)/shard_map/ppermute | solution.py:475
  178.4 1.7 collective-permute-start.12
  180.1 0.1 collective-permute-start.13
  180.2 0.9 shard_map.87.flow_ref
  181.1 0.9 collective-permute-done.12.n2_ref
  182.0 1.1 collective-permute-done.13.n3_ref
  183.2 0.2 shard_map.88
  183.4 1.2 copy-done.15
  184.6 4.7 %all-to-all-start.3 = ((f32[32,96,128]{2,1,0:T(8,128)}), f32[32,96,128]{2,1,0:T(8,128)S(1)}, u32[]{:S(2)}, u32[]{:S(2)}) async-start(f32[32,96,128]{2,1,0:T(8,128)} %bitcast.13), calls=%async_computation.3 | async-start | bytes 3145728 | tf_op jit(solution)/shard_map/all_to_all | solution.py:458
  189.3 1.1 copy-done.3
  190.5 1.1 copy-done.5
  191.6 0.1 shard_map.90.curl_ref
  191.7 1.2 copy-done.1
  193.0 1.3 shard_map.89
  194.2 18.9 %all-to-all-done.3.got_ref = f32[32,96,128]{2,1,0:T(8,128)S(1)} async-done(((f32[32,96,128]{2,1,0:T(8,128)}), f32[32,96,128]{2,1,0:T(8,128)S(1)}, u32[]{:S(2)}, u32[]{:S(2)}) %all-to-all-start.3) | async-done | bytes 1572896 | tf_op jit(solution)/shard_map/all_to_all | solution.py:458
  213.1 0.7 shard_map.91
  (40 shorter events, 0.1 us)
Async XLA Ops:
  0.6 0.8 copy-start.21
  1.4 0.8 copy-start.22
  3.5 10.9 %copy-start.19 = (f32[1,2,128,8,128]{4,3,2,1,0:T(8,128)S(1)}, f32[1,2,128,8,128]{4,3,2,1,0:T(8,128)}, u32[]{:S(2)}) copy-start(f32[1,2,128,8,128]{4,3,2,1,0:T(8,128)} %param.5) | copy-start | bytes 3145732
  3.5 10.9 %copy-start.20 = (f32[128,8,128]{2,1,0:T(8,128)S(1)}, f32[128,8,128]{2,1,0:T(8,128)}, u32[]{:S(2)}) copy-start(f32[128,8,128]{2,1,0:T(8,128)} %param.6) | copy-start | bytes 1572868
  3.5 34.4 %all-to-all-start = ((f32[32,96,128]{2,1,0:T(8,128)}), f32[32,96,128]{2,1,0:T(8,128)S(1)}, u32[]{:S(2)}, u32[]{:S(2)}) async-start(f32[32,96,128]{2,1,0:T(8,128)} %get-tuple-element.35), calls=%async_computation | async-start | bytes 3145728 | tf_op jit(solution)/shard_map/all_to_all | solution.py:458
  16.1 0.8 copy-start.12
  16.9 1.1 copy-start.17
  18.1 21.1 %collective-permute-start = (f32[14,128,128]{2,1,0:T(8,128)}, f32[14,128,128]{2,1,0:T(8,128)}, u32[]{:S(2)}, u32[]{:S(2)}) collective-permute-start(f32[14,128,128]{2,1,0:T(8,128)} %get-tuple-element.32), channel_id=1, source_target_pairs={{0,1},{1,0},{2,3},{3,2},{4,5},{5,4},{6,7},{7,6},{8,9},{9,8},{10,11... | collective-permute-start | bytes 2752520 | tf_op jit(solution)/shard_map/ppermute | solution.py:465
  18.1 22.1 %collective-permute-start.1 = (f32[14,128,128]{2,1,0:T(8,128)}, f32[14,128,128]{2,1,0:T(8,128)}, u32[]{:S(2)}, u32[]{:S(2)}) collective-permute-start(f32[14,128,128]{2,1,0:T(8,128)} %get-tuple-element.33), channel_id=1, source_target_pairs={{1,2},{2,1},{5,6},{6,5},{9,10},{10,9},{13,14},{14,13},{17,18},{18,... | collective-permute-start | bytes 2752520 | tf_op jit(solution)/shard_map/ppermute | solution.py:466
  37.9 3.3 %copy-start.13 = (f32[8,128,128]{2,1,0:T(8,128)S(1)}, f32[8,128,128]{2,1,0:T(8,128)}, u32[]{:S(2)}) copy-start(f32[8,128,128]{2,1,0:T(8,128)} %copy-done.12) | copy-start | bytes 1572868
  37.9 3.3 %copy-start.18 = (f32[10,2,144,128]{3,2,1,0:T(8,128)S(1)}, f32[10,2,144,128]{3,2,1,0:T(8,128)}, u32[]{:S(2)}) copy-start(f32[10,2,144,128]{3,2,1,0:T(8,128)} %copy-done.17) | copy-start | bytes 4423684
  38.2 2.9 %collective-permute-start.2 = (f32[4,3,128,128]{3,2,1,0:T(8,128)S(1)}, f32[4,3,128,128]{3,2,1,0:T(8,128)S(1)}, u32[]{:S(2)}, u32[]{:S(2)}) collective-permute-start(f32[4,3,128,128]{3,2,1,0:T(8,128)S(1)} %get-tuple-element.37), channel_id=1, source_target_pairs={{0,1},{1,0},{2,3},{3,2},{4,5},{5,4},{6,7},{7,6},{8,9},{9,8},{10,11... | collective-permute-start | bytes 2359304 | tf_op jit(solution)/shard_map/ppermute | solution.py:472
  38.3 2.9 %collective-permute-start.3 = (f32[4,3,128,128]{3,2,1,0:T(8,128)S(1)}, f32[4,3,128,128]{3,2,1,0:T(8,128)S(1)}, u32[]{:S(2)}, u32[]{:S(2)}) collective-permute-start(f32[4,3,128,128]{3,2,1,0:T(8,128)S(1)} %get-tuple-element.38), channel_id=1, source_target_pairs={{1,2},{2,1},{5,6},{6,5},{9,10},{10,9},{13,14},{14,13},{17,18},{18,... | collective-permute-start | bytes 2359304 | tf_op jit(solution)/shard_map/ppermute | solution.py:473
  41.1 20.0 %copy-start.10 = (f32[4,128,128]{2,1,0:T(8,128)}, f32[4,128,128]{2,1,0:T(8,128)S(1)}, u32[]{:S(2)}) copy-start(f32[4,128,128]{2,1,0:T(8,128)S(1)} %slice.9.vchip_ref) | copy-start | bytes 786436
  41.2 20.0 %copy-start.6 = (f32[4,3,128,128]{3,2,1,0:T(8,128)}, f32[4,3,128,128]{3,2,1,0:T(8,128)S(1)}, u32[]{:S(2)}) copy-start(f32[4,3,128,128]{3,2,1,0:T(8,128)S(1)} %collective-permute-done.2.acore_ref) | copy-start | bytes 2359300
  41.2 20.0 %copy-start.8 = (f32[4,3,128,128]{3,2,1,0:T(8,128)}, f32[4,3,128,128]{3,2,1,0:T(8,128)S(1)}, u32[]{:S(2)}) copy-start(f32[4,3,128,128]{3,2,1,0:T(8,128)S(1)} %collective-permute-done.3.achip_ref) | copy-start | bytes 2359300
  61.2 13.9 %collective-permute-start.4 = (f32[8,128]{1,0:T(8,128)S(1)}, f32[8,128]{1,0:T(8,128)S(1)}, u32[]{:S(2)}, u32[]{:S(2)}) collective-permute-start(f32[8,128]{1,0:T(8,128)S(1)} %get-tuple-element.39.n0_ref), channel_id=1, source_target_pairs={{0,1},{1,0},{2,3},{3,2},{4,5},{5,4},{6,7},{7,6},{8,9},{9,8},{10,11... | collective-permute-start | bytes 12296 | tf_op jit(solution)/shard_map/ppermute | solution.py:475
  72.1 3.6 %collective-permute-start.5 = (f32[8,128]{1,0:T(8,128)S(1)}, f32[8,128]{1,0:T(8,128)S(1)}, u32[]{:S(2)}, u32[]{:S(2)}) collective-permute-start(f32[8,128]{1,0:T(8,128)S(1)} %get-tuple-element.39.n0_ref), channel_id=1, source_target_pairs={{0,2},{1,3},{2,0},{3,1},{4,6},{5,7},{6,4},{7,5},{8,10},{9,11},{10,... | collective-permute-start | bytes 12296 | tf_op jit(solution)/shard_map/ppermute | solution.py:475
  73.4 3.0 %collective-permute-start.6 = (f32[8,128]{1,0:T(8,128)S(1)}, f32[8,128]{1,0:T(8,128)S(1)}, u32[]{:S(2)}, u32[]{:S(2)}) collective-permute-start(f32[8,128]{1,0:T(8,128)S(1)} %get-tuple-element.39.n0_ref), channel_id=1, source_target_pairs={{0,3},{1,2},{2,1},{3,0},{4,7},{5,6},{6,5},{7,4},{8,11},{9,10},{10,... | collective-permute-start | bytes 12296 | tf_op jit(solution)/shard_map/ppermute | solution.py:475
  76.7 1.1 copy-start.16
  76.7 1.1 copy-start.23
  77.9 32.2 %all-to-all-start.1 = ((f32[32,96,128]{2,1,0:T(8,128)}), f32[32,96,128]{2,1,0:T(8,128)}, u32[]{:S(2)}, u32[]{:S(2)}) async-start(f32[32,96,128]{2,1,0:T(8,128)} %bitcast.14), calls=%async_computation.1 | async-start | bytes 3145728 | tf_op jit(solution)/shard_map/all_to_all | solution.py:458
  86.3 1.1 copy-start.7
  87.4 1.1 copy-start.9
  140.6 6.0 %copy-start.11 = (f32[4,128,128]{2,1,0:T(8,128)S(1)}, f32[4,128,128]{2,1,0:T(8,128)}, u32[]{:S(2)}) copy-start(f32[4,128,128]{2,1,0:T(8,128)} %copy-done.10) | copy-start | bytes 786436
  140.6 6.0 %copy-start.14 = (f32[8,128,128]{2,1,0:T(8,128)S(1)}, f32[8,128,128]{2,1,0:T(8,128)}, u32[]{:S(2)}) copy-start(f32[8,128,128]{2,1,0:T(8,128)} %copy-done.12) | copy-start | bytes 1572868
  140.6 6.0 %copy-start.24 = (f32[8,128]{1,0:T(8,128)S(1)}, f32[8,128]{1,0:T(8,128)}, u32[]{:S(2)}) copy-start(f32[8,128]{1,0:T(8,128)} %copy-done.23) | copy-start | bytes 12292
  140.9 5.7 %collective-permute-start.10 = (f32[4,3,128,128]{3,2,1,0:T(8,128)S(1)}, f32[4,3,128,128]{3,2,1,0:T(8,128)S(1)}, u32[]{:S(2)}, u32[]{:S(2)}) collective-permute-start(f32[4,3,128,128]{3,2,1,0:T(8,128)S(1)} %get-tuple-element.50), channel_id=1, source_target_pairs={{1,2},{2,1},{5,6},{6,5},{9,10},{10,9},{13,14},{14,13},{17,18},{18,... | collective-permute-start | bytes 2359304 | tf_op jit(solution)/shard_map/ppermute | solution.py:473
  141.7 5.0 %collective-permute-start.9 = (f32[4,3,128,128]{3,2,1,0:T(8,128)S(1)}, f32[4,3,128,128]{3,2,1,0:T(8,128)S(1)}, u32[]{:S(2)}, u32[]{:S(2)}) collective-permute-start(f32[4,3,128,128]{3,2,1,0:T(8,128)S(1)} %get-tuple-element.49), channel_id=1, source_target_pairs={{0,1},{1,0},{2,3},{3,2},{4,5},{5,4},{6,7},{7,6},{8,9},{9,8},{10,11... | collective-permute-start | bytes 2359304 | tf_op jit(solution)/shard_map/ppermute | solution.py:472
  143.8 2.8 %collective-permute-start.7 = (f32[10,128,128]{2,1,0:T(8,128)S(1)}, f32[10,128,128]{2,1,0:T(8,128)S(1)}, u32[]{:S(2)}, u32[]{:S(2)}) collective-permute-start(f32[10,128,128]{2,1,0:T(8,128)S(1)} %get-tuple-element.42), channel_id=1, source_target_pairs={{0,1},{1,0},{2,3},{3,2},{4,5},{5,4},{6,7},{7,6},{8,9},{9,8},{10,11... | collective-permute-start | bytes 1966088 | tf_op jit(solution)/shard_map/ppermute | solution.py:482
  144.0 2.7 %collective-permute-start.8 = (f32[10,128,128]{2,1,0:T(8,128)S(1)}, f32[10,128,128]{2,1,0:T(8,128)S(1)}, u32[]{:S(2)}, u32[]{:S(2)}) collective-permute-start(f32[10,128,128]{2,1,0:T(8,128)S(1)} %get-tuple-element.43), channel_id=1, source_target_pairs={{1,2},{2,1},{5,6},{6,5},{9,10},{10,9},{13,14},{14,13},{17,18},{18,... | collective-permute-start | bytes 1966088 | tf_op jit(solution)/shard_map/ppermute | solution.py:483
  146.6 18.0 %copy-start.2 = (f32[4,3,128,128]{3,2,1,0:T(8,128)}, f32[4,3,128,128]{3,2,1,0:T(8,128)S(1)}, u32[]{:S(2)}) copy-start(f32[4,3,128,128]{3,2,1,0:T(8,128)S(1)} %collective-permute-done.10.achip_ref) | copy-start | bytes 2359300
  146.6 18.0 %copy-start.4 = (f32[4,3,128,128]{3,2,1,0:T(8,128)}, f32[4,3,128,128]{3,2,1,0:T(8,128)S(1)}, u32[]{:S(2)}) copy-start(f32[4,3,128,128]{3,2,1,0:T(8,128)S(1)} %collective-permute-done.9.acore_ref) | copy-start | bytes 2359300
  164.6 16.5 %copy-start = (f32[10,2,144,128]{3,2,1,0:T(8,128)}, f32[10,2,144,128]{3,2,1,0:T(8,128)S(1)}, u32[]{:S(2)}) copy-start(f32[10,2,144,128]{3,2,1,0:T(8,128)S(1)} %get-tuple-element.52.wide_ref) | copy-start | bytes 4423684
  164.6 16.5 %collective-permute-start.11 = (f32[8,128]{1,0:T(8,128)S(1)}, f32[8,128]{1,0:T(8,128)S(1)}, u32[]{:S(2)}, u32[]{:S(2)}) collective-permute-start(f32[8,128]{1,0:T(8,128)S(1)} %get-tuple-element.51.n0_ref), channel_id=1, source_target_pairs={{0,1},{1,0},{2,3},{3,2},{4,5},{5,4},{6,7},{7,6},{8,9},{9,8},{10,11... | collective-permute-start | bytes 12296 | tf_op jit(solution)/shard_map/ppermute | solution.py:475
  178.4 3.6 %collective-permute-start.12 = (f32[8,128]{1,0:T(8,128)S(1)}, f32[8,128]{1,0:T(8,128)S(1)}, u32[]{:S(2)}, u32[]{:S(2)}) collective-permute-start(f32[8,128]{1,0:T(8,128)S(1)} %get-tuple-element.51.n0_ref), channel_id=1, source_target_pairs={{0,2},{1,3},{2,0},{3,1},{4,6},{5,7},{6,4},{7,5},{8,10},{9,11},{10,... | collective-permute-start | bytes 12296 | tf_op jit(solution)/shard_map/ppermute | solution.py:475
  180.1 3.0 %collective-permute-start.13 = (f32[8,128]{1,0:T(8,128)S(1)}, f32[8,128]{1,0:T(8,128)S(1)}, u32[]{:S(2)}, u32[]{:S(2)}) collective-permute-start(f32[8,128]{1,0:T(8,128)S(1)} %get-tuple-element.51.n0_ref), channel_id=1, source_target_pairs={{0,3},{1,2},{2,1},{3,0},{4,7},{5,6},{6,5},{7,4},{8,11},{9,10},{10,... | collective-permute-start | bytes 12296 | tf_op jit(solution)/shard_map/ppermute | solution.py:475
  183.4 1.2 copy-start.15
  184.6 28.5 %all-to-all-start.3 = ((f32[32,96,128]{2,1,0:T(8,128)}), f32[32,96,128]{2,1,0:T(8,128)S(1)}, u32[]{:S(2)}, u32[]{:S(2)}) async-start(f32[32,96,128]{2,1,0:T(8,128)} %bitcast.13), calls=%async_computation.3 | async-start | bytes 3145728 | tf_op jit(solution)/shard_map/all_to_all | solution.py:458
  189.3 1.1 copy-start.3
  190.5 1.1 copy-start.5
  191.6 1.4 copy-start.1
where the time goes:
time: 215 us; the launch traced here: 214 us
  waiting for transfers between devices  63.8 us (30%)
  starting transfers between devices  58.1 us (27%)
  Pallas kernels  47.6 us (22%)
  blocking collectives  29 us (13%)
  local copies, waits for them, and re-layouts  13.6 us (6%)
    all_to_all x3, waiting for transfers between devices, everyone(): return lax.all_to_all(copies, 'orb', 0, 0, tiled=True)  58.4 us
    pallas_call x2, Pallas kernels, propagate(): call(propagate_body, [(DEPTH + 2, 2, XP, NY), (8, NY)], [vmem()] * 10, [p...  37.8 us
    all_to_all x1, blocking collectives, everyone(): return lax.all_to_all(copies, 'orb', 0, 0, tiled=True)  29 us
    ppermute x6, starting transfers between devices, per_device(): lax.ppermute(norm, 'slab', [(i, i ^ k) for i in range(SLABS)])  28 us
    all_to_all x3, starting transfers between devices, everyone(): return lax.all_to_all(copies, 'orb', 0, 0, tiled=True)  24 us
    unnamed x50, local copies, waits for them, and re-layouts  11.6 us
  transfers between devices with their start and end apart: 17, of which 8 were waited for; matrix products, arithmetic and copies ran while one was open for 1% of the time, Pallas kernels for 3%

commit v1 on v0

--- a/solution.py
+++ b/solution.py
@@ -27,7 +27,7 @@
 PAD = 8
 XP = NX + 2 * PAD
 PACK = 3 * DEPTH * ROWS
-CHUNK = 32
+CHUNK = 16
 F32 = jnp.float32
 
 CORE_PAIRS = [(0, 1), (1, 0), (2, 3), (3, 2)]
@@ -42,11 +42,12 @@
     return pl.BlockSpec(memory_space=pltpu.SMEM)
 
 
-def call(body, outs, ins, scratch=(), flops=1000000, limit=40):
+def call(name, body, outs, ins, scratch=(), flops=1000000, limit=8):
     shapes = [jax.ShapeDtypeStruct(s, F32) for s in outs]
     size = sum(4 * s.size for s in shapes)
     return pl.pallas_call(
         body,
+        name=name,
         out_shape=shapes,
         in_specs=ins,
         out_specs=[vmem()] * len(outs),
@@ -71,8 +72,15 @@
     return lax.broadcasted_iota(jnp.int32, shape, len(shape) - 2) % 8 < 4
 
 
-def prepare_body(orb_ref, pot_ref, wide_ref, weight_ref, core_ref, chip_ref):
+def to_rows(ref, rows_ref):
+    for comp in range(3):
+        for z in range(DEPTH):
+            rows_ref[pl.ds((comp * DEPTH + z) * ROWS, ROWS), :] = ref[comp, pl.ds(z, ROWS, stride=DEPTH), :]
+
+
+def prepare_body(orb_ref, pot_ref, e_ref, wide_ref, weight_ref, core_ref, chip_ref, e_rows_ref):
     core = core_index()
+    to_rows(e_ref, e_rows_ref)
     for z in range(DEPTH):
         for part in range(2):
             wide_ref[z + 1, part, PAD : PAD + NX, :] = orb_ref[part, pl.ds(z, NX, stride=DEPTH), :]
@@ -88,13 +96,19 @@
         chip_ref[2 * HALO + i] = weight_ref[core * (DEPTH - MARGIN) + i]
 
 
-def prepare(orbitals, potential):
+def prepare(orbitals, potential, e_field):
     planes = 2 * HALO + MARGIN
     return call(
+        "prepare",
         prepare_body,
-        [(DEPTH + 2, 2, XP, NY), (DEPTH, NX, NY), (planes, NX, NY), (planes, NX, NY)],
-        [vmem(), vmem()],
-    )(orbitals.reshape(2, NX * DEPTH, NY), potential.reshape(NX * DEPTH, NY))
+        [(DEPTH + 2, 2, XP, NY), (DEPTH, NX, NY), (planes, NX, NY), (planes, NX, NY), (PACK, NY)],
+        [vmem()] * 3,
+        limit=12,
+    )(
+        orbitals.reshape(2, NX * DEPTH, NY),
+        potential.reshape(NX * DEPTH, NY),
+        e_field.reshape(3, ROWS * DEPTH, NY),
+    )
 
 
 def rims_body(wide_ref, core_ref, chip_ref):
@@ -108,24 +122,19 @@
 
 
 def rims(wide):
-    return call(rims_body, [(2 * HALO, NX, NY)] * 2, [vmem()])(wide)
-
-
-def spread_body(a_ref, e_ref, copies_ref, a_rows_ref, e_rows_ref):
-    for comp in range(3):
-        for z in range(DEPTH):
-            rows = pl.ds((comp * DEPTH + z) * ROWS, ROWS)
-            a_rows_ref[rows, :] = a_ref[comp, pl.ds(z, ROWS, stride=DEPTH), :]
-            e_rows_ref[rows, :] = e_ref[comp, pl.ds(z, ROWS, stride=DEPTH), :]
+    return call("rims", rims_body, [(2 * HALO, NX, NY)] * 2, [vmem()])(wide)
+
+
+def spread_body(a_ref, copies_ref, a_rows_ref):
+    to_rows(a_ref, a_rows_ref)
     value = a_rows_ref[...]
     for i in range(ORBS):
         copies_ref[i] = value
 
 
-def spread(a_field, e_field):
-    flat = (3, ROWS * DEPTH, NY)
-    return call(spread_body, [(ORBS, PACK, NY), (PACK, NY), (PACK, NY)], [vmem(), vmem()])(
-        a_field.reshape(flat), e_field.reshape(flat)
+def spread(a_field):
+    return call("spread", spread_body, [(ORBS, PACK, NY), (PACK, NY)], [vmem()])(
+        a_field.reshape(3, ROWS * DEPTH, NY)
     )
 
 
@@ -149,6 +158,7 @@
 
 def assemble(got):
     return call(
+        "assemble",
         assemble_body,
         [(DEPTH, 3, NX, NY), (MARGIN, 3, NX, NY), (MARGIN, 3, NX, NY)],
         [vmem()],
@@ -157,7 +167,7 @@
 
 def propagate_body(
     scale_ref, wide_ref, hcore_ref, hchip_ref, weight_ref, vcore_ref, vchip_ref, field_ref, acore_ref, achip_ref,
-    out_ref, norm_ref, ping_ref, pong_ref, w_ref, a_ref,
+    out_ref, norm_ref, base_ref, ping_ref, pong_ref, w_ref, a_ref,
 ):
     core = core_index()
     scale = scale_ref[0:1, :]
@@ -170,6 +180,7 @@
                 ref[j, part, 0:PAD, :] = edge
                 ref[j, part, PAD + NX : XP, :] = edge
 
+    clear(base_ref, WIDE)
     clear(ping_ref, WIDE)
     clear(pong_ref, WIDE)
     clear(out_ref, DEPTH + 2)
@@ -185,100 +196,85 @@
     @pl.loop(0, DEPTH)
     def _(z):
         for part in range(2):
-            ping_ref[z + HALO, part, PAD : PAD + NX, :] = wide_ref[z + 1, part, PAD : PAD + NX, :] * scale
+            base_ref[z + HALO, part, PAD : PAD + NX, :] = wide_ref[z + 1, part, PAD : PAD + NX, :] * scale
         put_field(z + MARGIN, field_ref[z], weight_ref[z])
 
-    def put_halo(start, width, orb_ref, pot_ref, fld_ref):
+    def put_halo(above, orb_ref, pot_ref, fld_ref):
         @pl.loop(0, HALO)
         def _(i):
             for part in range(2):
-                ping_ref[start * (DEPTH + HALO) + i, part, PAD : PAD + NX, :] = orb_ref[2 * i + part] * scale
+                base_ref[above * (DEPTH + HALO) + i, part, PAD : PAD + NX, :] = orb_ref[2 * i + part] * scale
 
         @pl.loop(0, MARGIN)
         def _(i):
-            put_field(start * (DEPTH + MARGIN) + i, fld_ref[i], pot_ref[i])
+            put_field(above * (DEPTH + MARGIN) + i, fld_ref[i], pot_ref[2 * HALO + i])
 
     @pl.when(core == 1)
     def _():
-        put_halo(0, 0, hcore_ref, vcore_ref, acore_ref)
-        put_halo(1, 0, hchip_ref, vchip_ref, achip_ref)
+        put_halo(0, hcore_ref, vcore_ref, acore_ref)
+        put_halo(1, hchip_ref, vchip_ref, achip_ref)
 
     @pl.when(core == 0)
     def _():
-        put_halo(1, 0, hcore_ref, vcore_ref, acore_ref)
-        put_halo(0, 0, hchip_ref, vchip_ref, achip_ref)
-
-    slab = lax.axis_index("slab")
-    source, target = ping_ref, pong_ref
-    norm_ref[...] = jnp.zeros((8, NY), F32)
-    for order in range(1, TERMS + 1):
-
-        @pl.loop(order, WIDE - order)
-        def _(j, order=order, source=source, target=target):
-            depth = slab * DEPTH + j - HALO
-            inside = jnp.where((depth >= 0) & (depth < NZ), 1.0, 0.0).astype(F32)
-            factor = inside * (0.5 * TIME_STEP / order)
-            own = j - HALO + 1
-            squares = jnp.zeros((8, NY), F32)
-            for r in range(0, NX, CHUNK):
-                here = pl.ds(PAD + r, CHUNK)
-                centre, total, drift = [], [], []
-                fields = [a_ref[j - 1, comp, r : r + CHUNK, :] for comp in range(3)]
-                for part in range(2):
-                    mid = source[j, part, here, :]
-                    xp = source[j, part, pl.ds(PAD + r + 1, CHUNK), :]
-                    xm = source[j, part, pl.ds(PAD + r - 1, CHUNK), :]
-                    zp = source[j + 1, part, here, :]
-                    zm = source[j - 1, part, here, :]
-                    yp, ym = lane_shifts(mid)
-                    centre.append(mid)
-                    total.append((xp + xm) + (yp + ym) + (zp + zm))
-                    drift.append(fields[0] * (xp - xm) + fields[1] * (yp - ym) + fields[2] * (zp - zm))
-                weight = w_ref[j - 1, r : r + CHUNK, :]
-                real_h = weight * centre[0] - total[0] + drift[1]
-                imag_h = weight * centre[1] - total[1] - drift[0]
-                new = (factor * imag_h, -factor * real_h)
-                if order < TERMS:
-                    for part in range(2):
-                        target[j, part, here, :] = new[part]
-                if order == 1:
-
-                    @pl.when((own >= 0) & (own < DEPTH + 2))
-                    def _():
-                        for part in range(2):
-                            out_ref[own, part, here, :] = centre[part] + new[part]
-                elif order < TERMS:
-
-                    @pl.when((own >= 0) & (own < DEPTH + 2))
-                    def _():
-                        for part in range(2):
-                            out_ref[own, part, here, :] += new[part]
-                else:
-                    for part in range(2):
-                        moved = out_ref[own, part, here, :] + new[part]
-                        out_ref[own, part, here, :] = moved
-                        squares = squares + (moved * moved).reshape(CHUNK // 8, 8, NY).sum(0)
-            if order == TERMS:
-
-                @pl.when((own >= 1) & (own < DEPTH + 1))
-                def _():
-                    norm_ref[...] += squares
-
-        source, target = target, source
+        put_halo(1, hcore_ref, vcore_ref, acore_ref)
+        put_halo(0, hchip_ref, vchip_ref, achip_ref)
+
+    first = lax.axis_index("slab") * DEPTH - HALO
+
+    def plane(j, order, source, target, shift):
+        depth = first + j
+        inside = jnp.where((depth >= 0) & (depth < NZ), 1.0, 0.0).astype(F32)
+        factor = inside * (0.5 * TIME_STEP / order)
+        squares = jnp.zeros((8, NY), F32)
+        for r in range(0, NX, CHUNK):
+            here = pl.ds(PAD + r, CHUNK)
+            centre, total, drift = [], [], []
+            fields = [a_ref[j - 1, comp, r : r + CHUNK, :] for comp in range(3)]
+            for part in range(2):
+                mid = source[j, part, here, :]
+                xp = source[j, part, pl.ds(PAD + r + 1, CHUNK), :]
+                xm = source[j, part, pl.ds(PAD + r - 1, CHUNK), :]
+                zp = source[j + 1, part, here, :]
+                zm = source[j - 1, part, here, :]
+                yp, ym = lane_shifts(mid)
+                centre.append(mid)
+                total.append((xp + xm) + (yp + ym) + (zp + zm))
+                drift.append(fields[0] * (xp - xm) + fields[1] * (yp - ym) + fields[2] * (zp - zm))
+            weight = w_ref[j - 1, r : r + CHUNK, :]
+            real_h = weight * centre[0] - total[0] + drift[1]
+            imag_h = weight * centre[1] - total[1] - drift[0]
+            for part, change in enumerate((factor * imag_h, -factor * real_h)):
+                value = base_ref[j, part, here, :] + change
+                target[j + shift, part, here, :] = value
+                if order == 1 and HALO <= j < HALO + DEPTH:
+                    squares = squares + (value * value).reshape(CHUNK // 8, 8, NY).sum(0)
+        return squares
+
+    squares = jnp.zeros((8, NY), F32)
+    source = base_ref
+    for done, order in enumerate(range(TERMS, 0, -1)):
+        target = out_ref if order == 1 else (ping_ref, pong_ref)[done % 2]
+        for j in range(done + 1, WIDE - done - 1):
+            squares = squares + plane(j, order, source, target, 1 - HALO if order == 1 else 0)
+        source = target
+    norm_ref[...] = squares
 
 
 def propagate(scale, wide, hcore, hchip, weight, vcore, vchip, field, acore, achip):
     return call(
+        "propagate",
         propagate_body,
         [(DEPTH + 2, 2, XP, NY), (8, NY)],
         [vmem()] * 10,
         [
             pltpu.VMEM((WIDE, 2, XP, NY), F32),
             pltpu.VMEM((WIDE, 2, XP, NY), F32),
+            pltpu.VMEM((WIDE, 2, XP, NY), F32),
             pltpu.VMEM((DEPTH + 2 * MARGIN, NX, NY), F32),
             pltpu.VMEM((DEPTH + 2 * MARGIN, 3, NX, NY), F32),
         ],
         flops=60000000,
+        limit=28,
     )(scale, wide, hcore, hchip, weight, vcore, vchip, field, acore, achip)
 
 
@@ -324,7 +320,7 @@
 
 
 def current(wide, field):
-    return call(current_body, [(ORBS // 2, 2, PACK, NY)], [vmem(), vmem()], flops=10000000)(wide, field)[0]
+    return call("current", current_body, [(ORBS // 2, 2, PACK, NY)], [vmem(), vmem()], flops=10000000, limit=10)(wide, field)[0]
 
 
 def weigh_body(occ_ref, n0_ref, n1_ref, n2_ref, n3_ref, flow_ref, out_ref, scale_ref):
@@ -343,7 +339,7 @@
 
 def weigh(occupation, norms, flow):
     return call(
-        weigh_body, [(ORBS // 2, 2, PACK, NY), (8, NY)], [smem()] + [vmem()] * 5, flops=500000
+        "weigh", weigh_body, [(ORBS // 2, 2, PACK, NY), (8, NY)], [smem()] + [vmem()] * 5, flops=500000
     )(occupation, *norms, flow)
 
 
@@ -412,7 +408,7 @@
 
 
 def double_curl(field, acore, achip):
-    return call(curl_body, [(PACK, NY)], [vmem()] * 3, flops=1000000)(field, acore, achip)[0]
+    return call("double_curl", curl_body, [(PACK, NY)], [vmem()] * 3, flops=1000000)(field, acore, achip)[0]
 
 
 def update_body(last, got_ref, curl_ref, e_ref, a_ref, *outs):
@@ -440,7 +436,7 @@
         outs = [(3, ROWS * DEPTH, NY)] * 2
     else:
         outs = [(ORBS, PACK, NY), (PACK, NY), (PACK, NY)]
-    return call(functools.partial(update_body, last), outs, [vmem()] * 4, flops=500000)(got, curl, e_rows, a_rows)
+    return call("update", functools.partial(update_body, last), outs, [vmem()] * 4, flops=500000)(got, curl, e_rows, a_rows)
 
 
 def finish_body(scale_ref, wide_ref, out_ref):
@@ -451,7 +447,7 @@
 
 
 def finish(scale, wide):
-    return call(finish_body, [(2, NX * DEPTH, NY)], [vmem()] * 2)(scale, wide)[0]
+    return call("finish", finish_body, [(2, NX * DEPTH, NY)], [vmem()] * 2)(scale, wide)[0]
 
 
 def everyone(copies):
@@ -459,12 +455,12 @@
 
 
 def per_device(orbitals, potential, occupation, e_field, a_field):
-    copies, a_rows, e_rows = spread(a_field, e_field)
+    copies, a_rows = spread(a_field)
     got = everyone(copies)
-    wide, weight, core_send, chip_send = prepare(orbitals, potential)
+    wide, weight, core_send, chip_send, e_rows = prepare(orbitals, potential, e_field)
     hcore = lax.ppermute(core_send, "slab", CORE_PAIRS)
     hchip = lax.ppermute(chip_send, "slab", CHIP_PAIRS)
-    vcore, vchip = hcore[2 * HALO :], hchip[2 * HALO :]
+    vcore, vchip = hcore, hchip
     scale = jnp.ones((8, NY), F32)
     for step in range(STEPS):
         last = step == STEPS - 1
@@ -481,6 +477,7 @@
             core_send, chip_send = rims(wide)
             hcore = lax.ppermute(core_send, "slab", CORE_PAIRS)
             hchip = lax.ppermute(chip_send, "slab", CHIP_PAIRS)
+            flows, hcore, hchip = lax.optimization_barrier((flows, hcore, hchip))
             copies, a_rows, e_rows = update(last, flows, curl, e_rows, a_rows)
             got = everyone(copies)
         else:

time: 215 us -> 186 us (0.87)
  Pallas kernels: 47.6 us -> 21.4 us
  local copies, waits for them, and re-layouts: 13.6 us -> 20.2 us
  waiting for transfers between devices: 63.8 us -> 59.8 us
  blocking collectives: 29 us -> 25.6 us
    pallas_call x16, Pallas kernels: 47.6 us -> 21.4 us  [the longest x2 11.5 us: propagate(): call('propagate', propagate_body, [(DEPTH + 2, 2, XP, NY), (8, NY)], [vme...]
    unnamed x50 -> x66, local copies, waits for them, and re-layouts: 11.6 us -> 20.2 us
    all_to_all x1, blocking collectives: 29 us -> 25.6 us  [everyone(): return lax.all_to_all(copies, 'orb', 0, 0, tiled=True)]
    ppermute x2, starting transfers between devices: 2.18 us -> 5.41 us  [per_device(): acore = lax.ppermute(acore_send, 'slab', CORE_PAIRS)]
    ppermute x6, waiting for transfers between devices: 3.42 us -> 0.79 us  [per_device(): lax.ppermute(norm, 'slab', [(i, i ^ k) for i in range(SLABS)])]
  transfers between devices with their start and end apart: 17 -> 17, of which waited for: 8 -> 6; matrix products, arithmetic and copies ran while one was open for 1% -> 0% of each run, Pallas kernels for 3% -> 3%
where the time goes in v1:
time: 186 us; the launch traced here: 185 us
  waiting for transfers between devices  59.8 us (32%)
  starting transfers between devices  56.2 us (30%)
  blocking collectives  25.6 us (14%)
  Pallas kernels  21.4 us (12%)
  local copies, waits for them, and re-layouts  20.2 us (11%)
    all_to_all x3, waiting for transfers between devices, everyone(): return lax.all_to_all(copies, 'orb', 0, 0, tiled=True)  57.8 us
    ppermute x6, starting transfers between devices, per_device(): lax.ppermute(norm, 'slab', [(i, i ^ k) for i in range(SLABS)])  25.9 us
    all_to_all x1, blocking collectives, everyone(): return lax.all_to_all(copies, 'orb', 0, 0, tiled=True)  25.6 us
    all_to_all x3, starting transfers between devices, everyone(): return lax.all_to_all(copies, 'orb', 0, 0, tiled=True)  21.9 us
    unnamed x66, local copies, waits for them, and re-layouts  20.2 us
    pallas_call x2, Pallas kernels, propagate(): call('propagate', propagate_body, [(DEPTH + 2, 2, XP, NY), (8, NY)], [vme...  11.5 us
    ppermute x2, starting transfers between devices, per_device(): acore = lax.ppermute(acore_send, 'slab', CORE_PAIRS)  5.41 us
  transfers between devices with their start and end apart: 17, of which 6 were waited for; matrix products, arithmetic and copies ran while one was open for 0% of the time, Pallas kernels for 3%

profile of v1, /device:TPU:0, one launch (start us, length us, event | category | flops | bytes accessed | tf_op | source)
XLA Modules:
  0.0 185.0 jit_solution(8176447957385107729)
XLA Ops:
  0.6 0.8 copy-done.32
  1.4 1.3 spread.1
  2.7 10.8 %all-to-all-start = ((f32[32,96,128]{2,1,0:T(8,128)}), f32[32,96,128]{2,1,0:T(8,128)S(1)}, u32[]{:S(2)}, u32[]{:S(2)}) async-start(f32[32,96,128]{2,1,0:T(8,128)} %get-tuple-element.38), calls=%async_computation | async-start | bytes 3145728 | tf_op jit(solution)/shard_map/all_to_all | solution.py:454
  13.6 1.7 prepare.1
  15.4 0.8 copy-done.18
  16.2 1.1 copy-done.23
  17.3 0.0 collective-permute-start
  17.3 0.7 collective-permute-start.1
  18.0 19.1 %all-to-all-done = f32[32,96,128]{2,1,0:T(8,128)S(1)} async-done(((f32[32,96,128]{2,1,0:T(8,128)}), f32[32,96,128]{2,1,0:T(8,128)S(1)}, u32[]{:S(2)}, u32[]{:S(2)}) %all-to-all-start) | async-done | bytes 1572896 | tf_op jit(solution)/shard_map/all_to_all | solution.py:454
  37.1 1.2 copy-done.6
  38.3 1.4 copy-done.7
  39.7 0.3 assemble.2
  40.0 0.1 collective-permute-start.2
  40.1 0.7 collective-permute-start.3
  40.8 0.0 collective-permute-done.hcore_ref.vcore_ref
  40.8 0.0 copy-start
  40.8 0.9 copy-done
  41.8 0.0 collective-permute-done.1.hchip_ref.vchip_ref
  41.8 0.9 copy-done.3
  42.7 0.0 copy-start.1
  42.7 1.7 copy-done.1
  44.5 1.2 copy-done.4
  45.6 1.4 copy-done.24
  47.0 5.7 %propagate.2 = (f32[10,2,144,128]{3,2,1,0:T(8,128)S(1)}, f32[8,128]{1,0:T(8,128)S(1)}) custom-call(f32[8,128]{1,0:T(8,128)S(1)} %broadcast_in_dim.3.scale_ref, f32[10,2,144,128]{3,2,1,0:T(8,128)S(1)} %copy-done.24, f32[14,128,128]{2,1,0:T(8,128)S(1)} %copy-done.1, f32[14,128,128]{2,1,0:T(8,128)S(1)} %copy-done.4, f32[8,128,128]{2,1,0:T(8,128)S(1)} %copy-done.19, ...), custom_call_target="tpu_custom_call" | custom-call | flops 60000000 | bytes 2957312 | tf_op jit(solution)/shard_map/propagate/pallas_call | solution.py:264
  52.7 1.2 collective-permute-start.6
  53.9 11.4 %collective-permute-start.5 = (f32[8,128]{1,0:T(8,128)S(1)}, f32[8,128]{1,0:T(8,128)S(1)}, u32[]{:S(2)}, u32[]{:S(2)}) collective-permute-start(f32[8,128]{1,0:T(8,128)S(1)} %get-tuple-element.42.n0_ref), channel_id=1, source_target_pairs={{0,2},{1,3},{2,0},{3,1},{4,6},{5,7},{6,4},{7,5},{8,10},{9,11},{10,... | collective-permute-start | bytes 12296 | tf_op jit(solution)/shard_map/ppermute | solution.py:471
  66.0 0.8 current.2.flow_ref
  66.8 0.0 collective-permute-done.6.n3_ref
  66.8 0.1 collective-permute-done.5.n2_ref
  66.9 0.0 collective-permute-done.4.n1_ref
  67.0 0.2 weigh.2
  67.2 1.2 copy-done.21
  68.4 6.9 %all-to-all-start.1 = ((f32[32,96,128]{2,1,0:T(8,128)}), f32[32,96,128]{2,1,0:T(8,128)}, u32[]{:S(2)}, u32[]{:S(2)}) async-start(f32[32,96,128]{2,1,0:T(8,128)} %bitcast.13), calls=%async_computation.1 | async-start | bytes 3145728 | tf_op jit(solution)/shard_map/all_to_all | solution.py:454
  75.3 0.1 rims.1
  75.4 0.2 collective-permute-start.7
  75.7 0.7 collective-permute-start.8
  76.4 0.1 copy-done.15
  76.5 1.1 copy-done.17
  77.6 0.1 double_curl.2.curl_ref
  77.7 0.0 collective-permute-done.7.hcore_ref
  77.8 0.8 copy-done.26
  78.6 0.8 copy-done.28
  79.4 20.0 %all-to-all-done.1.got_ref = f32[32,96,128]{2,1,0:T(8,128)} async-done(((f32[32,96,128]{2,1,0:T(8,128)}), f32[32,96,128]{2,1,0:T(8,128)}, u32[]{:S(2)}, u32[]{:S(2)}) %all-to-all-start.1) | async-done | bytes 1572896 | tf_op jit(solution)/shard_map/all_to_all | solution.py:454
  99.4 1.6 update.2
  101.1 25.6 %all_to_all.20 = f32[32,96,128]{2,1,0:T(8,128)S(1)} all-to-all(f32[32,96,128]{2,1,0:T(8,128)S(1)} %get-tuple-element.53), channel_id=1, replica_groups=mesh['orb'=32,'slab'=4] {'orb'}, dimensions={0} | all-to-all | bytes 3145728 | tf_op jit(solution)/shard_map/all_to_all | solution.py:454
  126.7 0.3 assemble.3
  127.0 5.3 %collective-permute-start.9 = (f32[4,3,128,128]{3,2,1,0:T(8,128)S(1)}, f32[4,3,128,128]{3,2,1,0:T(8,128)S(1)}, u32[]{:S(2)}, u32[]{:S(2)}) collective-permute-start(f32[4,3,128,128]{3,2,1,0:T(8,128)S(1)} %get-tuple-element.55), channel_id=1, source_target_pairs={{0,1},{1,0},{2,3},{3,2},{4,5},{5,4},{6,7},{7,6},{8,9},{9,8},{10,11... | collective-permute-start | bytes 2359304 | tf_op jit(solution)/shard_map/ppermute | solution.py:468
  132.3 0.7 collective-permute-start.10
  133.0 1.2 collective-permute-done.9.acore_ref
  134.3 5.8 %propagate.3 = (f32[10,2,144,128]{3,2,1,0:T(8,128)S(1)}, f32[8,128]{1,0:T(8,128)S(1)}) custom-call(f32[8,128]{1,0:T(8,128)S(1)} %get-tuple-element.44.scale_ref, f32[10,2,144,128]{3,2,1,0:T(8,128)S(1)} %get-tuple-element.43.wide_ref, f32[10,128,128]{2,1,0:T(8,128)S(1)} %copy-done.27, f32[10,128,128]{2,1,0:T(8,128)S(1)} %copy-done.29, ...), custom_call_target="tpu_custom_call" | custom-call | flops 60000000 | bytes 2957312 | tf_op jit(solution)/shard_map/propagate/pallas_call | solution.py:264
  140.2 0.1 collective-permute-start.13
  140.3 13.2 %collective-permute-start.12 = (f32[8,128]{1,0:T(8,128)S(1)}, f32[8,128]{1,0:T(8,128)S(1)}, u32[]{:S(2)}, u32[]{:S(2)}) collective-permute-start(f32[8,128]{1,0:T(8,128)S(1)} %get-tuple-element.57.n0_ref), channel_id=1, source_target_pairs={{0,2},{1,3},{2,0},{3,1},{4,6},{5,7},{6,4},{7,5},{8,10},{9,11},{10,... | collective-permute-start | bytes 12296 | tf_op jit(solution)/shard_map/ppermute | solution.py:471
  153.5 0.9 current.3.flow_ref
  154.4 0.7 collective-permute-done.12.n2_ref
  155.1 0.2 weigh.3
  155.4 1.1 copy-done.22
  156.5 4.1 %all-to-all-start.3 = ((f32[32,96,128]{2,1,0:T(8,128)}), f32[32,96,128]{2,1,0:T(8,128)S(1)}, u32[]{:S(2)}, u32[]{:S(2)}) async-start(f32[32,96,128]{2,1,0:T(8,128)} %bitcast.14), calls=%async_computation.3 | async-start | bytes 3145728 | tf_op jit(solution)/shard_map/all_to_all | solution.py:454
  160.6 1.1 copy-done.11
  161.8 1.1 copy-done.13
  162.9 0.1 double_curl.3.curl_ref
  163.1 1.2 copy-done.9
  164.3 1.3 finish.1
  165.5 18.7 %all-to-all-done.3.got_ref = f32[32,96,128]{2,1,0:T(8,128)S(1)} async-done(((f32[32,96,128]{2,1,0:T(8,128)}), f32[32,96,128]{2,1,0:T(8,128)S(1)}, u32[]{:S(2)}, u32[]{:S(2)}) %all-to-all-start.3) | async-done | bytes 1572896 | tf_op jit(solution)/shard_map/all_to_all | solution.py:454
  184.2 0.7 update.3
  (54 shorter events, 0.1 us)
Async XLA Ops:
  0.6 0.8 copy-start.32
  2.7 10.9 %copy-start.25 = (f32[1,2,128,8,128]{4,3,2,1,0:T(8,128)S(1)}, f32[1,2,128,8,128]{4,3,2,1,0:T(8,128)}, u32[]{:S(2)}) copy-start(f32[1,2,128,8,128]{4,3,2,1,0:T(8,128)} %param.5) | copy-start | bytes 3145732
  2.7 10.9 %copy-start.30 = (f32[128,8,128]{2,1,0:T(8,128)S(1)}, f32[128,8,128]{2,1,0:T(8,128)}, u32[]{:S(2)}) copy-start(f32[128,8,128]{2,1,0:T(8,128)} %param.6) | copy-start | bytes 1572868
  2.7 10.9 %copy-start.31 = (f32[3,4,8,128]{3,2,1,0:T(8,128)S(1)}, f32[3,4,8,128]{3,2,1,0:T(8,128)}, u32[]{:S(2)}) copy-start(f32[3,4,8,128]{3,2,1,0:T(8,128)} %param.8) | copy-start | bytes 147460
  2.7 34.4 %all-to-all-start = ((f32[32,96,128]{2,1,0:T(8,128)}), f32[32,96,128]{2,1,0:T(8,128)S(1)}, u32[]{:S(2)}, u32[]{:S(2)}) async-start(f32[32,96,128]{2,1,0:T(8,128)} %get-tuple-element.38), calls=%async_computation | async-start | bytes 3145728 | tf_op jit(solution)/shard_map/all_to_all | solution.py:454
  15.4 0.8 copy-start.18
  16.2 1.1 copy-start.23
  17.3 23.5 %collective-permute-start = (f32[14,128,128]{2,1,0:T(8,128)}, f32[14,128,128]{2,1,0:T(8,128)S(1)}, u32[]{:S(2)}, u32[]{:S(2)}) collective-permute-start(f32[14,128,128]{2,1,0:T(8,128)} %get-tuple-element.35), channel_id=1, source_target_pairs={{0,1},{1,0},{2,3},{3,2},{4,5},{5,4},{6,7},{7,6},{8,9},{9,8},{10,11... | collective-permute-start | bytes 2752520 | tf_op jit(solution)/shard_map/ppermute | solution.py:461
  17.3 24.5 %collective-permute-start.1 = (f32[14,128,128]{2,1,0:T(8,128)}, f32[14,128,128]{2,1,0:T(8,128)S(1)}, u32[]{:S(2)}, u32[]{:S(2)}) collective-permute-start(f32[14,128,128]{2,1,0:T(8,128)} %get-tuple-element.36), channel_id=1, source_target_pairs={{1,2},{2,1},{5,6},{6,5},{9,10},{10,9},{13,14},{14,13},{17,18},{18,... | collective-permute-start | bytes 2752520 | tf_op jit(solution)/shard_map/ppermute | solution.py:462
  37.1 1.2 copy-start.6
  38.3 1.4 copy-start.7
  39.7 3.0 %copy-start.19 = (f32[8,128,128]{2,1,0:T(8,128)S(1)}, f32[8,128,128]{2,1,0:T(8,128)}, u32[]{:S(2)}) copy-start(f32[8,128,128]{2,1,0:T(8,128)} %copy-done.18) | copy-start | bytes 1572868
  40.0 2.7 %collective-permute-start.2 = (f32[4,3,128,128]{3,2,1,0:T(8,128)S(1)}, f32[4,3,128,128]{3,2,1,0:T(8,128)S(1)}, u32[]{:S(2)}, u32[]{:S(2)}) collective-permute-start(f32[4,3,128,128]{3,2,1,0:T(8,128)S(1)} %get-tuple-element.40), channel_id=1, source_target_pairs={{0,1},{1,0},{2,3},{3,2},{4,5},{5,4},{6,7},{7,6},{8,9},{9,8},{10,11... | collective-permute-start | bytes 2359304 | tf_op jit(solution)/shard_map/ppermute | solution.py:468
  40.1 2.6 %collective-permute-start.3 = (f32[4,3,128,128]{3,2,1,0:T(8,128)S(1)}, f32[4,3,128,128]{3,2,1,0:T(8,128)S(1)}, u32[]{:S(2)}, u32[]{:S(2)}) collective-permute-start(f32[4,3,128,128]{3,2,1,0:T(8,128)S(1)} %get-tuple-element.41), channel_id=1, source_target_pairs={{1,2},{2,1},{5,6},{6,5},{9,10},{10,9},{13,14},{14,13},{17,18},{18,... | collective-permute-start | bytes 2359304 | tf_op jit(solution)/shard_map/ppermute | solution.py:469
  40.8 0.9 copy-start
  41.8 0.9 copy-start.3
  42.7 10.0 %copy-start.14 = (f32[4,3,128,128]{3,2,1,0:T(8,128)}, f32[4,3,128,128]{3,2,1,0:T(8,128)S(1)}, u32[]{:S(2)}) copy-start(f32[4,3,128,128]{3,2,1,0:T(8,128)S(1)} %collective-permute-done.2.acore_ref) | copy-start | bytes 2359300
  42.7 10.0 %copy-start.16 = (f32[4,3,128,128]{3,2,1,0:T(8,128)}, f32[4,3,128,128]{3,2,1,0:T(8,128)S(1)}, u32[]{:S(2)}) copy-start(f32[4,3,128,128]{3,2,1,0:T(8,128)S(1)} %collective-permute-done.3.achip_ref) | copy-start | bytes 2359300
  42.7 1.7 copy-start.1
  44.5 1.2 copy-start.4
  45.6 1.4 copy-start.24
  52.7 14.1 %collective-permute-start.6 = (f32[8,128]{1,0:T(8,128)S(1)}, f32[8,128]{1,0:T(8,128)S(1)}, u32[]{:S(2)}, u32[]{:S(2)}) collective-permute-start(f32[8,128]{1,0:T(8,128)S(1)} %get-tuple-element.42.n0_ref), channel_id=1, source_target_pairs={{0,3},{1,2},{2,1},{3,0},{4,7},{5,6},{6,5},{7,4},{8,11},{9,10},{10,... | collective-permute-start | bytes 12296 | tf_op jit(solution)/shard_map/ppermute | solution.py:471
  53.9 13.1 %collective-permute-start.5 = (f32[8,128]{1,0:T(8,128)S(1)}, f32[8,128]{1,0:T(8,128)S(1)}, u32[]{:S(2)}, u32[]{:S(2)}) collective-permute-start(f32[8,128]{1,0:T(8,128)S(1)} %get-tuple-element.42.n0_ref), channel_id=1, source_target_pairs={{0,2},{1,3},{2,0},{3,1},{4,6},{5,7},{6,4},{7,5},{8,10},{9,11},{10,... | collective-permute-start | bytes 12296 | tf_op jit(solution)/shard_map/ppermute | solution.py:471
  65.3 1.6 collective-permute-start.4
  67.2 1.2 copy-start.21
  68.4 31.0 %all-to-all-start.1 = ((f32[32,96,128]{2,1,0:T(8,128)}), f32[32,96,128]{2,1,0:T(8,128)}, u32[]{:S(2)}, u32[]{:S(2)}) async-start(f32[32,96,128]{2,1,0:T(8,128)} %bitcast.13), calls=%async_computation.1 | async-start | bytes 3145728 | tf_op jit(solution)/shard_map/all_to_all | solution.py:454
  75.3 1.1 copy-start.15
  75.4 2.3 %collective-permute-start.7 = (f32[10,128,128]{2,1,0:T(8,128)S(1)}, f32[10,128,128]{2,1,0:T(8,128)S(1)}, u32[]{:S(2)}, u32[]{:S(2)}) collective-permute-start(f32[10,128,128]{2,1,0:T(8,128)S(1)} %get-tuple-element.46), channel_id=1, source_target_pairs={{0,1},{1,0},{2,3},{3,2},{4,5},{5,4},{6,7},{7,6},{8,9},{9,8},{10,11... | collective-permute-start | bytes 1966088 | tf_op jit(solution)/shard_map/ppermute | solution.py:478
  75.7 2.9 %collective-permute-start.8 = (f32[10,128,128]{2,1,0:T(8,128)S(1)}, f32[10,128,128]{2,1,0:T(8,128)S(1)}, u32[]{:S(2)}, u32[]{:S(2)}) collective-permute-start(f32[10,128,128]{2,1,0:T(8,128)S(1)} %get-tuple-element.47), channel_id=1, source_target_pairs={{1,2},{2,1},{5,6},{6,5},{9,10},{10,9},{13,14},{14,13},{17,18},{18,... | collective-permute-start | bytes 1966088 | tf_op jit(solution)/shard_map/ppermute | solution.py:479
  76.5 1.1 copy-start.17
  77.8 0.8 copy-start.26
  78.6 0.8 copy-start.28
  101.1 33.2 %copy-start.5 = (f32[14,128,128]{2,1,0:T(8,128)S(1)}, f32[14,128,128]{2,1,0:T(8,128)}, u32[]{:S(2)}) copy-start(f32[14,128,128]{2,1,0:T(8,128)} %copy-done.3) | copy-start | bytes 2752516
  101.1 33.2 %copy-start.27 = (f32[10,128,128]{2,1,0:T(8,128)S(1)}, f32[10,128,128]{2,1,0:T(8,128)}, u32[]{:S(2)}) copy-start(f32[10,128,128]{2,1,0:T(8,128)} %copy-done.26) | copy-start | bytes 1966084
  101.1 33.2 %copy-start.29 = (f32[10,128,128]{2,1,0:T(8,128)S(1)}, f32[10,128,128]{2,1,0:T(8,128)}, u32[]{:S(2)}) copy-start(f32[10,128,128]{2,1,0:T(8,128)} %copy-done.28) | copy-start | bytes 1966084
  126.7 7.6 %copy-start.2 = (f32[14,128,128]{2,1,0:T(8,128)S(1)}, f32[14,128,128]{2,1,0:T(8,128)}, u32[]{:S(2)}) copy-start(f32[14,128,128]{2,1,0:T(8,128)} %copy-done) | copy-start | bytes 2752516
  126.7 7.6 %copy-start.20 = (f32[8,128,128]{2,1,0:T(8,128)S(1)}, f32[8,128,128]{2,1,0:T(8,128)}, u32[]{:S(2)}) copy-start(f32[8,128,128]{2,1,0:T(8,128)} %copy-done.18) | copy-start | bytes 1572868
  127.0 7.2 %collective-permute-start.9 = (f32[4,3,128,128]{3,2,1,0:T(8,128)S(1)}, f32[4,3,128,128]{3,2,1,0:T(8,128)S(1)}, u32[]{:S(2)}, u32[]{:S(2)}) collective-permute-start(f32[4,3,128,128]{3,2,1,0:T(8,128)S(1)} %get-tuple-element.55), channel_id=1, source_target_pairs={{0,1},{1,0},{2,3},{3,2},{4,5},{5,4},{6,7},{7,6},{8,9},{9,8},{10,11... | collective-permute-start | bytes 2359304 | tf_op jit(solution)/shard_map/ppermute | solution.py:468
  132.3 1.9 %collective-permute-start.10 = (f32[4,3,128,128]{3,2,1,0:T(8,128)S(1)}, f32[4,3,128,128]{3,2,1,0:T(8,128)S(1)}, u32[]{:S(2)}, u32[]{:S(2)}) collective-permute-start(f32[4,3,128,128]{3,2,1,0:T(8,128)S(1)} %get-tuple-element.56), channel_id=1, source_target_pairs={{1,2},{2,1},{5,6},{6,5},{9,10},{10,9},{13,14},{14,13},{17,18},{18,... | collective-permute-start | bytes 2359304 | tf_op jit(solution)/shard_map/ppermute | solution.py:469
  134.2 5.9 %copy-start.10 = (f32[4,3,128,128]{3,2,1,0:T(8,128)}, f32[4,3,128,128]{3,2,1,0:T(8,128)S(1)}, u32[]{:S(2)}) copy-start(f32[4,3,128,128]{3,2,1,0:T(8,128)S(1)} %collective-permute-done.9.acore_ref) | copy-start | bytes 2359300
  134.2 5.9 %copy-start.12 = (f32[4,3,128,128]{3,2,1,0:T(8,128)}, f32[4,3,128,128]{3,2,1,0:T(8,128)S(1)}, u32[]{:S(2)}) copy-start(f32[4,3,128,128]{3,2,1,0:T(8,128)S(1)} %collective-permute-done.10.achip_ref) | copy-start | bytes 2359300
  140.2 14.2 %copy-start.8 = (f32[10,2,144,128]{3,2,1,0:T(8,128)}, f32[10,2,144,128]{3,2,1,0:T(8,128)S(1)}, u32[]{:S(2)}) copy-start(f32[10,2,144,128]{3,2,1,0:T(8,128)S(1)} %get-tuple-element.58.wide_ref) | copy-start | bytes 4423684
  140.2 14.2 %collective-permute-start.13 = (f32[8,128]{1,0:T(8,128)S(1)}, f32[8,128]{1,0:T(8,128)S(1)}, u32[]{:S(2)}, u32[]{:S(2)}) collective-permute-start(f32[8,128]{1,0:T(8,128)S(1)} %get-tuple-element.57.n0_ref), channel_id=1, source_target_pairs={{0,3},{1,2},{2,1},{3,0},{4,7},{5,6},{6,5},{7,4},{8,11},{9,10},{10,... | collective-permute-start | bytes 12296 | tf_op jit(solution)/shard_map/ppermute | solution.py:471
  140.3 14.8 %collective-permute-start.12 = (f32[8,128]{1,0:T(8,128)S(1)}, f32[8,128]{1,0:T(8,128)S(1)}, u32[]{:S(2)}, u32[]{:S(2)}) collective-permute-start(f32[8,128]{1,0:T(8,128)S(1)} %get-tuple-element.57.n0_ref), channel_id=1, source_target_pairs={{0,2},{1,3},{2,0},{3,1},{4,6},{5,7},{6,4},{7,5},{8,10},{9,11},{10,... | collective-permute-start | bytes 12296 | tf_op jit(solution)/shard_map/ppermute | solution.py:471
  153.5 1.6 collective-permute-start.11
  155.3 1.2 copy-start.22
  156.5 27.7 %all-to-all-start.3 = ((f32[32,96,128]{2,1,0:T(8,128)}), f32[32,96,128]{2,1,0:T(8,128)S(1)}, u32[]{:S(2)}, u32[]{:S(2)}) async-start(f32[32,96,128]{2,1,0:T(8,128)} %bitcast.14), calls=%async_computation.3 | async-start | bytes 3145728 | tf_op jit(solution)/shard_map/all_to_all | solution.py:454
  160.6 1.1 copy-start.11
  161.8 1.1 copy-start.13
  162.9 1.4 copy-start.9

commit v2 on v1

v2 whole, which is shorter than its diff:
```python
import functools

import jax
import jax.numpy as jnp
from jax import lax
from jax.experimental import pallas as pl
from jax.experimental.pallas import tpu as pltpu
from jax.sharding import PartitionSpec as P

TERMS = 4
STEPS = 2
TIME_STEP = 0.3
WAVE_STEP = 0.5
EPSILON = 1e-06

NX = 128
NY = 128
NZ = 32
ORBS = 32
SLABS = 4
CELLS = NX * NY * NZ
DEPTH = NZ // SLABS
ROWS = NX // ORBS
HALO = TERMS + 1
MARGIN = TERMS
WIDE = DEPTH + 2 * HALO
PAD = 8
PACK = 3 * DEPTH * ROWS
CHUNK = 8
F32 = jnp.float32

HALF = NX // 2
LOCAL = HALF + 8
XL = LOCAL + 2 * PAD
GROUP = ORBS // 2
TILES = LOCAL // 8
ALL = ("orb", "slab")
MEETING = (1, 2)


def pairs(flip, move):
    found = []
    for orb in range(ORBS):
        for slab in range(SLABS):
            to = move(slab)
            if to is not None:
                found.append((orb * SLABS + slab, (orb ^ flip) * SLABS + to))
    return found


def over_core(slab):
    return slab ^ 1


def over_chip(slab):
    return 3 - slab if slab in MEETING else None


HALVES = pairs(GROUP, lambda slab: slab)
CORE = pairs(0, over_core)
CHIP = pairs(0, over_chip)
CORE_ACROSS = pairs(GROUP, over_core)
CHIP_ACROSS = pairs(GROUP, over_chip)
CHIP_SUM = pairs(0, lambda slab: slab ^ 2)
BOTH_SUM = pairs(GROUP, lambda slab: slab ^ 2)
GROUPS = [list(range(GROUP)), list(range(GROUP, ORBS))]


def send(value, table):
    return lax.ppermute(value, ALL, table)


def vmem():
    return pl.BlockSpec(memory_space=pltpu.VMEM)


def smem():
    return pl.BlockSpec(memory_space=pltpu.SMEM)


def call(name, body, outs, ins, scratch=(), flops=1000000, limit=8):
    shapes = [jax.ShapeDtypeStruct(s, F32) for s in outs]
    size = sum(4 * s.size for s in shapes)
    return pl.pallas_call(
        body,
        name=name,
        out_shape=shapes,
        in_specs=ins,
        out_specs=[vmem()] * len(outs),
        scratch_shapes=list(scratch),
        compiler_params=pltpu.CompilerParams(vmem_limit_bytes=limit * 1024 * 1024),
        cost_estimate=pl.CostEstimate(flops=flops, bytes_accessed=2 * size, transcendentals=0),
    )


def core_index():
    return lax.rem(lax.axis_index("slab"), 2)


def half_index():
    return lax.axis_index("orb") // GROUP


def split_rows(value, half):
    low, high = value[0:LOCAL], value[NX - LOCAL : NX]
    return jnp.where(half == 0, low, high), jnp.where(half == 0, high, low)


def own_rows(value, half):
    return jnp.where(half == 0, value[0:HALF], value[8 : 8 + HALF])


def lane_shifts(value):
    lane = lax.broadcasted_iota(jnp.int32, value.shape, value.ndim - 1)
    plus = jnp.where(lane == NY - 1, 0.0, pltpu.roll(value, NY - 1, value.ndim - 1))
    minus = jnp.where(lane == 0, 0.0, pltpu.roll(value, 1, value.ndim - 1))
    return plus, minus


def half_rows(shape):
    return lax.broadcasted_iota(jnp.int32, shape, len(shape) - 2) % 8 < 4


def to_rows(ref, rows_ref):
    for comp in range(3):
        for z in range(DEPTH):
            rows_ref[pl.ds((comp * DEPTH + z) * ROWS, ROWS), :] = ref[comp, pl.ds(z, ROWS, stride=DEPTH), :]


def prepare_body(
    orb_ref, pot_ref, e_ref, own_ref, swap_ref, weight_ref, core_ref, chip_ref, corex_ref, chipx_ref, e_rows_ref
):
    core, half = core_index(), half_index()
    to_rows(e_ref, e_rows_ref)
    for z in range(DEPTH):
        for part in range(2):
            own_ref[z, part], swap_ref[z, part] = split_rows(orb_ref[part, pl.ds(z, NX, stride=DEPTH), :], half)
        weight_ref[z] = split_rows(2.0 * pot_ref[pl.ds(z, NX, stride=DEPTH), :] + 6.0, half)[0]
    to_core = (1 - core) * (DEPTH - HALO)
    to_chip = core * (DEPTH - HALO)
    for i in range(HALO):
        for part in range(2):
            core_ref[2 * i + part] = own_ref[to_core + i, part]
            chip_ref[2 * i + part] = own_ref[to_chip + i, part]
            corex_ref[2 * i + part] = swap_ref[to_core + i, part]
            chipx_ref[2 * i + part] = swap_ref[to_chip + i, part]
    for i in range(MARGIN):
        core_ref[2 * HALO + i] = weight_ref[(1 - core) * (DEPTH - MARGIN) + i]
        chip_ref[2 * HALO + i] = weight_ref[core * (DEPTH - MARGIN) + i]


def prepare(orbitals, potential, e_field):
    planes = 2 * HALO + MARGIN
    return call(
        "prepare",
        prepare_body,
        [(DEPTH, 2, LOCAL, NY)] * 2
        + [(DEPTH, LOCAL, NY)]
        + [(planes, LOCAL, NY)] * 2
        + [(2 * HALO, LOCAL, NY)] * 2
        + [(PACK, NY)],
        [vmem()] * 3,
        limit=12,
    )(
        orbitals.reshape(2, NX * DEPTH, NY),
        potential.reshape(NX * DEPTH, NY),
        e_field.reshape(3, ROWS * DEPTH, NY),
    )


def edges_body(wide_ref, out_ref):
    half = half_index()
    for z in range(DEPTH):
        for k in range(4):
            low = wide_ref[z + 1, k, PAD + HALF - 8 : PAD + HALF, :]
            out_ref[z, k] = jnp.where(half == 0, low, wide_ref[z + 1, k, PAD + 8 : PAD + 16, :])


def edges(wide):
    return call("edges", edges_body, [(DEPTH, 4, 8, NY)], [vmem()])(wide)[0]


def rims_body(wide_ref, edge_ref, own_ref, other_ref, core_ref, chip_ref, corex_ref, chipx_ref):
    core, half = core_index(), half_index()
    for z in range(DEPTH):
        for slot, ref in enumerate((own_ref, other_ref)):
            for part in range(2):
                value = wide_ref[z + 1, 2 * slot + part, PAD : PAD + LOCAL, :]
                edge = edge_ref[z, 2 * (1 - slot) + part]
                ref[z, part, 0:8, :] = jnp.where(half == 0, value[0:8], edge)
                ref[z, part, 8:HALF, :] = value[8:HALF]
                ref[z, part, HALF:LOCAL, :] = jnp.where(half == 0, edge, value[HALF:LOCAL])
    to_core = (1 - core) * (DEPTH - HALO)
    to_chip = core * (DEPTH - HALO)
    for i in range(HALO):
        for part in range(2):
            core_ref[2 * i + part] = own_ref[to_core + i, part]
            chip_ref[2 * i + part] = own_ref[to_chip + i, part]
            corex_ref[2 * i + part] = other_ref[to_core + i, part]
            chipx_ref[2 * i + part] = other_ref[to_chip + i, part]


def rims(wide, edge):
    return call(
        "rims", rims_body, [(DEPTH, 2, LOCAL, NY)] * 2 + [(2 * HALO, LOCAL, NY)] * 4, [vmem()] * 2, limit=12
    )(wide, edge)


def spread_body(a_ref, copies_ref, a_rows_ref):
    to_rows(a_ref, a_rows_ref)
    value = a_rows_ref[...]
    for i in range(GROUP):
        copies_ref[i] = value


def spread(a_field):
    return call("spread", spread_body, [(GROUP, PACK, NY), (PACK, NY)], [vmem()])(
        a_field.reshape(3, ROWS * DEPTH, NY)
    )


def assemble_body(got_ref, field_ref, edge_ref, core_ref, chip_ref, corex_ref, chipx_ref):
    core, half = core_index(), half_index()
    low = half_rows((GROUP // 2, 8, NY))
    for comp in range(3):
        for pair in range(DEPTH // 2):
            rows = pl.ds((comp * DEPTH + 2 * pair) * ROWS, 8)
            first = got_ref[:, 0, rows, :]
            second = got_ref[:, 1, rows, :]
            even = jnp.where(low, first, pltpu.roll(second, 4, 1))
            odd = jnp.where(low, pltpu.roll(first, 4, 1), second)
            for z, value in ((2 * pair, even), (2 * pair + 1, odd)):
                field_ref[z, comp] = value.reshape(HALF, NY)
                edge_ref[z, comp] = jnp.where(half == 0, value[GROUP // 2 - 1], value[0])
    for i in range(MARGIN):
        to_core = (1 - core) * (DEPTH - MARGIN) + i
        to_chip = core * (DEPTH - MARGIN) + i
        for comp in range(3):
            core_ref[i, comp] = field_ref[to_core, comp]
            chip_ref[i, comp] = field_ref[to_chip, comp]
            corex_ref[i, comp] = edge_ref[to_core, comp]
            chipx_ref[i, comp] = edge_ref[to_chip, comp]


def assemble(got):
    return call(
        "assemble",
        assemble_body,
        [(DEPTH, 3, HALF, NY), (DEPTH, 3, 8, NY)]
        + [(MARGIN, 3, HALF, NY)] * 2
        + [(MARGIN, 3, 8, NY)] * 2,
        [vmem()],
    )(got.reshape(GROUP // 2, 2, PACK, NY))


def propagate_body(
    own_ref, other_ref, hcore_ref, hchip_ref, hcorex_ref, hchipx_ref, weight_ref, vcore_ref, vchip_ref,
    field_ref, edge_ref, acore_ref, achip_ref, acorex_ref, achipx_ref,
    out_ref, norm_ref, a_ref, base_ref, ping_ref, pong_ref, w_ref,
):
    core, half = core_index(), half_index()
    zeros = jnp.zeros((PAD, NY), F32)

    def clear(ref, count):
        @pl.loop(0, count)
        def _(j):
            for k in range(4):
                ref[j, k, 0:PAD, :] = zeros
                ref[j, k, PAD + LOCAL : XL, :] = zeros

    clear(base_ref, WIDE)
    clear(ping_ref, WIDE)
    clear(pong_ref, WIDE)
    clear(out_ref, DEPTH + 2)

    def put_field(j, fld_ref, edg_ref, i, base):
        total = base
        for comp in range(3):
            value, edge = fld_ref[i, comp], edg_ref[i, comp]
            joined = jnp.where(
                half == 0, jnp.concatenate([value, edge], axis=0), jnp.concatenate([edge, value], axis=0)
            )
            a_ref[j, comp] = joined
            total = total + joined * joined
        w_ref[j] = total

    @pl.loop(0, DEPTH)
    def _(z):
        for part in range(2):
            base_ref[z + HALO, part, PAD : PAD + LOCAL, :] = own_ref[z, part]
            base_ref[z + HALO, 2 + part, PAD : PAD + LOCAL, :] = other_ref[z, part]
        put_field(z + MARGIN, field_ref, edge_ref, z, weight_ref[z])

    def put_halo(above, orb_ref, orbx_ref, pot_ref, fld_ref, edg_ref):
        @pl.loop(0, HALO)
        def _(i):
            j = above * (DEPTH + HALO) + i
            for part in range(2):
                base_ref[j, part, PAD : PAD + LOCAL, :] = orb_ref[2 * i + part]
                base_ref[j, 2 + part, PAD : PAD + LOCAL, :] = orbx_ref[2 * i + part]

        @pl.loop(0, MARGIN)
        def _(i):
            put_field(above * (DEPTH + MARGIN) + i, fld_ref, edg_ref, i, pot_ref[2 * HALO + i])

    @pl.when(core == 1)
    def _():
        put_halo(0, hcore_ref, hcorex_ref, vcore_ref, acore_ref, acorex_ref)
        put_halo(1, hchip_ref, hchipx_ref, vchip_ref, achip_ref, achipx_ref)

    @pl.when(core == 0)
    def _():
        put_halo(1, hcore_ref, hcorex_ref, vcore_ref, acore_ref, acorex_ref)
        put_halo(0, hchip_ref, hchipx_ref, vchip_ref, achip_ref, achipx_ref)

    first = lax.axis_index("slab") * DEPTH - HALO
    sums = [jnp.zeros((8, NY), F32), jnp.zeros((8, NY), F32)]

    def plane(j, order, source, target, shift):
        depth = first + j
        inside = jnp.where((depth >= 0) & (depth < NZ), 1.0, 0.0).astype(F32)
        factor = inside * (0.5 * TIME_STEP / order)
        for r in range(0, LOCAL, CHUNK):
            here = pl.ds(PAD + r, CHUNK)
            fields = [a_ref[j - 1, comp, r : r + CHUNK, :] for comp in range(3)]
            weight = w_ref[j - 1, r : r + CHUNK, :]
            for slot in range(2):
                centre, total, drift = [], [], []
                for k in (2 * slot, 2 * slot + 1):
                    mid = source[j, k, here, :]
                    xp = source[j, k, pl.ds(PAD + r + 1, CHUNK), :]
                    xm = source[j, k, pl.ds(PAD + r - 1, CHUNK), :]
                    zp = source[j + 1, k, here, :]
                    zm = source[j - 1, k, here, :]
                    yp, ym = lane_shifts(mid)
                    centre.append(mid)
                    total.append((xp + xm) + (yp + ym) + (zp + zm))
                    drift.append(fields[0] * (xp - xm) + fields[1] * (yp - ym) + fields[2] * (zp - zm))
                real_h = weight * centre[0] - total[0] + drift[1]
                imag_h = weight * centre[1] - total[1] - drift[0]
                for part, change in enumerate((factor * imag_h, -factor * real_h)):
                    value = base_ref[j, 2 * slot + part, here, :] + change
                    target[j + shift, 2 * slot + part, here, :] = value
                    if order == 1 and HALO <= j < HALO + DEPTH:
                        square = value * value
                        if r == 0:
                            square = jnp.where(half == 0, square, 0.0)
                        if r == LOCAL - 8:
                            square = jnp.where(half == 1, square, 0.0)
                        sums[slot] = sums[slot] + square

    source = base_ref
    for done, order in enumerate(range(TERMS, 0, -1)):
        target = out_ref if order == 1 else (ping_ref, pong_ref)[done % 2]
        for j in range(done + 1, WIDE - done - 1):
            plane(j, order, source, target, 1 - HALO if order == 1 else 0)
        source = target
    norm_ref[0] = sums[0]
    norm_ref[1] = sums[1]


def propagate(orbs, weight, vcore, vchip, fields):
    return call(
        "propagate",
        propagate_body,
        [(DEPTH + 2, 4, XL, NY), (2, 8, NY), (DEPTH + 2 * MARGIN, 3, LOCAL, NY)],
        [vmem()] * 15,
        [
            pltpu.VMEM((WIDE, 4, XL, NY), F32),
            pltpu.VMEM((WIDE, 4, XL, NY), F32),
            pltpu.VMEM((WIDE, 4, XL, NY), F32),
            pltpu.VMEM((DEPTH + 2 * MARGIN, LOCAL, NY), F32),
        ],
        flops=60000000,
        limit=32,
    )(*orbs, weight, vcore, vchip, *fields)


def current_body(wide_ref, field_ref, flow_ref):
    low = half_rows((8, NY))

    @pl.loop(0, DEPTH // 2)
    def _(pair):
        for tile in range(TILES):
            r = 8 * tile
            here = pl.ds(PAD + r, 8)
            for slot in range(2):
                both = []
                for z in range(2):
                    j = 2 * pair + z + 1
                    mids, grads = [], []
                    for k in (2 * slot, 2 * slot + 1):
                        mid = wide_ref[j, k, here, :]
                        yp, ym = lane_shifts(mid)
                        mids.append(mid)
                        grads.append(
                            (
                                wide_ref[j, k, pl.ds(PAD + r + 1, 8), :] - wide_ref[j, k, pl.ds(PAD + r - 1, 8), :],
                                yp - ym,
                                wide_ref[j + 1, k, here, :] - wide_ref[j - 1, k, here, :],
                            )
                        )
                    u, w = mids
                    density = u * u + w * w
                    both.append(
                        [
                            0.5 * (u * grads[1][comp] - w * grads[0][comp])
                            + field_ref[j + MARGIN - 1, comp, r : r + 8, :] * density
                            for comp in range(3)
                        ]
                    )
                for comp in range(3):
                    even, odd = both[0][comp], both[1][comp]
                    rows = pl.ds(pl.multiple_of((comp * DEPTH + 2 * pair) * ROWS, 8), 8)
                    flow_ref[slot, tile, 0, rows, :] = jnp.where(low, even, pltpu.roll(odd, 4, 0))
                    flow_ref[slot, tile, 1, rows, :] = jnp.where(low, pltpu.roll(even, 4, 0), odd)


def current(wide, field):
    return call("current", current_body, [(2, TILES, 2, PACK, NY)], [vmem(), vmem()], flops=10000000, limit=10)(
        wide, field
    )[0]


def weigh_body(occ_ref, occx_ref, prior_ref, n_ref, nchip_ref, nhalf_ref, nboth_ref, flow_ref, out_ref, scale_ref):
    half = half_index()
    weights = []
    for slot, occ in enumerate((occ_ref, occx_ref)):
        sums = (n_ref[slot] + nchip_ref[slot]) + (nhalf_ref[1 - slot] + nboth_ref[1 - slot])
        norm = jnp.sum(jnp.sum(sums, axis=1, keepdims=True), axis=0, keepdims=True)
        prior = prior_ref[slot, 0:1, :]
        mean = prior * prior * (norm * (1.0 / CELLS)) + EPSILON
        scale = prior / jnp.sqrt(mean)
        scale_ref[slot] = jnp.broadcast_to(scale, (8, NY))
        weights.append(scale * scale * (occ[0] * (1.0 / ORBS)))

    @pl.loop(0, GROUP // 2)
    def _(i):
        for side in range(2):
            out_ref[i, side] = flow_ref[0, i + half, side] * weights[0] + flow_ref[1, i + half, side] * weights[1]


def weigh(occupations, prior, norms, flow):
    return call(
        "weigh", weigh_body, [(GROUP // 2, 2, PACK, NY), (2, 8, NY)], [smem()] * 2 + [vmem()] * 6, flops=500000
    )(*occupations, prior, *norms, flow)


def curl_body(field_ref, out_ref):
    owner = lax.axis_index("orb")
    place = lax.rem(owner, GROUP)
    tile = place // 2 + half_index()
    odd = lax.rem(place, 2)
    row = lax.broadcasted_iota(jnp.int32, (8, NY), 0)
    keep = ((owner > 0) | (row != 0)) & ((owner < ORBS - 1) | (row != ROWS + 1))
    starts = [pl.multiple_of(8 * jnp.clip(tile + k, 0, TILES - 1), 8) for k in (-1, 0, 1)]

    def window(z, comp):
        before, middle, after = [field_ref[z + MARGIN, comp, pl.ds(s, 8), :] for s in starts]
        first = jnp.where(odd == 1, middle, before)
        second = jnp.where(odd == 1, after, middle)
        shift_first = jnp.where(odd == 1, pltpu.roll(first, 5, 0), pltpu.roll(first, 1, 0))
        shift_second = jnp.where(odd == 1, pltpu.roll(second, 5, 0), pltpu.roll(second, 1, 0))
        split = jnp.where(odd == 1, 5, 1)
        return jnp.where(keep, jnp.where(row < split, shift_first, shift_second), 0.0)

    def x_plus(v):
        return pltpu.roll(v, 7, 0)

    def x_minus(v):
        return pltpu.roll(v, 1, 0)

    planes = [[window(z, comp) for comp in range(3)] for z in range(-1, DEPTH + 1)]
    for z in range(DEPTH):
        ax, ay, az = planes[z + 1]
        axm, aym, azm = planes[z]
        axp, ayp, azp = planes[z + 2]
        ax_up, ax_dn = lane_shifts(ax)
        ay_dn = lane_shifts(ay)[1]
        az_up, az_dn = lane_shifts(az)
        dy_ay = ay - ay_dn
        dx_ax = ax - x_minus(ax)
        inner_x = dy_ay + (az - azm)
        inner_y = dx_ax + (az - azm)
        inner_z = dx_ax + dy_ay
        up_inner_z = (axp - x_minus(axp)) + (ayp - lane_shifts(ayp)[1])
        out_x = (x_plus(inner_x) - inner_x) - (ax_up + ax_dn + axp + axm - 4.0 * ax)
        out_y = (lane_shifts(inner_y)[0] - inner_y) - (x_plus(ay) + x_minus(ay) + ayp + aym - 4.0 * ay)
        out_z = (up_inner_z - inner_z) - (x_plus(az) + x_minus(az) + az_up + az_dn - 4.0 * az)
        for comp, value in enumerate((out_x, out_y, out_z)):
            out_ref[pl.ds((comp * DEPTH + z) * ROWS, ROWS), :] = pltpu.roll(value, 7, 0)[0:ROWS]


def double_curl(field):
    return call("double_curl", curl_body, [(PACK, NY)], [vmem()], flops=1000000)(field)[0]


def update_body(last, got_ref, curl_ref, e_ref, a_ref, *outs):
    total = got_ref[0]
    for i in range(1, GROUP):
        total = total + got_ref[i]
    e_new = e_ref[...] + WAVE_STEP * (curl_ref[...] - total)
    a_new = a_ref[...] - WAVE_STEP * e_new
    if last:
        for ref, value in zip(outs, (e_new, a_new)):
            for comp in range(3):
                for z in range(DEPTH):
                    start = (comp * DEPTH + z) * ROWS
                    ref[comp, pl.ds(z, ROWS, stride=DEPTH), :] = value[start : start + ROWS]
    else:
        copies_ref, a_out_ref, e_out_ref = outs
        a_out_ref[...] = a_new
        e_out_ref[...] = e_new
        for i in range(GROUP):
            copies_ref[i] = a_new


def update(last, got, curl, e_rows, a_rows):
    if last:
        outs = [(3, ROWS * DEPTH, NY)] * 2
    else:
        outs = [(GROUP, PACK, NY), (PACK, NY), (PACK, NY)]
    return call("update", functools.partial(update_body, last), outs, [vmem()] * 4, flops=500000)(got, curl, e_rows, a_rows)


def hand_back_body(wide_ref, out_ref):
    half = half_index()
    for z in range(DEPTH):
        for part in range(2):
            out_ref[z, part] = own_rows(wide_ref[z + 1, 2 + part, PAD : PAD + LOCAL, :], half)


def hand_back(wide):
    return call("hand_back", hand_back_body, [(DEPTH, 2, HALF, NY)], [vmem()])(wide)[0]


def finish_body(scale_ref, wide_ref, theirs_ref, out_ref):
    half = half_index()
    scale = scale_ref[0, 0:1, :]
    for z in range(DEPTH):
        for part in range(2):
            mine = own_rows(wide_ref[z + 1, part, PAD : PAD + LOCAL, :], half) * scale
            theirs = theirs_ref[z, part] * scale
            out_ref[part, pl.ds(z, HALF, stride=DEPTH), :] = jnp.where(half == 0, mine, theirs)
            out_ref[part, pl.ds(HALF * DEPTH + z, HALF, stride=DEPTH), :] = jnp.where(half == 0, theirs, mine)


def finish(scale, wide, theirs):
    return call("finish", finish_body, [(2, NX * DEPTH, NY)], [vmem()] * 3)(scale, wide, theirs)[0]


def everyone(copies):
    return lax.all_to_all(copies, "orb", 0, 0, tiled=True, axis_index_groups=GROUPS)


def per_device(orbitals, potential, occupation, e_field, a_field):
    copies, a_rows = spread(a_field)
    got = everyone(copies)
    own, swap, weight, core, chip, corex, chipx, e_rows = prepare(orbitals, potential, e_field)
    other = send(swap, HALVES)
    vcore, vchip = send(core, CORE), send(chip, CHIP)
    orbs = (own, other, vcore, vchip, send(corex, CORE_ACROSS), send(chipx, CHIP_ACROSS))
    occupations = (occupation, send(occupation, HALVES))
    scale = jnp.ones((2, 8, NY), F32)
    for step in range(STEPS):
        last = step == STEPS - 1
        field, edge, acore, achip, acorex, achipx = assemble(got)
        fields = (
            field,
            send(edge, HALVES),
            send(acore, CORE),
            send(achip, CHIP),
            send(acorex, CORE_ACROSS),
            send(achipx, CHIP_ACROSS),
        )
        wide, norm, field = propagate(orbs, weight, vcore, vchip, fields)
        norm = norm + send(norm, CORE)
        norms = (norm, send(norm, CHIP_SUM), send(norm, HALVES), send(norm, BOTH_SUM))
        flow = current(wide, field)
        flow, scale = weigh(occupations, scale, norms, flow)
        flows = everyone(flow.reshape(GROUP, PACK, NY))
        curl = double_curl(field)
        if not last:
            edge = send(edges(wide), HALVES)
            own, other, core, chip, corex, chipx = rims(wide, edge)
            flows, core, chip, corex, chipx = lax.optimization_barrier((flows, core, chip, corex, chipx))
            orbs = (
                own,
                other,
                send(core, CORE),
                send(chip, CHIP),
                send(corex, CORE),
                send(chipx, CHIP),
            )
            copies, a_rows, e_rows = update(last, flows, curl, e_rows, a_rows)
            got = everyone(copies)
            got, orbs = lax.optimization_barrier((got, orbs))
        else:
            theirs = send(hand_back(wide), HALVES)
            e_new, a_new = update(last, flows, curl, e_rows, a_rows)
            orbitals = finish(scale, wide, theirs)
    return (
        orbitals.reshape(1, 2, NX, DEPTH, NY),
        e_new.reshape(3, ROWS, DEPTH, NY),
        a_new.reshape(3, ROWS, DEPTH, NY),
    )


def solution(mesh):
    return jax.shard_map(
        per_device,
        mesh=mesh,
        in_specs=(
            P("orb", None, None, "slab", None),
            P(None, "slab", None),
            P("orb"),
            P(None, "orb", "slab", None),
            P(None, "orb", "slab", None),
        ),
        out_specs=(
            P("orb", None, None, "slab", None),
            P(None, "orb", "slab", None),
            P(None, "orb", "slab", None),
        ),
        check_vma=False,
    )
```

time: 186 us -> 183 us (0.984)
  starting transfers between devices: 56.2 us -> 84.4 us
  blocking collectives: 25.6 us -> 0 us
  waiting for transfers between devices: 59.8 us -> 49.3 us
  Pallas kernels: 21.4 us -> 24.5 us
    all_to_all x3 -> x4, waiting for transfers between devices: 57.8 us -> 9.5 us  [everyone(): lax.all_to_all(copies, 'orb', 0, 0, tiled=True, axis_index_groups=GROUPS)]
    ppermute x14 -> x30, waiting for transfers between devices: 2.01 us -> 39.8 us  [send(): return lax.ppermute(value, ALL, table)]
    all_to_all x1 -> x0, blocking collectives: 25.6 us -> none  [everyone(): return lax.all_to_all(copies, 'orb', 0, 0, tiled=True)]
    ppermute x14 -> x30, starting transfers between devices: 34.4 us -> 58.3 us  [send(): return lax.ppermute(value, ALL, table)]
    all_to_all x3 -> x4, starting transfers between devices: 21.9 us -> 26.2 us  [everyone(): lax.all_to_all(copies, 'orb', 0, 0, tiled=True, axis_index_groups=GROUPS)]
    pallas_call x14 -> x16, Pallas kernels: 19 us -> 21.7 us  [the longest x2 12.2 us: propagate(): call('propagate', propagate_body, [(DEPTH + 2, 4, XL, NY), (2, 8, NY), (D...]
    unnamed x66 -> x68, local copies, waits for them, and re-layouts: 20.2 us -> 21.5 us
  transfers between devices with their start and end apart: 17 -> 34, of which waited for: 6 -> 13; matrix products, arithmetic and copies ran while one was open for 0% -> 0% of each run, Pallas kernels for 3% -> 4%
where the time goes in v2:
time: 183 us; the launch traced here: 182 us
  starting transfers between devices  84.4 us (46%)
  waiting for transfers between devices  49.3 us (27%)
  Pallas kernels  24.5 us (13%)
  local copies, waits for them, and re-layouts  21.5 us (12%)
    ppermute x30, starting transfers between devices, send(): return lax.ppermute(value, ALL, table)  58.3 us
    ppermute x30, waiting for transfers between devices, send(): return lax.ppermute(value, ALL, table)  39.8 us
    all_to_all x4, starting transfers between devices, everyone(): lax.all_to_all(copies, 'orb', 0, 0, tiled=True, axis_index_groups=GROUPS)  26.2 us
    unnamed x68, local copies, waits for them, and re-layouts  21.5 us
    pallas_call x2, Pallas kernels, propagate(): call('propagate', propagate_body, [(DEPTH + 2, 4, XL, NY), (2, 8, NY), (D...  12.2 us
    all_to_all x4, waiting for transfers between devices, everyone(): lax.all_to_all(copies, 'orb', 0, 0, tiled=True, axis_index_groups=GROUPS)  9.5 us
  transfers between devices with their start and end apart: 34, of which 13 were waited for; matrix products, arithmetic and copies ran while one was open for 0% of the time, Pallas kernels for 4%

profile of v2, /device:TPU:0, one launch (start us, length us, event | category | flops | bytes accessed | tf_op | source)
XLA Modules:
  0.0 181.6 jit_solution(9062327418017124615)
XLA Ops:
  0.6 0.9 copy-done.31
  1.5 1.0 spread.1
  2.5 7.1 %all-to-all-start = ((f32[16,96,128]{2,1,0:T(8,128)}), f32[16,96,128]{2,1,0:T(8,128)S(1)}, u32[]{:S(2)}, u32[]{:S(2)}) async-start(f32[16,96,128]{2,1,0:T(8,128)} %get-tuple-element.65), calls=%async_computation | async-start | bytes 1572864 | tf_op jit(solution)/shard_map/all_to_all | solution.py:553
  9.6 1.0 copy-done.15
  10.7 0.8 copy-done.24
  11.5 1.9 %prepare.1 = (f32[8,2,72,128]{3,2,1,0:T(8,128)S(1)}, f32[8,2,72,128]{3,2,1,0:T(8,128)}, f32[8,72,128]{2,1,0:T(8,128)S(1)}, f32[14,72,128]{2,1,0:T(8,128)}, f32[1...) custom-call(f32[2,1024,128]{2,1,0:T(8,128)S(1)} %bitcast.13, ...), custom_call_target="tpu_custom_call" | custom-call | flops 1000000 | bytes 6586368 | tf_op jit(solution)/shard_map/prepare/pallas_call | solution.py:154
  13.4 0.8 copy-done.7
  14.8 3.0 %collective-permute-start.4 = (f32[10,72,128]{2,1,0:T(8,128)}, f32[10,72,128]{2,1,0:T(8,128)S(1)}, u32[]{:S(2)}, u32[]{:S(2)}) collective-permute-start(f32[10,72,128]{2,1,0:T(8,128)} %get-tuple-element.62), channel_id=1, source_target_pairs={{0,65},{1,64},{2,67},{3,66},{4,69},{5,68},{6,71},{7,70},{8,73},{9,... | collective-permute-start | bytes 1105928 | tf_op jit(solution)/shard_map/ppermute | solution.py:70
  18.5 0.9 collective-permute-start.1
  19.4 3.3 %collective-permute-start.2 = (f32[14,72,128]{2,1,0:T(8,128)}, f32[14,72,128]{2,1,0:T(8,128)S(1)}, u32[]{:S(2)}, u32[]{:S(2)}) collective-permute-start(f32[14,72,128]{2,1,0:T(8,128)} %get-tuple-element.60), channel_id=1, source_target_pairs={{0,1},{1,0},{2,3},{3,2},{4,5},{5,4},{6,7},{7,6},{8,9},{9,8},{10,11... | collective-permute-start | bytes 1548296 | tf_op jit(solution)/shard_map/ppermute | solution.py:70
  24.1 2.8 %collective-permute-done.4.hcorex_ref = f32[10,72,128]{2,1,0:T(8,128)S(1)} collective-permute-done((f32[10,72,128]{2,1,0:T(8,128)}, f32[10,72,128]{2,1,0:T(8,128)S(1)}, u32[]{:S(2)}, u32[]{:S(2)}) %collective-permute-start.4) | collective-permute-done | bytes 368672 | tf_op jit(solution)/shard_map/ppermute | solution.py:70
  26.9 1.3 collective-permute-start.7
  28.2 0.7 copy-done.16
  29.6 3.2 %collective-permute-start.6 = (f32[8,3,8,128]{3,2,1,0:T(8,128)S(1)}, f32[8,3,8,128]{3,2,1,0:T(8,128)S(1)}, u32[]{:S(2)}, u32[]{:S(2)}) collective-permute-start(f32[8,3,8,128]{3,2,1,0:T(8,128)S(1)} %get-tuple-element.67), channel_id=1, source_target_pairs={{0,64},{1,65},{2,66},{3,67},{4,68},{5,69},{6,70},{7,71},{8,72},{9,... | collective-permute-start | bytes 294920 | tf_op jit(solution)/shard_map/ppermute | solution.py:70
  32.9 19.9 %collective-permute-start.9 = (f32[4,3,8,128]{3,2,1,0:T(8,128)S(1)}, f32[4,3,8,128]{3,2,1,0:T(8,128)S(1)}, u32[]{:S(2)}, u32[]{:S(2)}) collective-permute-start(f32[4,3,8,128]{3,2,1,0:T(8,128)S(1)} %get-tuple-element.70), channel_id=1, source_target_pairs={{0,65},{1,64},{2,67},{3,66},{4,69},{5,68},{6,71},{7,70},{8,73},{9,... | collective-permute-start | bytes 147464 | tf_op jit(solution)/shard_map/ppermute | solution.py:70
  52.8 0.8 copy-done.9
  54.3 5.9 %collective-permute-done.9.acorex_ref = f32[4,3,8,128]{3,2,1,0:T(8,128)S(1)} collective-permute-done((f32[4,3,8,128]{3,2,1,0:T(8,128)S(1)}, f32[4,3,8,128]{3,2,1,0:T(8,128)S(1)}, u32[]{:S(2)}, u32[]{:S(2)}) %collective-permute-start.9) | collective-permute-done | bytes 49184 | tf_op jit(solution)/shard_map/ppermute | solution.py:70
  60.2 1.1 copy-done.8
  61.3 1.1 copy-done.10
  62.3 1.0 copy-done.17
  63.3 6.1 %propagate.2 = (f32[10,4,88,128]{3,2,1,0:T(8,128)S(1)}, f32[2,8,128]{2,1,0:T(8,128)S(1)}, f32[16,3,72,128]{3,2,1,0:T(8,128)S(1)}) custom-call(f32[8,2,72,128]{3,2,1,0:T(8,128)S(1)} %copy-done.8, f32[8,2,72,128]{3,2,1,0:T(8,128)S(1)} %copy-done.10, f32[14,72,128]{2,1,0:T(8,128)S(1)} %collective-permute-done.2.hcore_ref.vcore_ref, ...), custom_call_target="tpu_custom_call" | custom-call | flops 60000000 | bytes 7159808 | tf_op jit(solution)/shard_map/propagate/pallas_call | solution.py:363
  69.8 0.9 collective-permute-done.11
  71.1 1.1 collective-permute-start.13
  72.3 2.5 %collective-permute-start.12 = (f32[2,8,128]{2,1,0:T(8,128)S(1)}, f32[2,8,128]{2,1,0:T(8,128)S(1)}, u32[]{:S(2)}, u32[]{:S(2)}) collective-permute-start(f32[2,8,128]{2,1,0:T(8,128)S(1)} %add.6.n_ref), channel_id=1, source_target_pairs={{0,2},{1,3},{2,0},{3,1},{4,6},{5,7},{6,4},{7,5},{8,10},{9,11},{10,... | collective-permute-start | bytes 24584 | tf_op jit(solution)/shard_map/ppermute | solution.py:70
  76.1 1.0 current.2.flow_ref
  77.1 2.9 %collective-permute-done.occx_ref = f32[1]{0:T(128)} collective-permute-done((f32[1]{0:T(128)}, f32[1]{0:T(128)}, u32[]{:S(2)}, u32[]{:S(2)}) %collective-permute-start) | collective-permute-done | bytes 36 | tf_op jit(solution)/shard_map/ppermute | solution.py:70
  79.9 0.9 weigh.2
  80.9 0.9 copy-done.5
  81.7 7.0 %all-to-all-start.1 = ((f32[16,96,128]{2,1,0:T(8,128)}), f32[16,96,128]{2,1,0:T(8,128)}, u32[]{:S(2)}, u32[]{:S(2)}) async-start(f32[16,96,128]{2,1,0:T(8,128)} %bitcast.14), calls=%async_computation.1 | async-start | bytes 1572864 | tf_op jit(solution)/shard_map/all_to_all | solution.py:553
  89.5 0.7 copy-done.1
  90.3 5.0 %collective-permute-done.15.edge_ref = f32[8,4,8,128]{3,2,1,0:T(8,128)S(1)} collective-permute-done((f32[8,4,8,128]{3,2,1,0:T(8,128)S(1)}, f32[8,4,8,128]{3,2,1,0:T(8,128)S(1)}, u32[]{:S(2)}, u32[]{:S(2)}) %collective-permute-start.15) | collective-permute-done | bytes 131104 | tf_op jit(solution)/shard_map/ppermute | solution.py:70
  95.3 1.0 rims.1
  96.4 0.8 copy-done.11
  97.2 0.8 copy-done.13
  98.0 0.7 copy-done.32
  98.8 0.7 copy-done.33
  99.5 2.2 %all-to-all-done.1.got_ref = f32[16,96,128]{2,1,0:T(8,128)} async-done(((f32[16,96,128]{2,1,0:T(8,128)}), f32[16,96,128]{2,1,0:T(8,128)}, u32[]{:S(2)}, u32[]{:S(2)}) %all-to-all-start.1) | async-done | bytes 786464 | tf_op jit(solution)/shard_map/all_to_all | solution.py:553
  101.7 2.1 %update.2 = (f32[16,96,128]{2,1,0:T(8,128)}, f32[96,128]{1,0:T(8,128)S(1)}, f32[96,128]{1,0:T(8,128)S(1)}) custom-call(f32[16,96,128]{2,1,0:T(8,128)} %all-to-all-done.1.got_ref, f32[96,128]{1,0:T(8,128)S(1)} %double_curl.2.curl_ref, f32[96,128]{1,0:T(8,128)S(1)} %copy-done.26, f32[96,128]{1,0:T(8,128)S(1)} %get-tuple-element.83.a_ref), custom_call_target="tpu_custom_call" | custom-call | flops 500000 | bytes 1769472 | tf_op jit(solution)/shard_map/update/pallas_call | solution.py:523
  105.1 4.9 %all-to-all-start.2 = ((f32[16,96,128]{2,1,0:T(8,128)}), f32[16,96,128]{2,1,0:T(8,128)S(1)}, u32[]{:S(2)}, u32[]{:S(2)}) async-start(f32[16,96,128]{2,1,0:T(8,128)} %get-tuple-element.84), calls=%async_computation.2 | async-start | bytes 1572864 | tf_op jit(solution)/shard_map/all_to_all | solution.py:553
  110.8 1.8 collective-permute-start.18
  113.3 0.8 collective-permute-done.18.hcorex_ref
  114.2 0.8 copy-done.22
  114.9 6.7 %all-to-all-done.2 = f32[16,96,128]{2,1,0:T(8,128)S(1)} async-done(((f32[16,96,128]{2,1,0:T(8,128)}), f32[16,96,128]{2,1,0:T(8,128)S(1)}, u32[]{:S(2)}, u32[]{:S(2)}) %all-to-all-start.2) | async-done | bytes 786464 | tf_op jit(solution)/shard_map/all_to_all | solution.py:553
  121.8 2.8 %collective-permute-start.21 = (f32[4,3,64,128]{3,2,1,0:T(8,128)S(1)}, f32[4,3,64,128]{3,2,1,0:T(8,128)S(1)}, u32[]{:S(2)}, u32[]{:S(2)}) collective-permute-start(f32[4,3,64,128]{3,2,1,0:T(8,128)S(1)} %get-tuple-element.100), channel_id=1, source_target_pairs={{0,1},{1,0},{2,3},{3,2},{4,5},{5,4},{6,7},{7,6},{8,9},{9,8},{10,11... | collective-permute-start | bytes 1179656 | tf_op jit(solution)/shard_map/ppermute | solution.py:70
  126.0 3.5 %collective-permute-start.23 = (f32[4,3,8,128]{3,2,1,0:T(8,128)S(1)}, f32[4,3,8,128]{3,2,1,0:T(8,128)S(1)}, u32[]{:S(2)}, u32[]{:S(2)}) collective-permute-start(f32[4,3,8,128]{3,2,1,0:T(8,128)S(1)} %get-tuple-element.102), channel_id=1, source_target_pairs={{0,65},{1,64},{2,67},{3,66},{4,69},{5,68},{6,71},{7,70},{8,73},{9,... | collective-permute-start | bytes 147464 | tf_op jit(solution)/shard_map/ppermute | solution.py:70
  130.1 6.5 %collective-permute-done.23.acorex_ref = f32[4,3,8,128]{3,2,1,0:T(8,128)S(1)} collective-permute-done((f32[4,3,8,128]{3,2,1,0:T(8,128)S(1)}, f32[4,3,8,128]{3,2,1,0:T(8,128)S(1)}, u32[]{:S(2)}, u32[]{:S(2)}) %collective-permute-start.23) | collective-permute-done | bytes 49184 | tf_op jit(solution)/shard_map/ppermute | solution.py:70
  136.7 1.1 copy-done.12
  137.8 1.1 copy-done.14
  138.8 1.0 copy-done.19
  139.8 1.0 copy-done.21
  140.8 1.0 copy-done.23
  141.8 6.1 %propagate.3 = (f32[10,4,88,128]{3,2,1,0:T(8,128)S(1)}, f32[2,8,128]{2,1,0:T(8,128)S(1)}, f32[16,3,72,128]{3,2,1,0:T(8,128)S(1)}) custom-call(f32[8,2,72,128]{3,2,1,0:T(8,128)S(1)} %copy-done.12, f32[8,2,72,128]{3,2,1,0:T(8,128)S(1)} %copy-done.14, f32[10,72,128]{2,1,0:T(8,128)S(1)} %collective-permute-done.16.hcore_ref, f32[10,72,128]{2,1,0:T(8,128)S(1)} %copy-done.19, ...), custom_call_target="tpu_custom_call" | custom-call | flops 60000000 | bytes 7159808 | tf_op jit(solution)/shard_map/propagate/pallas_call | solution.py:363
  148.2 0.9 collective-permute-done.25
  149.1 2.5 %collective-permute-start.28 = (f32[2,8,128]{2,1,0:T(8,128)S(1)}, f32[2,8,128]{2,1,0:T(8,128)S(1)}, u32[]{:S(2)}, u32[]{:S(2)}) collective-permute-start(f32[2,8,128]{2,1,0:T(8,128)S(1)} %add.7.n_ref), channel_id=1, source_target_pairs={{0,66},{1,67},{2,64},{3,65},{4,70},{5,71},{6,68},{7,69},{8,74},{9,... | collective-permute-start | bytes 24584 | tf_op jit(solution)/shard_map/ppermute | solution.py:70
  151.6 1.6 collective-permute-start.26
  153.2 1.0 current.3.flow_ref
  154.2 2.5 %collective-permute-done.27.nhalf_ref = f32[2,8,128]{2,1,0:T(8,128)S(1)} collective-permute-done((f32[2,8,128]{2,1,0:T(8,128)S(1)}, f32[2,8,128]{2,1,0:T(8,128)S(1)}, u32[]{:S(2)}, u32[]{:S(2)}) %collective-permute-start.27) | collective-permute-done | bytes 8224 | tf_op jit(solution)/shard_map/ppermute | solution.py:70
  156.7 0.9 weigh.3
  157.7 0.9 copy-done.6
  158.6 7.1 %all-to-all-start.3 = ((f32[16,96,128]{2,1,0:T(8,128)}), f32[16,96,128]{2,1,0:T(8,128)S(1)}, u32[]{:S(2)}, u32[]{:S(2)}) async-start(f32[16,96,128]{2,1,0:T(8,128)} %bitcast.15), calls=%async_computation.3 | async-start | bytes 1572864 | tf_op jit(solution)/shard_map/all_to_all | solution.py:553
  165.8 2.1 %collective-permute-start.29 = (f32[8,2,64,128]{3,2,1,0:T(8,128)S(1)}, f32[8,2,64,128]{3,2,1,0:T(8,128)S(1)}, u32[]{:S(2)}, u32[]{:S(2)}) collective-permute-start(f32[8,2,64,128]{3,2,1,0:T(8,128)S(1)} %hand_back.1), channel_id=1, source_target_pairs={{0,64},{1,65},{2,66},{3,67},{4,68},{5,69},{6,70},{7,71},{8,72},{9,... | collective-permute-start | bytes 1572872 | tf_op jit(solution)/shard_map/ppermute | solution.py:70
  168.0 11.6 %collective-permute-done.29.theirs_ref = f32[8,2,64,128]{3,2,1,0:T(8,128)S(1)} collective-permute-done((f32[8,2,64,128]{3,2,1,0:T(8,128)S(1)}, f32[8,2,64,128]{3,2,1,0:T(8,128)S(1)}, u32[]{:S(2)}, u32[]{:S(2)}) %collective-permute-start.29) | collective-permute-done | bytes 524320 | tf_op jit(solution)/shard_map/ppermute | solution.py:70
  179.6 1.3 finish.1
  180.9 0.7 update.3
  (93 shorter events, 11.8 us)
Async XLA Ops:
  0.6 9.0 %copy-start.4 = (f32[1,2,128,8,128]{4,3,2,1,0:T(8,128)S(1)}, f32[1,2,128,8,128]{4,3,2,1,0:T(8,128)}, u32[]{:S(2)}) copy-start(f32[1,2,128,8,128]{4,3,2,1,0:T(8,128)} %param.5) | copy-start | bytes 3145732
  0.6 0.9 copy-start.31
  2.5 21.5 %all-to-all-start = ((f32[16,96,128]{2,1,0:T(8,128)}), f32[16,96,128]{2,1,0:T(8,128)S(1)}, u32[]{:S(2)}, u32[]{:S(2)}) async-start(f32[16,96,128]{2,1,0:T(8,128)} %get-tuple-element.65), calls=%async_computation | async-start | bytes 1572864 | tf_op jit(solution)/shard_map/all_to_all | solution.py:553
  9.6 1.0 copy-start.15
  10.7 0.8 copy-start.24
  13.4 0.8 copy-start.7
  14.8 12.1 %collective-permute-start.4 = (f32[10,72,128]{2,1,0:T(8,128)}, f32[10,72,128]{2,1,0:T(8,128)S(1)}, u32[]{:S(2)}, u32[]{:S(2)}) collective-permute-start(f32[10,72,128]{2,1,0:T(8,128)} %get-tuple-element.62), channel_id=1, source_target_pairs={{0,65},{1,64},{2,67},{3,66},{4,69},{5,68},{6,71},{7,70},{8,73},{9,... | collective-permute-start | bytes 1105928 | tf_op jit(solution)/shard_map/ppermute | solution.py:70
  17.8 10.4 %collective-permute-start.5 = (f32[10,72,128]{2,1,0:T(8,128)}, f32[10,72,128]{2,1,0:T(8,128)S(1)}, u32[]{:S(2)}, u32[]{:S(2)}) collective-permute-start(f32[10,72,128]{2,1,0:T(8,128)} %get-tuple-element.63), channel_id=1, source_target_pairs={{1,66},{2,65},{5,70},{6,69},{9,74},{10,73},{13,78},{14,77},{17,82}... | collective-permute-start | bytes 1105928 | tf_op jit(solution)/shard_map/ppermute | solution.py:70
  18.5 34.3 %collective-permute-start.1 = (f32[8,2,72,128]{3,2,1,0:T(8,128)}, f32[8,2,72,128]{3,2,1,0:T(8,128)S(1)}, u32[]{:S(2)}, u32[]{:S(2)}) collective-permute-start(f32[8,2,72,128]{3,2,1,0:T(8,128)} %get-tuple-element.59), channel_id=1, source_target_pairs={{0,64},{1,65},{2,66},{3,67},{4,68},{5,69},{6,70},{7,71},{8,72},{9,... | collective-permute-start | bytes 1769480 | tf_op jit(solution)/shard_map/ppermute | solution.py:70
  19.4 10.2 %collective-permute-start.2 = (f32[14,72,128]{2,1,0:T(8,128)}, f32[14,72,128]{2,1,0:T(8,128)S(1)}, u32[]{:S(2)}, u32[]{:S(2)}) collective-permute-start(f32[14,72,128]{2,1,0:T(8,128)} %get-tuple-element.60), channel_id=1, source_target_pairs={{0,1},{1,0},{2,3},{3,2},{4,5},{5,4},{6,7},{7,6},{8,9},{9,8},{10,11... | collective-permute-start | bytes 1548296 | tf_op jit(solution)/shard_map/ppermute | solution.py:70
  22.7 10.1 %collective-permute-start.3 = (f32[14,72,128]{2,1,0:T(8,128)}, f32[14,72,128]{2,1,0:T(8,128)S(1)}, u32[]{:S(2)}, u32[]{:S(2)}) collective-permute-start(f32[14,72,128]{2,1,0:T(8,128)} %get-tuple-element.61), channel_id=1, source_target_pairs={{1,2},{2,1},{5,6},{6,5},{9,10},{10,9},{13,14},{14,13},{17,18},{18,... | collective-permute-start | bytes 1548296 | tf_op jit(solution)/shard_map/ppermute | solution.py:70
  26.9 33.3 %collective-permute-start.7 = (f32[4,3,64,128]{3,2,1,0:T(8,128)S(1)}, f32[4,3,64,128]{3,2,1,0:T(8,128)S(1)}, u32[]{:S(2)}, u32[]{:S(2)}) collective-permute-start(f32[4,3,64,128]{3,2,1,0:T(8,128)S(1)} %get-tuple-element.68), channel_id=1, source_target_pairs={{0,1},{1,0},{2,3},{3,2},{4,5},{5,4},{6,7},{7,6},{8,9},{9,8},{10,11... | collective-permute-start | bytes 1179656 | tf_op jit(solution)/shard_map/ppermute | solution.py:70
  29.0 31.2 %collective-permute-start.8 = (f32[4,3,64,128]{3,2,1,0:T(8,128)S(1)}, f32[4,3,64,128]{3,2,1,0:T(8,128)S(1)}, u32[]{:S(2)}, u32[]{:S(2)}) collective-permute-start(f32[4,3,64,128]{3,2,1,0:T(8,128)S(1)} %get-tuple-element.69), channel_id=1, source_target_pairs={{1,2},{2,1},{5,6},{6,5},{9,10},{10,9},{13,14},{14,13},{17,18},{18,... | collective-permute-start | bytes 1179656 | tf_op jit(solution)/shard_map/ppermute | solution.py:70
  29.6 30.5 %collective-permute-start.6 = (f32[8,3,8,128]{3,2,1,0:T(8,128)S(1)}, f32[8,3,8,128]{3,2,1,0:T(8,128)S(1)}, u32[]{:S(2)}, u32[]{:S(2)}) collective-permute-start(f32[8,3,8,128]{3,2,1,0:T(8,128)S(1)} %get-tuple-element.67), channel_id=1, source_target_pairs={{0,64},{1,65},{2,66},{3,67},{4,68},{5,69},{6,70},{7,71},{8,72},{9,... | collective-permute-start | bytes 294920 | tf_op jit(solution)/shard_map/ppermute | solution.py:70
  32.9 27.3 %collective-permute-start.9 = (f32[4,3,8,128]{3,2,1,0:T(8,128)S(1)}, f32[4,3,8,128]{3,2,1,0:T(8,128)S(1)}, u32[]{:S(2)}, u32[]{:S(2)}) collective-permute-start(f32[4,3,8,128]{3,2,1,0:T(8,128)S(1)} %get-tuple-element.70), channel_id=1, source_target_pairs={{0,65},{1,64},{2,67},{3,66},{4,69},{5,68},{6,71},{7,70},{8,73},{9,... | collective-permute-start | bytes 147464 | tf_op jit(solution)/shard_map/ppermute | solution.py:70
  52.8 0.8 copy-start.9
  53.6 6.6 %collective-permute-start.10 = (f32[4,3,8,128]{3,2,1,0:T(8,128)S(1)}, f32[4,3,8,128]{3,2,1,0:T(8,128)S(1)}, u32[]{:S(2)}, u32[]{:S(2)}) collective-permute-start(f32[4,3,8,128]{3,2,1,0:T(8,128)S(1)} %get-tuple-element.71), channel_id=1, source_target_pairs={{1,66},{2,65},{5,70},{6,69},{9,74},{10,73},{13,78},{14,77},{17,82}... | collective-permute-start | bytes 147464 | tf_op jit(solution)/shard_map/ppermute | solution.py:70
  60.2 1.1 copy-start.8
  61.3 1.1 copy-start.10
  62.3 1.0 copy-start.17
  69.4 7.6 %copy-start = (f32[16,3,72,128]{3,2,1,0:T(8,128)}, f32[16,3,72,128]{3,2,1,0:T(8,128)S(1)}, u32[]{:S(2)}) copy-start(f32[16,3,72,128]{3,2,1,0:T(8,128)S(1)} %get-tuple-element.74.field_ref) | copy-start | bytes 5308420
  69.4 1.3 collective-permute-start.11
  70.7 9.2 %collective-permute-start.14 = (f32[2,8,128]{2,1,0:T(8,128)S(1)}, f32[2,8,128]{2,1,0:T(8,128)S(1)}, u32[]{:S(2)}, u32[]{:S(2)}) collective-permute-start(f32[2,8,128]{2,1,0:T(8,128)S(1)} %add.6.n_ref), channel_id=1, source_target_pairs={{0,66},{1,67},{2,64},{3,65},{4,70},{5,71},{6,68},{7,69},{8,74},{9,... | collective-permute-start | bytes 24584 | tf_op jit(solution)/shard_map/ppermute | solution.py:70
  71.1 8.8 %collective-permute-start.13 = (f32[2,8,128]{2,1,0:T(8,128)S(1)}, f32[2,8,128]{2,1,0:T(8,128)S(1)}, u32[]{:S(2)}, u32[]{:S(2)}) collective-permute-start(f32[2,8,128]{2,1,0:T(8,128)S(1)} %add.6.n_ref), channel_id=1, source_target_pairs={{0,64},{1,65},{2,66},{3,67},{4,68},{5,69},{6,70},{7,71},{8,72},{9,... | collective-permute-start | bytes 24584 | tf_op jit(solution)/shard_map/ppermute | solution.py:70
  72.3 7.7 %collective-permute-start.12 = (f32[2,8,128]{2,1,0:T(8,128)S(1)}, f32[2,8,128]{2,1,0:T(8,128)S(1)}, u32[]{:S(2)}, u32[]{:S(2)}) collective-permute-start(f32[2,8,128]{2,1,0:T(8,128)S(1)} %add.6.n_ref), channel_id=1, source_target_pairs={{0,2},{1,3},{2,0},{3,1},{4,6},{5,7},{6,4},{7,5},{8,10},{9,11},{10,... | collective-permute-start | bytes 24584 | tf_op jit(solution)/shard_map/ppermute | solution.py:70
  74.8 5.1 %collective-permute-start = (f32[1]{0:T(128)}, f32[1]{0:T(128)}, u32[]{:S(2)}, u32[]{:S(2)}) collective-permute-start(f32[1]{0:T(128)} %param.7), channel_id=1, source_target_pairs={{0,64},{1,65},{2,66},{3,67},{4,68},{5,69},{6,70},{7,71},{8,72},{9,... | collective-permute-start | bytes 20 | tf_op jit(solution)/shard_map/ppermute | solution.py:70
  80.9 0.9 copy-start.5
  81.7 20.0 %all-to-all-start.1 = ((f32[16,96,128]{2,1,0:T(8,128)}), f32[16,96,128]{2,1,0:T(8,128)}, u32[]{:S(2)}, u32[]{:S(2)}) async-start(f32[16,96,128]{2,1,0:T(8,128)} %bitcast.14), calls=%async_computation.1 | async-start | bytes 1572864 | tf_op jit(solution)/shard_map/all_to_all | solution.py:553
  88.7 1.5 copy-start.1
  88.8 13.0 %copy-start.26 = (f32[96,128]{1,0:T(8,128)S(1)}, f32[96,128]{1,0:T(8,128)}, u32[]{:S(2)}) copy-start(f32[96,128]{1,0:T(8,128)} %copy-done.25) | copy-start | bytes 147460
  88.8 6.6 %collective-permute-start.15 = (f32[8,4,8,128]{3,2,1,0:T(8,128)S(1)}, f32[8,4,8,128]{3,2,1,0:T(8,128)S(1)}, u32[]{:S(2)}, u32[]{:S(2)}) collective-permute-start(f32[8,4,8,128]{3,2,1,0:T(8,128)S(1)} %edges.1), channel_id=1, source_target_pairs={{0,64},{1,65},{2,66},{3,67},{4,68},{5,69},{6,70},{7,71},{8,72},{9,... | collective-permute-start | bytes 393224 | tf_op jit(solution)/shard_map/ppermute | solution.py:70
  96.4 0.8 copy-start.11
  97.2 0.8 copy-start.13
  98.0 0.7 copy-start.32
  98.8 0.7 copy-start.33
  105.1 16.6 %all-to-all-start.2 = ((f32[16,96,128]{2,1,0:T(8,128)}), f32[16,96,128]{2,1,0:T(8,128)S(1)}, u32[]{:S(2)}, u32[]{:S(2)}) async-start(f32[16,96,128]{2,1,0:T(8,128)} %get-tuple-element.84), calls=%async_computation.2 | async-start | bytes 1572864 | tf_op jit(solution)/shard_map/all_to_all | solution.py:553
  110.0 3.3 %collective-permute-start.16 = (f32[10,72,128]{2,1,0:T(8,128)}, f32[10,72,128]{2,1,0:T(8,128)S(1)}, u32[]{:S(2)}, u32[]{:S(2)}) collective-permute-start(f32[10,72,128]{2,1,0:T(8,128)} %get-tuple-element.87), channel_id=1, source_target_pairs={{0,1},{1,0},{2,3},{3,2},{4,5},{5,4},{6,7},{7,6},{8,9},{9,8},{10,11... | collective-permute-start | bytes 1105928 | tf_op jit(solution)/shard_map/ppermute | solution.py:70
  110.1 3.2 %collective-permute-start.17 = (f32[10,72,128]{2,1,0:T(8,128)}, f32[10,72,128]{2,1,0:T(8,128)S(1)}, u32[]{:S(2)}, u32[]{:S(2)}) collective-permute-start(f32[10,72,128]{2,1,0:T(8,128)} %get-tuple-element.88), channel_id=1, source_target_pairs={{1,2},{2,1},{5,6},{6,5},{9,10},{10,9},{13,14},{14,13},{17,18},{18,... | collective-permute-start | bytes 1105928 | tf_op jit(solution)/shard_map/ppermute | solution.py:70
  110.8 3.3 %collective-permute-start.18 = (f32[10,72,128]{2,1,0:T(8,128)}, f32[10,72,128]{2,1,0:T(8,128)S(1)}, u32[]{:S(2)}, u32[]{:S(2)}) collective-permute-start(f32[10,72,128]{2,1,0:T(8,128)} %copy-done.33), channel_id=1, source_target_pairs={{0,1},{1,0},{2,3},{3,2},{4,5},{5,4},{6,7},{7,6},{8,9},{9,8},{10,11... | collective-permute-start | bytes 1105928 | tf_op jit(solution)/shard_map/ppermute | solution.py:70
  112.6 1.5 collective-permute-start.19
  113.3 23.3 %copy-start.18 = (f32[10,72,128]{2,1,0:T(8,128)}, f32[10,72,128]{2,1,0:T(8,128)S(1)}, u32[]{:S(2)}) copy-start(f32[10,72,128]{2,1,0:T(8,128)S(1)} %collective-permute-done.17.hchip_ref) | copy-start | bytes 1105924
  114.2 22.5 %copy-start.20 = (f32[10,72,128]{2,1,0:T(8,128)}, f32[10,72,128]{2,1,0:T(8,128)S(1)}, u32[]{:S(2)}) copy-start(f32[10,72,128]{2,1,0:T(8,128)S(1)} %collective-permute-done.18.hcorex_ref) | copy-start | bytes 1105924
  114.2 0.8 copy-start.22
  121.8 14.8 %collective-permute-start.21 = (f32[4,3,64,128]{3,2,1,0:T(8,128)S(1)}, f32[4,3,64,128]{3,2,1,0:T(8,128)S(1)}, u32[]{:S(2)}, u32[]{:S(2)}) collective-permute-start(f32[4,3,64,128]{3,2,1,0:T(8,128)S(1)} %get-tuple-element.100), channel_id=1, source_target_pairs={{0,1},{1,0},{2,3},{3,2},{4,5},{5,4},{6,7},{7,6},{8,9},{9,8},{10,11... | collective-permute-start | bytes 1179656 | tf_op jit(solution)/shard_map/ppermute | solution.py:70
  124.6 12.1 %collective-permute-start.22 = (f32[4,3,64,128]{3,2,1,0:T(8,128)S(1)}, f32[4,3,64,128]{3,2,1,0:T(8,128)S(1)}, u32[]{:S(2)}, u32[]{:S(2)}) collective-permute-start(f32[4,3,64,128]{3,2,1,0:T(8,128)S(1)} %get-tuple-element.101), channel_id=1, source_target_pairs={{1,2},{2,1},{5,6},{6,5},{9,10},{10,9},{13,14},{14,13},{17,18},{18,... | collective-permute-start | bytes 1179656 | tf_op jit(solution)/shard_map/ppermute | solution.py:70
  125.3 11.4 %collective-permute-start.20 = (f32[8,3,8,128]{3,2,1,0:T(8,128)S(1)}, f32[8,3,8,128]{3,2,1,0:T(8,128)S(1)}, u32[]{:S(2)}, u32[]{:S(2)}) collective-permute-start(f32[8,3,8,128]{3,2,1,0:T(8,128)S(1)} %get-tuple-element.99), channel_id=1, source_target_pairs={{0,64},{1,65},{2,66},{3,67},{4,68},{5,69},{6,70},{7,71},{8,72},{9,... | collective-permute-start | bytes 294920 | tf_op jit(solution)/shard_map/ppermute | solution.py:70
  126.0 10.7 %collective-permute-start.23 = (f32[4,3,8,128]{3,2,1,0:T(8,128)S(1)}, f32[4,3,8,128]{3,2,1,0:T(8,128)S(1)}, u32[]{:S(2)}, u32[]{:S(2)}) collective-permute-start(f32[4,3,8,128]{3,2,1,0:T(8,128)S(1)} %get-tuple-element.102), channel_id=1, source_target_pairs={{0,65},{1,64},{2,67},{3,66},{4,69},{5,68},{6,71},{7,70},{8,73},{9,... | collective-permute-start | bytes 147464 | tf_op jit(solution)/shard_map/ppermute | solution.py:70
  129.5 7.2 %collective-permute-start.24 = (f32[4,3,8,128]{3,2,1,0:T(8,128)S(1)}, f32[4,3,8,128]{3,2,1,0:T(8,128)S(1)}, u32[]{:S(2)}, u32[]{:S(2)}) collective-permute-start(f32[4,3,8,128]{3,2,1,0:T(8,128)S(1)} %get-tuple-element.103), channel_id=1, source_target_pairs={{1,66},{2,65},{5,70},{6,69},{9,74},{10,73},{13,78},{14,77},{17,82}... | collective-permute-start | bytes 147464 | tf_op jit(solution)/shard_map/ppermute | solution.py:70
  136.7 1.1 copy-start.12
  137.7 1.1 copy-start.14
  138.8 1.0 copy-start.19
  139.8 1.0 copy-start.21
  140.8 1.0 copy-start.23
  147.9 6.3 %copy-start.2 = (f32[16,3,72,128]{3,2,1,0:T(8,128)}, f32[16,3,72,128]{3,2,1,0:T(8,128)S(1)}, u32[]{:S(2)}) copy-start(f32[16,3,72,128]{3,2,1,0:T(8,128)S(1)} %get-tuple-element.106.field_ref) | copy-start | bytes 5308420
  147.9 1.3 collective-permute-start.25
  149.1 5.1 %collective-permute-start.28 = (f32[2,8,128]{2,1,0:T(8,128)S(1)}, f32[2,8,128]{2,1,0:T(8,128)S(1)}, u32[]{:S(2)}, u32[]{:S(2)}) collective-permute-start(f32[2,8,128]{2,1,0:T(8,128)S(1)} %add.7.n_ref), channel_id=1, source_target_pairs={{0,66},{1,67},{2,64},{3,65},{4,70},{5,71},{6,68},{7,69},{8,74},{9,... | collective-permute-start | bytes 24584 | tf_op jit(solution)/shard_map/ppermute | solution.py:70
  151.6 5.2 %collective-permute-start.27 = (f32[2,8,128]{2,1,0:T(8,128)S(1)}, f32[2,8,128]{2,1,0:T(8,128)S(1)}, u32[]{:S(2)}, u32[]{:S(2)}) collective-permute-start(f32[2,8,128]{2,1,0:T(8,128)S(1)} %add.7.n_ref), channel_id=1, source_target_pairs={{0,64},{1,65},{2,66},{3,67},{4,68},{5,69},{6,70},{7,71},{8,72},{9,... | collective-permute-start | bytes 24584 | tf_op jit(solution)/shard_map/ppermute | solution.py:70
  151.6 5.2 %collective-permute-start.26 = (f32[2,8,128]{2,1,0:T(8,128)S(1)}, f32[2,8,128]{2,1,0:T(8,128)S(1)}, u32[]{:S(2)}, u32[]{:S(2)}) collective-permute-start(f32[2,8,128]{2,1,0:T(8,128)S(1)} %add.7.n_ref), channel_id=1, source_target_pairs={{0,2},{1,3},{2,0},{3,1},{4,6},{5,7},{6,4},{7,5},{8,10},{9,11},{10,... | collective-permute-start | bytes 24584 | tf_op jit(solution)/shard_map/ppermute | solution.py:70
  157.7 0.9 copy-start.6
  158.6 22.4 %all-to-all-start.3 = ((f32[16,96,128]{2,1,0:T(8,128)}), f32[16,96,128]{2,1,0:T(8,128)S(1)}, u32[]{:S(2)}, u32[]{:S(2)}) async-start(f32[16,96,128]{2,1,0:T(8,128)} %bitcast.15), calls=%async_computation.3 | async-start | bytes 1572864 | tf_op jit(solution)/shard_map/all_to_all | solution.py:553
  165.7 2.2 %copy-start.3 = (f32[16,3,72,128]{3,2,1,0:T(8,128)S(1)}, f32[16,3,72,128]{3,2,1,0:T(8,128)}, u32[]{:S(2)}) copy-start(f32[16,3,72,128]{3,2,1,0:T(8,128)} %copy-done.2) | copy-start | bytes 5308420
  165.8 13.9 %collective-permute-start.29 = (f32[8,2,64,128]{3,2,1,0:T(8,128)S(1)}, f32[8,2,64,128]{3,2,1,0:T(8,128)S(1)}, u32[]{:S(2)}, u32[]{:S(2)}) collective-permute-start(f32[8,2,64,128]{3,2,1,0:T(8,128)S(1)} %hand_back.1), channel_id=1, source_target_pairs={{0,64},{1,65},{2,66},{3,67},{4,68},{5,69},{6,70},{7,71},{8,72},{9,... | collective-permute-start | bytes 1572872 | tf_op jit(solution)/shard_map/ppermute | solution.py:70
  168.0 12.9 %copy-start.28 = (f32[96,128]{1,0:T(8,128)S(1)}, f32[96,128]{1,0:T(8,128)}, u32[]{:S(2)}) copy-start(f32[96,128]{1,0:T(8,128)} %copy-done.27) | copy-start | bytes 147460
  168.0 12.9 %copy-start.30 = (f32[96,128]{1,0:T(8,128)S(1)}, f32[96,128]{1,0:T(8,128)}, u32[]{:S(2)}) copy-start(f32[96,128]{1,0:T(8,128)} %copy-done.29) | copy-start | bytes 147460
  (4 other events, 2.6 us)

commit v3 on v2

--- a/solution.py
+++ b/solution.py
@@ -180,7 +180,7 @@
     return call("edges", edges_body, [(DEPTH, 4, 8, NY)], [vmem()])(wide)[0]
 
 
-def rims_body(wide_ref, edge_ref, own_ref, other_ref, core_ref, chip_ref, corex_ref, chipx_ref):
+def rims_body(wide_ref, edge_ref, own_ref, other_ref, core_ref, chip_ref):
     core, half = core_index(), half_index()
     for z in range(DEPTH):
         for slot, ref in enumerate((own_ref, other_ref)):
@@ -193,16 +193,15 @@
     to_core = (1 - core) * (DEPTH - HALO)
     to_chip = core * (DEPTH - HALO)
     for i in range(HALO):
-        for part in range(2):
-            core_ref[2 * i + part] = own_ref[to_core + i, part]
-            chip_ref[2 * i + part] = own_ref[to_chip + i, part]
-            corex_ref[2 * i + part] = other_ref[to_core + i, part]
-            chipx_ref[2 * i + part] = other_ref[to_chip + i, part]
+        for slot, ref in enumerate((own_ref, other_ref)):
+            for part in range(2):
+                core_ref[2 * (HALO * slot + i) + part] = ref[to_core + i, part]
+                chip_ref[2 * (HALO * slot + i) + part] = ref[to_chip + i, part]
 
 
 def rims(wide, edge):
     return call(
-        "rims", rims_body, [(DEPTH, 2, LOCAL, NY)] * 2 + [(2 * HALO, LOCAL, NY)] * 4, [vmem()] * 2, limit=12
+        "rims", rims_body, [(DEPTH, 2, LOCAL, NY)] * 2 + [(4 * HALO, LOCAL, NY)] * 2, [vmem()] * 2, limit=12
     )(wide, edge)
 
 
@@ -253,28 +252,75 @@
     )(got.reshape(GROUP // 2, 2, PACK, NY))
 
 
+def clear(ref, count):
+    zeros = jnp.zeros((PAD, NY), F32)
+
+    @pl.loop(0, count)
+    def _(j):
+        for k in range(4):
+            ref[j, k, 0:PAD, :] = zeros
+            ref[j, k, PAD + LOCAL : XL, :] = zeros
+
+
+def stage_body(
+    first, own_ref, other_ref, hcore_ref, hchip_ref, hcorex_ref, hchipx_ref, weight_ref, vcore_ref, vchip_ref,
+    base_ref, v_ref,
+):
+    core = core_index()
+    clear(base_ref, WIDE)
+
+    @pl.loop(0, DEPTH)
+    def _(z):
+        for part in range(2):
+            base_ref[z + HALO, part, PAD : PAD + LOCAL, :] = own_ref[z, part]
+            base_ref[z + HALO, 2 + part, PAD : PAD + LOCAL, :] = other_ref[z, part]
+        v_ref[z + MARGIN] = weight_ref[z]
+
+    def put_halo(above, orb_ref, orbx_ref, pot_ref):
+        @pl.loop(0, HALO)
+        def _(i):
+            j = above * (DEPTH + HALO) + i
+            for part in range(2):
+                base_ref[j, part, PAD : PAD + LOCAL, :] = orb_ref[2 * i + part]
+                base_ref[j, 2 + part, PAD : PAD + LOCAL, :] = orbx_ref[first + 2 * i + part]
+
+        @pl.loop(0, MARGIN)
+        def _(i):
+            v_ref[above * (DEPTH + MARGIN) + i] = pot_ref[2 * HALO + i]
+
+    @pl.when(core == 1)
+    def _():
+        put_halo(0, hcore_ref, hcorex_ref, vcore_ref)
+        put_halo(1, hchip_ref, hchipx_ref, vchip_ref)
+
+    @pl.when(core == 0)
+    def _():
+        put_halo(1, hcore_ref, hcorex_ref, vcore_ref)
+        put_halo(0, hchip_ref, hchipx_ref, vchip_ref)
+
+
+def stage(first, orbs, weight, vcore, vchip):
+    return call(
+        "stage",
+        functools.partial(stage_body, first),
+        [(WIDE, 4, XL, NY), (DEPTH + 2 * MARGIN, LOCAL, NY)],
+        [vmem()] * 9,
+        flops=1000000,
+        limit=16,
+    )(*orbs, weight, vcore, vchip)
+
+
 def propagate_body(
-    own_ref, other_ref, hcore_ref, hchip_ref, hcorex_ref, hchipx_ref, weight_ref, vcore_ref, vchip_ref,
-    field_ref, edge_ref, acore_ref, achip_ref, acorex_ref, achipx_ref,
-    out_ref, norm_ref, a_ref, base_ref, ping_ref, pong_ref, w_ref,
+    occ_ref, base_ref, v_ref, field_ref, edge_ref, acore_ref, achip_ref, acorex_ref, achipx_ref,
+    out_ref, norm_ref, a_ref, ping_ref, pong_ref, w_ref,
 ):
     core, half = core_index(), half_index()
-    zeros = jnp.zeros((PAD, NY), F32)
-
-    def clear(ref, count):
-        @pl.loop(0, count)
-        def _(j):
-            for k in range(4):
-                ref[j, k, 0:PAD, :] = zeros
-                ref[j, k, PAD + LOCAL : XL, :] = zeros
-
-    clear(base_ref, WIDE)
     clear(ping_ref, WIDE)
     clear(pong_ref, WIDE)
     clear(out_ref, DEPTH + 2)
 
-    def put_field(j, fld_ref, edg_ref, i, base):
-        total = base
+    def put_field(j, fld_ref, edg_ref, i):
+        total = v_ref[j]
         for comp in range(3):
             value, edge = fld_ref[i, comp], edg_ref[i, comp]
             joined = jnp.where(
@@ -286,32 +332,22 @@
 
     @pl.loop(0, DEPTH)
     def _(z):
-        for part in range(2):
-            base_ref[z + HALO, part, PAD : PAD + LOCAL, :] = own_ref[z, part]
-            base_ref[z + HALO, 2 + part, PAD : PAD + LOCAL, :] = other_ref[z, part]
-        put_field(z + MARGIN, field_ref, edge_ref, z, weight_ref[z])
-
-    def put_halo(above, orb_ref, orbx_ref, pot_ref, fld_ref, edg_ref):
-        @pl.loop(0, HALO)
-        def _(i):
-            j = above * (DEPTH + HALO) + i
-            for part in range(2):
-                base_ref[j, part, PAD : PAD + LOCAL, :] = orb_ref[2 * i + part]
-                base_ref[j, 2 + part, PAD : PAD + LOCAL, :] = orbx_ref[2 * i + part]
-
+        put_field(z + MARGIN, field_ref, edge_ref, z)
+
+    def put_halo(above, fld_ref, edg_ref):
         @pl.loop(0, MARGIN)
         def _(i):
-            put_field(above * (DEPTH + MARGIN) + i, fld_ref, edg_ref, i, pot_ref[2 * HALO + i])
+            put_field(above * (DEPTH + MARGIN) + i, fld_ref, edg_ref, i)
 
     @pl.when(core == 1)
     def _():
-        put_halo(0, hcore_ref, hcorex_ref, vcore_ref, acore_ref, acorex_ref)
-        put_halo(1, hchip_ref, hchipx_ref, vchip_ref, achip_ref, achipx_ref)
+        put_halo(0, acore_ref, acorex_ref)
+        put_halo(1, achip_ref, achipx_ref)
 
     @pl.when(core == 0)
     def _():
-        put_halo(1, hcore_ref, hcorex_ref, vcore_ref, acore_ref, acorex_ref)
-        put_halo(0, hchip_ref, hchipx_ref, vchip_ref, achip_ref, achipx_ref)
+        put_halo(1, acore_ref, acorex_ref)
+        put_halo(0, achip_ref, achipx_ref)
 
     first = lax.axis_index("slab") * DEPTH - HALO
     sums = [jnp.zeros((8, NY), F32), jnp.zeros((8, NY), F32)]
@@ -357,23 +393,23 @@
         source = target
     norm_ref[0] = sums[0]
     norm_ref[1] = sums[1]
-
-
-def propagate(orbs, weight, vcore, vchip, fields):
+    norm_ref[2] = jnp.broadcast_to(occ_ref[0], (8, NY))
+
+
+def propagate(occupation, base, v, fields):
     return call(
         "propagate",
         propagate_body,
-        [(DEPTH + 2, 4, XL, NY), (2, 8, NY), (DEPTH + 2 * MARGIN, 3, LOCAL, NY)],
-        [vmem()] * 15,
+        [(DEPTH + 2, 4, XL, NY), (3, 8, NY), (DEPTH + 2 * MARGIN, 3, LOCAL, NY)],
+        [smem()] + [vmem()] * 8,
         [
-            pltpu.VMEM((WIDE, 4, XL, NY), F32),
             pltpu.VMEM((WIDE, 4, XL, NY), F32),
             pltpu.VMEM((WIDE, 4, XL, NY), F32),
             pltpu.VMEM((DEPTH + 2 * MARGIN, LOCAL, NY), F32),
         ],
         flops=60000000,
-        limit=32,
-    )(*orbs, weight, vcore, vchip, *fields)
+        limit=26,
+    )(occupation, base, v, *fields)
 
 
 def current_body(wide_ref, field_ref, flow_ref):
@@ -422,17 +458,17 @@
     )[0]
 
 
-def weigh_body(occ_ref, occx_ref, prior_ref, n_ref, nchip_ref, nhalf_ref, nboth_ref, flow_ref, out_ref, scale_ref):
+def weigh_body(prior_ref, n_ref, nchip_ref, nhalf_ref, nboth_ref, flow_ref, out_ref, scale_ref):
     half = half_index()
     weights = []
-    for slot, occ in enumerate((occ_ref, occx_ref)):
+    for slot, occ_ref in enumerate((n_ref, nhalf_ref)):
         sums = (n_ref[slot] + nchip_ref[slot]) + (nhalf_ref[1 - slot] + nboth_ref[1 - slot])
         norm = jnp.sum(jnp.sum(sums, axis=1, keepdims=True), axis=0, keepdims=True)
         prior = prior_ref[slot, 0:1, :]
         mean = prior * prior * (norm * (1.0 / CELLS)) + EPSILON
         scale = prior / jnp.sqrt(mean)
         scale_ref[slot] = jnp.broadcast_to(scale, (8, NY))
-        weights.append(scale * scale * (occ[0] * (1.0 / ORBS)))
+        weights.append(scale * scale * (occ_ref[2, 0:1, :] * (0.5 / ORBS)))
 
     @pl.loop(0, GROUP // 2)
     def _(i):
@@ -440,10 +476,10 @@
             out_ref[i, side] = flow_ref[0, i + half, side] * weights[0] + flow_ref[1, i + half, side] * weights[1]
 
 
-def weigh(occupations, prior, norms, flow):
+def weigh(prior, norms, flow):
     return call(
-        "weigh", weigh_body, [(GROUP // 2, 2, PACK, NY), (2, 8, NY)], [smem()] * 2 + [vmem()] * 6, flops=500000
-    )(*occupations, prior, *norms, flow)
+        "weigh", weigh_body, [(GROUP // 2, 2, PACK, NY), (2, 8, NY)], [vmem()] * 6, flops=500000
+    )(prior, *norms, flow)
 
 
 def curl_body(field_ref, out_ref):
@@ -554,13 +590,13 @@
 
 
 def per_device(orbitals, potential, occupation, e_field, a_field):
-    copies, a_rows = spread(a_field)
-    got = everyone(copies)
     own, swap, weight, core, chip, corex, chipx, e_rows = prepare(orbitals, potential, e_field)
     other = send(swap, HALVES)
     vcore, vchip = send(core, CORE), send(chip, CHIP)
     orbs = (own, other, vcore, vchip, send(corex, CORE_ACROSS), send(chipx, CHIP_ACROSS))
-    occupations = (occupation, send(occupation, HALVES))
+    a_field, swap = lax.optimization_barrier((a_field, swap))
+    copies, a_rows = spread(a_field)
+    got = everyone(copies)
     scale = jnp.ones((2, 8, NY), F32)
     for step in range(STEPS):
         last = step == STEPS - 1
@@ -573,30 +609,30 @@
             send(acorex, CORE_ACROSS),
             send(achipx, CHIP_ACROSS),
         )
-        wide, norm, field = propagate(orbs, weight, vcore, vchip, fields)
+        base, v = stage(2 * HALO * step, orbs, weight, vcore, vchip)
+        wide, norm, field = propagate(occupation, base, v, fields)
         norm = norm + send(norm, CORE)
         norms = (norm, send(norm, CHIP_SUM), send(norm, HALVES), send(norm, BOTH_SUM))
         flow = current(wide, field)
-        flow, scale = weigh(occupations, scale, norms, flow)
+        if last:
+            theirs = hand_back(wide)
+            flow, theirs = lax.optimization_barrier((flow, theirs))
+            theirs = send(theirs, HALVES)
+        else:
+            edge = send(edges(wide), HALVES)
+            flow, edge = lax.optimization_barrier((flow, edge))
+        flow, scale = weigh(scale, norms, flow)
         flows = everyone(flow.reshape(GROUP, PACK, NY))
         curl = double_curl(field)
         if not last:
-            edge = send(edges(wide), HALVES)
-            own, other, core, chip, corex, chipx = rims(wide, edge)
-            flows, core, chip, corex, chipx = lax.optimization_barrier((flows, core, chip, corex, chipx))
-            orbs = (
-                own,
-                other,
-                send(core, CORE),
-                send(chip, CHIP),
-                send(corex, CORE),
-                send(chipx, CHIP),
-            )
+            own, other, core, chip = rims(wide, edge)
+            flows, core, chip = lax.optimization_barrier((flows, core, chip))
+            core, chip = send(core, CORE), send(chip, CHIP)
             copies, a_rows, e_rows = update(last, flows, curl, e_rows, a_rows)
             got = everyone(copies)
-            got, orbs = lax.optimization_barrier((got, orbs))
+            got, core, chip = lax.optimization_barrier((got, core, chip))
+            orbs = (own, other, core, chip, core, chip)
         else:
-            theirs = send(hand_back(wide), HALVES)
             e_new, a_new = update(last, flows, curl, e_rows, a_rows)
             orbitals = finish(scale, wide, theirs)
     return (

time: 183 us -> 171 us (0.934)
  starting transfers between devices: 84.4 us -> 75.6 us
  local copies, waits for them, and re-layouts: 21.5 us -> 15.4 us
  waiting for transfers between devices: 49.3 us -> 52.8 us
    all_to_all x4, waiting for transfers between devices: 9.5 us -> 24.7 us  [everyone(): lax.all_to_all(copies, 'orb', 0, 0, tiled=True, axis_index_groups=GROUPS)]
    ppermute x30 -> x27, waiting for transfers between devices: 39.8 us -> 28 us  [send(): return lax.ppermute(value, ALL, table)]
    ppermute x30 -> x27, starting transfers between devices: 58.3 us -> 51 us  [send(): return lax.ppermute(value, ALL, table)]
    unnamed x68 -> x40, local copies, waits for them, and re-layouts: 21.5 us -> 15.4 us
    pallas_call x5 -> x7, Pallas kernels: 15 us -> 16.3 us  [the longest x2 11.6 us: propagate(): call('propagate', propagate_body, [(DEPTH + 2, 4, XL, NY), (3, 8, NY), (D...]
  transfers between devices with their start and end apart: 34 -> 31, of which waited for: 13 -> 12; matrix products, arithmetic and copies ran while one was open for 0% -> 0% of each run, Pallas kernels for 4% -> 4%
where the time goes in v3:
time: 171 us; the launch traced here: 170 us
  starting transfers between devices  75.6 us (44%)
  waiting for transfers between devices  52.8 us (31%)
  Pallas kernels  24.5 us (14%)
  local copies, waits for them, and re-layouts  15.4 us (9%)
    ppermute x27, starting transfers between devices, send(): return lax.ppermute(value, ALL, table)  51 us
    ppermute x27, waiting for transfers between devices, send(): return lax.ppermute(value, ALL, table)  28 us
    all_to_all x4, waiting for transfers between devices, everyone(): lax.all_to_all(copies, 'orb', 0, 0, tiled=True, axis_index_groups=GROUPS)  24.7 us
    all_to_all x4, starting transfers between devices, everyone(): lax.all_to_all(copies, 'orb', 0, 0, tiled=True, axis_index_groups=GROUPS)  24.6 us
    unnamed x40, local copies, waits for them, and re-layouts  15.4 us
    pallas_call x2, Pallas kernels, propagate(): call('propagate', propagate_body, [(DEPTH + 2, 4, XL, NY), (3, 8, NY), (D...  11.6 us
  transfers between devices with their start and end apart: 31, of which 12 were waited for; matrix products, arithmetic and copies ran while one was open for 0% of the time, Pallas kernels for 4%

profile of v3, /device:TPU:0, one launch (start us, length us, event | category | flops | bytes accessed | tf_op | source)
XLA Modules:
  0.0 169.9 jit_solution(4401075476180815368)
XLA Ops:
  0.6 1.2 copy-done.4
  1.9 1.0 copy-done.11
  2.9 0.8 copy-done.13
  3.7 1.4 prepare.1
  5.1 0.8 copy-done.17
  5.9 0.8 copy-done.18
  6.7 0.8 copy-done.19
  7.5 0.8 copy-done.14
  8.3 1.0 spread.1
  9.2 7.1 %all-to-all-start = ((f32[16,96,128]{2,1,0:T(8,128)}), f32[16,96,128]{2,1,0:T(8,128)S(1)}, u32[]{:S(2)}, u32[]{:S(2)}) async-start(f32[16,96,128]{2,1,0:T(8,128)} %get-tuple-element.69), calls=%async_computation | async-start | bytes 1572864 | tf_op jit(solution)/shard_map/all_to_all | solution.py:589
  16.4 3.1 %collective-permute-start.3 = (f32[10,72,128]{2,1,0:T(8,128)}, f32[10,72,128]{2,1,0:T(8,128)}, u32[]{:S(2)}, u32[]{:S(2)}) collective-permute-start(f32[10,72,128]{2,1,0:T(8,128)} %get-tuple-element.63), channel_id=1, source_target_pairs={{0,65},{1,64},{2,67},{3,66},{4,69},{5,68},{6,71},{7,70},{8,73},{9,... | collective-permute-start | bytes 1105928 | tf_op jit(solution)/shard_map/ppermute | solution.py:70
  19.5 1.4 collective-permute-start.4
  20.9 0.9 collective-permute-start
  21.8 2.6 %collective-permute-start.1 = (f32[14,72,128]{2,1,0:T(8,128)}, f32[14,72,128]{2,1,0:T(8,128)S(1)}, u32[]{:S(2)}, u32[]{:S(2)}) collective-permute-start(f32[14,72,128]{2,1,0:T(8,128)} %copy-done.19), channel_id=1, source_target_pairs={{0,1},{1,0},{2,3},{3,2},{4,5},{5,4},{6,7},{7,6},{8,9},{9,8},{10,11... | collective-permute-start | bytes 1548296 | tf_op jit(solution)/shard_map/ppermute | solution.py:70
  24.4 0.7 collective-permute-start.2
  25.1 5.6 %all-to-all-done = f32[16,96,128]{2,1,0:T(8,128)S(1)} async-done(((f32[16,96,128]{2,1,0:T(8,128)}), f32[16,96,128]{2,1,0:T(8,128)S(1)}, u32[]{:S(2)}, u32[]{:S(2)}) %all-to-all-start) | async-done | bytes 786464 | tf_op jit(solution)/shard_map/all_to_all | solution.py:589
  31.0 0.7 collective-permute-start.7
  31.7 4.0 %collective-permute-start.5 = (f32[8,3,8,128]{3,2,1,0:T(8,128)S(1)}, f32[8,3,8,128]{3,2,1,0:T(8,128)S(1)}, u32[]{:S(2)}, u32[]{:S(2)}) collective-permute-start(f32[8,3,8,128]{3,2,1,0:T(8,128)S(1)} %get-tuple-element.71), channel_id=1, source_target_pairs={{0,64},{1,65},{2,66},{3,67},{4,68},{5,69},{6,70},{7,71},{8,72},{9,... | collective-permute-start | bytes 294920 | tf_op jit(solution)/shard_map/ppermute | solution.py:70
  35.7 18.2 %collective-permute-start.8 = (f32[4,3,8,128]{3,2,1,0:T(8,128)S(1)}, f32[4,3,8,128]{3,2,1,0:T(8,128)S(1)}, u32[]{:S(2)}, u32[]{:S(2)}) collective-permute-start(f32[4,3,8,128]{3,2,1,0:T(8,128)S(1)} %get-tuple-element.74), channel_id=1, source_target_pairs={{0,65},{1,64},{2,67},{3,66},{4,69},{5,68},{6,71},{7,70},{8,73},{9,... | collective-permute-start | bytes 147464 | tf_op jit(solution)/shard_map/ppermute | solution.py:70
  53.9 0.7 collective-permute-start.9
  55.2 1.5 stage.2
  56.7 4.7 %collective-permute-done.8.acorex_ref = f32[4,3,8,128]{3,2,1,0:T(8,128)S(1)} collective-permute-done((f32[4,3,8,128]{3,2,1,0:T(8,128)S(1)}, f32[4,3,8,128]{3,2,1,0:T(8,128)S(1)}, u32[]{:S(2)}, u32[]{:S(2)}) %collective-permute-start.8) | collective-permute-done | bytes 49184 | tf_op jit(solution)/shard_map/ppermute | solution.py:70
  61.3 5.8 %propagate.2 = (f32[10,4,88,128]{3,2,1,0:T(8,128)S(1)}, f32[3,8,128]{2,1,0:T(8,128)S(1)}, f32[16,3,72,128]{3,2,1,0:T(8,128)S(1)}) custom-call(f32[1]{0:T(128)S(6)} %copy.8.occ_ref, f32[18,4,88,128]{3,2,1,0:T(8,128)S(1)} %get-tuple-element.66.base_ref, f32[16,72,128]{2,1,0:T(8,128)S(1)} %get-tuple-element.67.v_ref, ...), custom_call_target="tpu_custom_call" | custom-call | flops 60000000 | bytes 7168000 | tf_op jit(solution)/shard_map/propagate/pallas_call | solution.py:400
  67.6 1.1 collective-permute-done.10
  68.7 1.0 collective-permute-start.11
  69.7 2.3 %collective-permute-start.12 = (f32[3,8,128]{2,1,0:T(8,128)S(1)}, f32[3,8,128]{2,1,0:T(8,128)S(1)}, u32[]{:S(2)}, u32[]{:S(2)}) collective-permute-start(f32[3,8,128]{2,1,0:T(8,128)S(1)} %add.6.n_ref), channel_id=1, source_target_pairs={{0,64},{1,65},{2,66},{3,67},{4,68},{5,69},{6,70},{7,71},{8,72},{9,... | collective-permute-start | bytes 36872 | tf_op jit(solution)/shard_map/ppermute | solution.py:70
  72.0 1.4 collective-permute-start.13
  73.4 1.0 current.2.flow_ref
  74.3 0.3 collective-permute-done.14.edge_ref
  74.9 2.0 %collective-permute-done.13.nboth_ref = f32[3,8,128]{2,1,0:T(8,128)S(1)} collective-permute-done((f32[3,8,128]{2,1,0:T(8,128)S(1)}, f32[3,8,128]{2,1,0:T(8,128)S(1)}, u32[]{:S(2)}, u32[]{:S(2)}) %collective-permute-start.13) | collective-permute-done | bytes 12320 | tf_op jit(solution)/shard_map/ppermute | solution.py:70
  77.1 0.9 copy-done.5
  78.0 6.9 %all-to-all-start.1 = ((f32[16,96,128]{2,1,0:T(8,128)}), f32[16,96,128]{2,1,0:T(8,128)}, u32[]{:S(2)}, u32[]{:S(2)}) async-start(f32[16,96,128]{2,1,0:T(8,128)} %bitcast.14), calls=%async_computation.1 | async-start | bytes 1572864 | tf_op jit(solution)/shard_map/all_to_all | solution.py:589
  84.9 1.5 copy-done.1
  86.7 0.8 copy-done.7
  87.6 0.8 copy-done.9
  88.4 0.9 copy-done.15
  89.3 0.9 copy-done.16
  90.1 8.1 %all-to-all-done.1.got_ref = f32[16,96,128]{2,1,0:T(8,128)} async-done(((f32[16,96,128]{2,1,0:T(8,128)}), f32[16,96,128]{2,1,0:T(8,128)}, u32[]{:S(2)}, u32[]{:S(2)}) %all-to-all-start.1) | async-done | bytes 786464 | tf_op jit(solution)/shard_map/all_to_all | solution.py:589
  98.2 1.3 update.2
  99.5 0.9 copy-done.6
  100.4 3.6 %all-to-all-start.2 = ((f32[16,96,128]{2,1,0:T(8,128)}), f32[16,96,128]{2,1,0:T(8,128)S(1)}, u32[]{:S(2)}, u32[]{:S(2)}) async-start(f32[16,96,128]{2,1,0:T(8,128)} %copy-done.6), calls=%async_computation.2 | async-start | bytes 1572864 | tf_op jit(solution)/shard_map/all_to_all | solution.py:589
  104.3 1.5 collective-permute-start.16
  105.8 11.0 %all-to-all-done.2 = f32[16,96,128]{2,1,0:T(8,128)S(1)} async-done(((f32[16,96,128]{2,1,0:T(8,128)}), f32[16,96,128]{2,1,0:T(8,128)S(1)}, u32[]{:S(2)}, u32[]{:S(2)}) %all-to-all-start.2) | async-done | bytes 786464 | tf_op jit(solution)/shard_map/all_to_all | solution.py:589
  117.0 1.1 collective-permute-start.18
  118.1 0.7 collective-permute-start.19
  118.8 0.8 collective-permute-start.17
  119.6 3.4 %collective-permute-start.20 = (f32[4,3,8,128]{3,2,1,0:T(8,128)S(1)}, f32[4,3,8,128]{3,2,1,0:T(8,128)S(1)}, u32[]{:S(2)}, u32[]{:S(2)}) collective-permute-start(f32[4,3,8,128]{3,2,1,0:T(8,128)S(1)} %get-tuple-element.102), channel_id=1, source_target_pairs={{0,65},{1,64},{2,67},{3,66},{4,69},{5,68},{6,71},{7,70},{8,73},{9,... | collective-permute-start | bytes 147464 | tf_op jit(solution)/shard_map/ppermute | solution.py:70
  123.0 0.7 collective-permute-start.21
  123.6 1.1 copy-done.10
  124.7 1.7 %stage.3 = (f32[18,4,88,128]{3,2,1,0:T(8,128)S(1)}, f32[16,72,128]{2,1,0:T(8,128)S(1)}) custom-call(f32[8,2,72,128]{3,2,1,0:T(8,128)S(1)} %copy-done.8, f32[8,2,72,128]{3,2,1,0:T(8,128)S(1)} %copy-done.10, f32[20,72,128]{2,1,0:T(8,128)S(1)} %collective-permute-done.15.hcore_ref.hcorex_ref, f32[20,72,128]{2,1,0:T(8,128)} %collective-permute-done.16.hchip_ref.hchipx_ref, ...), custom_call_target="tpu_custom_call" | custom-call | flops 1000000 | bytes 7667712 | tf_op jit(solution)/shard_map/stage/pallas_call | solution.py:303
  126.4 4.4 %collective-permute-done.20.acorex_ref = f32[4,3,8,128]{3,2,1,0:T(8,128)S(1)} collective-permute-done((f32[4,3,8,128]{3,2,1,0:T(8,128)S(1)}, f32[4,3,8,128]{3,2,1,0:T(8,128)S(1)}, u32[]{:S(2)}, u32[]{:S(2)}) %collective-permute-start.20) | collective-permute-done | bytes 49184 | tf_op jit(solution)/shard_map/ppermute | solution.py:70
  130.8 5.8 %propagate.3 = (f32[10,4,88,128]{3,2,1,0:T(8,128)S(1)}, f32[3,8,128]{2,1,0:T(8,128)S(1)}, f32[16,3,72,128]{3,2,1,0:T(8,128)S(1)}) custom-call(f32[1]{0:T(128)S(6)} %copy.8.occ_ref, f32[18,4,88,128]{3,2,1,0:T(8,128)S(1)} %get-tuple-element.95.base_ref, f32[16,72,128]{2,1,0:T(8,128)S(1)} %get-tuple-element.96.v_ref, ...), custom_call_target="tpu_custom_call" | custom-call | flops 60000000 | bytes 7168000 | tf_op jit(solution)/shard_map/propagate/pallas_call | solution.py:400
  136.8 1.1 collective-permute-done.22
  137.9 3.2 %collective-permute-start.24 = (f32[3,8,128]{2,1,0:T(8,128)S(1)}, f32[3,8,128]{2,1,0:T(8,128)S(1)}, u32[]{:S(2)}, u32[]{:S(2)}) collective-permute-start(f32[3,8,128]{2,1,0:T(8,128)S(1)} %add.7.n_ref), channel_id=1, source_target_pairs={{0,64},{1,65},{2,66},{3,67},{4,68},{5,69},{6,70},{7,71},{8,72},{9,... | collective-permute-start | bytes 36872 | tf_op jit(solution)/shard_map/ppermute | solution.py:70
  141.2 1.4 collective-permute-start.25
  142.7 1.0 current.3.flow_ref
  143.7 2.4 %collective-permute-done.25.nboth_ref = f32[3,8,128]{2,1,0:T(8,128)S(1)} collective-permute-done((f32[3,8,128]{2,1,0:T(8,128)S(1)}, f32[3,8,128]{2,1,0:T(8,128)S(1)}, u32[]{:S(2)}, u32[]{:S(2)}) %collective-permute-start.25) | collective-permute-done | bytes 12320 | tf_op jit(solution)/shard_map/ppermute | solution.py:70
  146.1 1.1 weigh.3
  147.2 6.9 %all-to-all-start.3 = ((f32[16,96,128]{2,1,0:T(8,128)}), f32[16,96,128]{2,1,0:T(8,128)S(1)}, u32[]{:S(2)}, u32[]{:S(2)}) async-start(f32[16,96,128]{2,1,0:T(8,128)} %bitcast.8), calls=%async_computation.3 | async-start | bytes 1572864 | tf_op jit(solution)/shard_map/all_to_all | solution.py:589
  154.1 0.4 collective-permute-start.26
  154.5 1.5 copy-done.3
  156.1 11.8 %collective-permute-done.26.theirs_ref = f32[8,2,64,128]{3,2,1,0:T(8,128)S(1)} collective-permute-done((f32[8,2,64,128]{3,2,1,0:T(8,128)}, f32[8,2,64,128]{3,2,1,0:T(8,128)S(1)}, u32[]{:S(2)}, u32[]{:S(2)}) %collective-permute-start.26) | collective-permute-done | bytes 524320 | tf_op jit(solution)/shard_map/ppermute | solution.py:70
  167.9 1.3 finish.1
  169.2 0.7 update.3
  (61 shorter events, 2.3 us)
Async XLA Ops:
  0.6 1.2 copy-start.4
  1.9 1.0 copy-start.11
  2.9 0.8 copy-start.13
  5.1 0.8 copy-start.17
  5.9 0.8 copy-start.18
  6.7 0.8 copy-start.19
  7.5 0.8 copy-start.14
  9.2 21.5 %all-to-all-start = ((f32[16,96,128]{2,1,0:T(8,128)}), f32[16,96,128]{2,1,0:T(8,128)S(1)}, u32[]{:S(2)}, u32[]{:S(2)}) async-start(f32[16,96,128]{2,1,0:T(8,128)} %get-tuple-element.69), calls=%async_computation | async-start | bytes 1572864 | tf_op jit(solution)/shard_map/all_to_all | solution.py:589
  16.4 14.5 %collective-permute-start.3 = (f32[10,72,128]{2,1,0:T(8,128)}, f32[10,72,128]{2,1,0:T(8,128)}, u32[]{:S(2)}, u32[]{:S(2)}) collective-permute-start(f32[10,72,128]{2,1,0:T(8,128)} %get-tuple-element.63), channel_id=1, source_target_pairs={{0,65},{1,64},{2,67},{3,66},{4,69},{5,68},{6,71},{7,70},{8,73},{9,... | collective-permute-start | bytes 1105928 | tf_op jit(solution)/shard_map/ppermute | solution.py:70
  19.5 11.5 %collective-permute-start.4 = (f32[10,72,128]{2,1,0:T(8,128)}, f32[10,72,128]{2,1,0:T(8,128)}, u32[]{:S(2)}, u32[]{:S(2)}) collective-permute-start(f32[10,72,128]{2,1,0:T(8,128)} %get-tuple-element.64), channel_id=1, source_target_pairs={{1,66},{2,65},{5,70},{6,69},{9,74},{10,73},{13,78},{14,77},{17,82}... | collective-permute-start | bytes 1105928 | tf_op jit(solution)/shard_map/ppermute | solution.py:70
  20.9 33.0 %collective-permute-start = (f32[8,2,72,128]{3,2,1,0:T(8,128)}, f32[8,2,72,128]{3,2,1,0:T(8,128)S(1)}, u32[]{:S(2)}, u32[]{:S(2)}) collective-permute-start(f32[8,2,72,128]{3,2,1,0:T(8,128)} %copy-done.17), channel_id=1, source_target_pairs={{0,64},{1,65},{2,66},{3,67},{4,68},{5,69},{6,70},{7,71},{8,72},{9,... | collective-permute-start | bytes 1769480 | tf_op jit(solution)/shard_map/ppermute | solution.py:70
  21.8 9.9 %collective-permute-start.1 = (f32[14,72,128]{2,1,0:T(8,128)}, f32[14,72,128]{2,1,0:T(8,128)S(1)}, u32[]{:S(2)}, u32[]{:S(2)}) collective-permute-start(f32[14,72,128]{2,1,0:T(8,128)} %copy-done.19), channel_id=1, source_target_pairs={{0,1},{1,0},{2,3},{3,2},{4,5},{5,4},{6,7},{7,6},{8,9},{9,8},{10,11... | collective-permute-start | bytes 1548296 | tf_op jit(solution)/shard_map/ppermute | solution.py:70
  24.4 11.3 %collective-permute-start.2 = (f32[14,72,128]{2,1,0:T(8,128)}, f32[14,72,128]{2,1,0:T(8,128)S(1)}, u32[]{:S(2)}, u32[]{:S(2)}) collective-permute-start(f32[14,72,128]{2,1,0:T(8,128)} %copy-done.18), channel_id=1, source_target_pairs={{1,2},{2,1},{5,6},{6,5},{9,10},{10,9},{13,14},{14,13},{17,18},{18,... | collective-permute-start | bytes 1548296 | tf_op jit(solution)/shard_map/ppermute | solution.py:70
  30.9 30.4 %collective-permute-start.6 = (f32[4,3,64,128]{3,2,1,0:T(8,128)S(1)}, f32[4,3,64,128]{3,2,1,0:T(8,128)S(1)}, u32[]{:S(2)}, u32[]{:S(2)}) collective-permute-start(f32[4,3,64,128]{3,2,1,0:T(8,128)S(1)} %get-tuple-element.72), channel_id=1, source_target_pairs={{0,1},{1,0},{2,3},{3,2},{4,5},{5,4},{6,7},{7,6},{8,9},{9,8},{10,11... | collective-permute-start | bytes 1179656 | tf_op jit(solution)/shard_map/ppermute | solution.py:70
  31.0 30.3 %collective-permute-start.7 = (f32[4,3,64,128]{3,2,1,0:T(8,128)S(1)}, f32[4,3,64,128]{3,2,1,0:T(8,128)S(1)}, u32[]{:S(2)}, u32[]{:S(2)}) collective-permute-start(f32[4,3,64,128]{3,2,1,0:T(8,128)S(1)} %get-tuple-element.73), channel_id=1, source_target_pairs={{1,2},{2,1},{5,6},{6,5},{9,10},{10,9},{13,14},{14,13},{17,18},{18,... | collective-permute-start | bytes 1179656 | tf_op jit(solution)/shard_map/ppermute | solution.py:70
  31.7 29.6 %collective-permute-start.5 = (f32[8,3,8,128]{3,2,1,0:T(8,128)S(1)}, f32[8,3,8,128]{3,2,1,0:T(8,128)S(1)}, u32[]{:S(2)}, u32[]{:S(2)}) collective-permute-start(f32[8,3,8,128]{3,2,1,0:T(8,128)S(1)} %get-tuple-element.71), channel_id=1, source_target_pairs={{0,64},{1,65},{2,66},{3,67},{4,68},{5,69},{6,70},{7,71},{8,72},{9,... | collective-permute-start | bytes 294920 | tf_op jit(solution)/shard_map/ppermute | solution.py:70
  35.7 25.6 %collective-permute-start.8 = (f32[4,3,8,128]{3,2,1,0:T(8,128)S(1)}, f32[4,3,8,128]{3,2,1,0:T(8,128)S(1)}, u32[]{:S(2)}, u32[]{:S(2)}) collective-permute-start(f32[4,3,8,128]{3,2,1,0:T(8,128)S(1)} %get-tuple-element.74), channel_id=1, source_target_pairs={{0,65},{1,64},{2,67},{3,66},{4,69},{5,68},{6,71},{7,70},{8,73},{9,... | collective-permute-start | bytes 147464 | tf_op jit(solution)/shard_map/ppermute | solution.py:70
  53.9 7.5 %collective-permute-start.9 = (f32[4,3,8,128]{3,2,1,0:T(8,128)S(1)}, f32[4,3,8,128]{3,2,1,0:T(8,128)S(1)}, u32[]{:S(2)}, u32[]{:S(2)}) collective-permute-start(f32[4,3,8,128]{3,2,1,0:T(8,128)S(1)} %get-tuple-element.75), channel_id=1, source_target_pairs={{1,66},{2,65},{5,70},{6,69},{9,74},{10,73},{13,78},{14,77},{17,82}... | collective-permute-start | bytes 147464 | tf_op jit(solution)/shard_map/ppermute | solution.py:70
  67.1 7.2 %copy-start = (f32[16,3,72,128]{3,2,1,0:T(8,128)}, f32[16,3,72,128]{3,2,1,0:T(8,128)S(1)}, u32[]{:S(2)}) copy-start(f32[16,3,72,128]{3,2,1,0:T(8,128)S(1)} %get-tuple-element.78.field_ref) | copy-start | bytes 5308420
  67.2 7.5 %collective-permute-start.14 = (f32[8,4,8,128]{3,2,1,0:T(8,128)S(1)}, f32[8,4,8,128]{3,2,1,0:T(8,128)S(1)}, u32[]{:S(2)}, u32[]{:S(2)}) collective-permute-start(f32[8,4,8,128]{3,2,1,0:T(8,128)S(1)} %edges.1), channel_id=1, source_target_pairs={{0,64},{1,65},{2,66},{3,67},{4,68},{5,69},{6,70},{7,71},{8,72},{9,... | collective-permute-start | bytes 393224 | tf_op jit(solution)/shard_map/ppermute | solution.py:70
  67.5 1.2 collective-permute-start.10
  68.7 6.0 %collective-permute-start.11 = (f32[3,8,128]{2,1,0:T(8,128)S(1)}, f32[3,8,128]{2,1,0:T(8,128)S(1)}, u32[]{:S(2)}, u32[]{:S(2)}) collective-permute-start(f32[3,8,128]{2,1,0:T(8,128)S(1)} %add.6.n_ref), channel_id=1, source_target_pairs={{0,2},{1,3},{2,0},{3,1},{4,6},{5,7},{6,4},{7,5},{8,10},{9,11},{10,... | collective-permute-start | bytes 36872 | tf_op jit(solution)/shard_map/ppermute | solution.py:70
  69.7 5.3 %collective-permute-start.12 = (f32[3,8,128]{2,1,0:T(8,128)S(1)}, f32[3,8,128]{2,1,0:T(8,128)S(1)}, u32[]{:S(2)}, u32[]{:S(2)}) collective-permute-start(f32[3,8,128]{2,1,0:T(8,128)S(1)} %add.6.n_ref), channel_id=1, source_target_pairs={{0,64},{1,65},{2,66},{3,67},{4,68},{5,69},{6,70},{7,71},{8,72},{9,... | collective-permute-start | bytes 36872 | tf_op jit(solution)/shard_map/ppermute | solution.py:70
  72.0 4.9 %collective-permute-start.13 = (f32[3,8,128]{2,1,0:T(8,128)S(1)}, f32[3,8,128]{2,1,0:T(8,128)S(1)}, u32[]{:S(2)}, u32[]{:S(2)}) collective-permute-start(f32[3,8,128]{2,1,0:T(8,128)S(1)} %add.6.n_ref), channel_id=1, source_target_pairs={{0,66},{1,67},{2,64},{3,65},{4,70},{5,71},{6,68},{7,69},{8,74},{9,... | collective-permute-start | bytes 36872 | tf_op jit(solution)/shard_map/ppermute | solution.py:70
  77.1 0.9 copy-start.5
  78.0 20.2 %all-to-all-start.1 = ((f32[16,96,128]{2,1,0:T(8,128)}), f32[16,96,128]{2,1,0:T(8,128)}, u32[]{:S(2)}, u32[]{:S(2)}) async-start(f32[16,96,128]{2,1,0:T(8,128)} %bitcast.14), calls=%async_computation.1 | async-start | bytes 1572864 | tf_op jit(solution)/shard_map/all_to_all | solution.py:589
  84.9 1.5 copy-start.1
  86.7 0.8 copy-start.7
  87.6 0.8 copy-start.9
  88.4 0.9 copy-start.15
  89.3 0.9 copy-start.16
  98.2 25.4 %copy-start.8 = (f32[8,2,72,128]{3,2,1,0:T(8,128)S(1)}, f32[8,2,72,128]{3,2,1,0:T(8,128)}, u32[]{:S(2)}) copy-start(f32[8,2,72,128]{3,2,1,0:T(8,128)} %copy-done.7) | copy-start | bytes 1769476
  99.5 0.9 copy-start.6
  100.4 16.4 %all-to-all-start.2 = ((f32[16,96,128]{2,1,0:T(8,128)}), f32[16,96,128]{2,1,0:T(8,128)S(1)}, u32[]{:S(2)}, u32[]{:S(2)}) async-start(f32[16,96,128]{2,1,0:T(8,128)} %copy-done.6), calls=%async_computation.2 | async-start | bytes 1572864 | tf_op jit(solution)/shard_map/all_to_all | solution.py:589
  104.0 12.8 %collective-permute-start.15 = (f32[20,72,128]{2,1,0:T(8,128)}, f32[20,72,128]{2,1,0:T(8,128)S(1)}, u32[]{:S(2)}, u32[]{:S(2)}) collective-permute-start(f32[20,72,128]{2,1,0:T(8,128)} %copy-done.16), channel_id=1, source_target_pairs={{0,1},{1,0},{2,3},{3,2},{4,5},{5,4},{6,7},{7,6},{8,9},{9,8},{10,11... | collective-permute-start | bytes 2211848 | tf_op jit(solution)/shard_map/ppermute | solution.py:70
  104.3 12.6 %collective-permute-start.16 = (f32[20,72,128]{2,1,0:T(8,128)}, f32[20,72,128]{2,1,0:T(8,128)}, u32[]{:S(2)}, u32[]{:S(2)}) collective-permute-start(f32[20,72,128]{2,1,0:T(8,128)} %copy-done.15), channel_id=1, source_target_pairs={{1,2},{2,1},{5,6},{6,5},{9,10},{10,9},{13,14},{14,13},{17,18},{18,... | collective-permute-start | bytes 2211848 | tf_op jit(solution)/shard_map/ppermute | solution.py:70
  117.0 13.8 %collective-permute-start.18 = (f32[4,3,64,128]{3,2,1,0:T(8,128)S(1)}, f32[4,3,64,128]{3,2,1,0:T(8,128)S(1)}, u32[]{:S(2)}, u32[]{:S(2)}) collective-permute-start(f32[4,3,64,128]{3,2,1,0:T(8,128)S(1)} %get-tuple-element.100), channel_id=1, source_target_pairs={{0,1},{1,0},{2,3},{3,2},{4,5},{5,4},{6,7},{7,6},{8,9},{9,8},{10,11... | collective-permute-start | bytes 1179656 | tf_op jit(solution)/shard_map/ppermute | solution.py:70
  118.1 12.7 %collective-permute-start.19 = (f32[4,3,64,128]{3,2,1,0:T(8,128)S(1)}, f32[4,3,64,128]{3,2,1,0:T(8,128)S(1)}, u32[]{:S(2)}, u32[]{:S(2)}) collective-permute-start(f32[4,3,64,128]{3,2,1,0:T(8,128)S(1)} %get-tuple-element.101), channel_id=1, source_target_pairs={{1,2},{2,1},{5,6},{6,5},{9,10},{10,9},{13,14},{14,13},{17,18},{18,... | collective-permute-start | bytes 1179656 | tf_op jit(solution)/shard_map/ppermute | solution.py:70
  118.8 12.0 %collective-permute-start.17 = (f32[8,3,8,128]{3,2,1,0:T(8,128)S(1)}, f32[8,3,8,128]{3,2,1,0:T(8,128)S(1)}, u32[]{:S(2)}, u32[]{:S(2)}) collective-permute-start(f32[8,3,8,128]{3,2,1,0:T(8,128)S(1)} %get-tuple-element.99), channel_id=1, source_target_pairs={{0,64},{1,65},{2,66},{3,67},{4,68},{5,69},{6,70},{7,71},{8,72},{9,... | collective-permute-start | bytes 294920 | tf_op jit(solution)/shard_map/ppermute | solution.py:70
  119.6 11.2 %collective-permute-start.20 = (f32[4,3,8,128]{3,2,1,0:T(8,128)S(1)}, f32[4,3,8,128]{3,2,1,0:T(8,128)S(1)}, u32[]{:S(2)}, u32[]{:S(2)}) collective-permute-start(f32[4,3,8,128]{3,2,1,0:T(8,128)S(1)} %get-tuple-element.102), channel_id=1, source_target_pairs={{0,65},{1,64},{2,67},{3,66},{4,69},{5,68},{6,71},{7,70},{8,73},{9,... | collective-permute-start | bytes 147464 | tf_op jit(solution)/shard_map/ppermute | solution.py:70
  123.0 7.8 %collective-permute-start.21 = (f32[4,3,8,128]{3,2,1,0:T(8,128)S(1)}, f32[4,3,8,128]{3,2,1,0:T(8,128)S(1)}, u32[]{:S(2)}, u32[]{:S(2)}) collective-permute-start(f32[4,3,8,128]{3,2,1,0:T(8,128)S(1)} %get-tuple-element.103), channel_id=1, source_target_pairs={{1,66},{2,65},{5,70},{6,69},{9,74},{10,73},{13,78},{14,77},{17,82}... | collective-permute-start | bytes 147464 | tf_op jit(solution)/shard_map/ppermute | solution.py:70
  123.6 1.1 copy-start.10
  136.6 7.0 %copy-start.2 = (f32[16,3,72,128]{3,2,1,0:T(8,128)}, f32[16,3,72,128]{3,2,1,0:T(8,128)S(1)}, u32[]{:S(2)}) copy-start(f32[16,3,72,128]{3,2,1,0:T(8,128)S(1)} %get-tuple-element.106.field_ref) | copy-start | bytes 5308420
  136.7 1.3 collective-permute-start.22
  137.9 5.7 %collective-permute-start.23 = (f32[3,8,128]{2,1,0:T(8,128)S(1)}, f32[3,8,128]{2,1,0:T(8,128)S(1)}, u32[]{:S(2)}, u32[]{:S(2)}) collective-permute-start(f32[3,8,128]{2,1,0:T(8,128)S(1)} %add.7.n_ref), channel_id=1, source_target_pairs={{0,2},{1,3},{2,0},{3,1},{4,6},{5,7},{6,4},{7,5},{8,10},{9,11},{10,... | collective-permute-start | bytes 36872 | tf_op jit(solution)/shard_map/ppermute | solution.py:70
  137.9 5.8 %collective-permute-start.24 = (f32[3,8,128]{2,1,0:T(8,128)S(1)}, f32[3,8,128]{2,1,0:T(8,128)S(1)}, u32[]{:S(2)}, u32[]{:S(2)}) collective-permute-start(f32[3,8,128]{2,1,0:T(8,128)S(1)} %add.7.n_ref), channel_id=1, source_target_pairs={{0,64},{1,65},{2,66},{3,67},{4,68},{5,69},{6,70},{7,71},{8,72},{9,... | collective-permute-start | bytes 36872 | tf_op jit(solution)/shard_map/ppermute | solution.py:70
  141.2 4.9 %collective-permute-start.25 = (f32[3,8,128]{2,1,0:T(8,128)S(1)}, f32[3,8,128]{2,1,0:T(8,128)S(1)}, u32[]{:S(2)}, u32[]{:S(2)}) collective-permute-start(f32[3,8,128]{2,1,0:T(8,128)S(1)} %add.7.n_ref), channel_id=1, source_target_pairs={{0,66},{1,67},{2,64},{3,65},{4,70},{5,71},{6,68},{7,69},{8,74},{9,... | collective-permute-start | bytes 36872 | tf_op jit(solution)/shard_map/ppermute | solution.py:70
  142.7 1.0 copy-start.12
  147.2 22.0 %all-to-all-start.3 = ((f32[16,96,128]{2,1,0:T(8,128)}), f32[16,96,128]{2,1,0:T(8,128)S(1)}, u32[]{:S(2)}, u32[]{:S(2)}) async-start(f32[16,96,128]{2,1,0:T(8,128)} %bitcast.8), calls=%async_computation.3 | async-start | bytes 1572864 | tf_op jit(solution)/shard_map/all_to_all | solution.py:589
  154.1 13.8 %collective-permute-start.26 = (f32[8,2,64,128]{3,2,1,0:T(8,128)}, f32[8,2,64,128]{3,2,1,0:T(8,128)S(1)}, u32[]{:S(2)}, u32[]{:S(2)}) collective-permute-start(f32[8,2,64,128]{3,2,1,0:T(8,128)} %copy-done.12), channel_id=1, source_target_pairs={{0,64},{1,65},{2,66},{3,67},{4,68},{5,69},{6,70},{7,71},{8,72},{9,... | collective-permute-start | bytes 1572872 | tf_op jit(solution)/shard_map/ppermute | solution.py:70
  154.5 1.5 copy-start.3

commit v4 on v3

--- a/solution.py
+++ b/solution.py
@@ -34,6 +34,7 @@
 XL = LOCAL + 2 * PAD
 GROUP = ORBS // 2
 TILES = LOCAL // 8
+EARLY = 3
 ALL = ("orb", "slab")
 MEETING = (1, 2)
 
@@ -59,7 +60,6 @@
 HALVES = pairs(GROUP, lambda slab: slab)
 CORE = pairs(0, over_core)
 CHIP = pairs(0, over_chip)
-CORE_ACROSS = pairs(GROUP, over_core)
 CHIP_ACROSS = pairs(GROUP, over_chip)
 CHIP_SUM = pairs(0, lambda slab: slab ^ 2)
 BOTH_SUM = pairs(GROUP, lambda slab: slab ^ 2)
@@ -128,7 +128,7 @@
 
 
 def prepare_body(
-    orb_ref, pot_ref, e_ref, own_ref, swap_ref, weight_ref, core_ref, chip_ref, corex_ref, chipx_ref, e_rows_ref
+    orb_ref, pot_ref, e_ref, own_ref, swap_ref, weight_ref, core_ref, chip_ref, chipx_ref, e_rows_ref
 ):
     core, half = core_index(), half_index()
     to_rows(e_ref, e_rows_ref)
@@ -142,7 +142,6 @@
         for part in range(2):
             core_ref[2 * i + part] = own_ref[to_core + i, part]
             chip_ref[2 * i + part] = own_ref[to_chip + i, part]
-            corex_ref[2 * i + part] = swap_ref[to_core + i, part]
             chipx_ref[2 * i + part] = swap_ref[to_chip + i, part]
     for i in range(MARGIN):
         core_ref[2 * HALO + i] = weight_ref[(1 - core) * (DEPTH - MARGIN) + i]
@@ -157,7 +156,7 @@
         [(DEPTH, 2, LOCAL, NY)] * 2
         + [(DEPTH, LOCAL, NY)]
         + [(planes, LOCAL, NY)] * 2
-        + [(2 * HALO, LOCAL, NY)] * 2
+        + [(2 * HALO, LOCAL, NY)]
         + [(PACK, NY)],
         [vmem()] * 3,
         limit=12,
@@ -168,6 +167,17 @@
     )
 
 
+def lend_body(other_ref, out_ref):
+    to_core = (1 - core_index()) * (DEPTH - HALO)
+    for i in range(HALO):
+        for part in range(2):
+            out_ref[2 * i + part] = other_ref[to_core + i, part]
+
+
+def lend(other):
+    return call("lend", lend_body, [(2 * HALO, LOCAL, NY)], [vmem()])(other)[0]
+
+
 def edges_body(wide_ref, out_ref):
     half = half_index()
     for z in range(DEPTH):
@@ -180,7 +190,7 @@
     return call("edges", edges_body, [(DEPTH, 4, 8, NY)], [vmem()])(wide)[0]
 
 
-def rims_body(wide_ref, edge_ref, own_ref, other_ref, core_ref, chip_ref):
+def rims_body(wide_ref, edge_ref, own_ref, other_ref, core_ref, chip_ref, chipx_ref):
     core, half = core_index(), half_index()
     for z in range(DEPTH):
         for slot, ref in enumerate((own_ref, other_ref)):
@@ -196,12 +206,12 @@
         for slot, ref in enumerate((own_ref, other_ref)):
             for part in range(2):
                 core_ref[2 * (HALO * slot + i) + part] = ref[to_core + i, part]
-                chip_ref[2 * (HALO * slot + i) + part] = ref[to_chip + i, part]
+                (chip_ref, chipx_ref)[slot][2 * i + part] = ref[to_chip + i, part]
 
 
 def rims(wide, edge):
     return call(
-        "rims", rims_body, [(DEPTH, 2, LOCAL, NY)] * 2 + [(4 * HALO, LOCAL, NY)] * 2, [vmem()] * 2, limit=12
+        "rims", rims_body, [(DEPTH, 2, LOCAL, NY)] * 2 + [(4 * HALO, LOCAL, NY)] + [(2 * HALO, LOCAL, NY)] * 2, [vmem()] * 2, limit=12
     )(wide, edge)
 
 
@@ -218,7 +228,7 @@
     )
 
 
-def assemble_body(got_ref, field_ref, edge_ref, core_ref, chip_ref, corex_ref, chipx_ref):
+def assemble_body(got_ref, field_ref, edge_ref, core_ref, chip_ref, chipx_ref):
     core, half = core_index(), half_index()
     low = half_rows((GROUP // 2, 8, NY))
     for comp in range(3):
@@ -237,7 +247,6 @@
         for comp in range(3):
             core_ref[i, comp] = field_ref[to_core, comp]
             chip_ref[i, comp] = field_ref[to_chip, comp]
-            corex_ref[i, comp] = edge_ref[to_core, comp]
             chipx_ref[i, comp] = edge_ref[to_chip, comp]
 
 
@@ -247,9 +256,24 @@
         assemble_body,
         [(DEPTH, 3, HALF, NY), (DEPTH, 3, 8, NY)]
         + [(MARGIN, 3, HALF, NY)] * 2
-        + [(MARGIN, 3, 8, NY)] * 2,
+        + [(MARGIN, 3, 8, NY)],
         [vmem()],
     )(got.reshape(GROUP // 2, 2, PACK, NY))
+
+
+def corners_body(edge_ref, core_ref, out_ref):
+    core, half = core_index(), half_index()
+    for comp in range(3):
+        for z in range(DEPTH):
+            out_ref[z + MARGIN * core, comp] = edge_ref[z, comp]
+        for i in range(MARGIN):
+            out_ref[(1 - core) * DEPTH + i, comp] = jnp.where(
+                half == 0, core_ref[i, comp, HALF - 8 : HALF, :], core_ref[i, comp, 0:8, :]
+            )
+
+
+def corners(edge, acore):
+    return call("corners", corners_body, [(DEPTH + MARGIN, 3, 8, NY)], [vmem()] * 2)(edge, acore)[0]
 
 
 def clear(ref, count):
@@ -276,13 +300,13 @@
             base_ref[z + HALO, 2 + part, PAD : PAD + LOCAL, :] = other_ref[z, part]
         v_ref[z + MARGIN] = weight_ref[z]
 
-    def put_halo(above, orb_ref, orbx_ref, pot_ref):
+    def put_halo(above, orb_ref, orbx_ref, offset, pot_ref):
         @pl.loop(0, HALO)
         def _(i):
             j = above * (DEPTH + HALO) + i
             for part in range(2):
                 base_ref[j, part, PAD : PAD + LOCAL, :] = orb_ref[2 * i + part]
-                base_ref[j, 2 + part, PAD : PAD + LOCAL, :] = orbx_ref[first + 2 * i + part]
+                base_ref[j, 2 + part, PAD : PAD + LOCAL, :] = orbx_ref[offset + 2 * i + part]
 
         @pl.loop(0, MARGIN)
         def _(i):
@@ -290,13 +314,13 @@
 
     @pl.when(core == 1)
     def _():
-        put_halo(0, hcore_ref, hcorex_ref, vcore_ref)
-        put_halo(1, hchip_ref, hchipx_ref, vchip_ref)
+        put_halo(0, hcore_ref, hcorex_ref, first, vcore_ref)
+        put_halo(1, hchip_ref, hchipx_ref, 0, vchip_ref)
 
     @pl.when(core == 0)
     def _():
-        put_halo(1, hcore_ref, hcorex_ref, vcore_ref)
-        put_halo(0, hchip_ref, hchipx_ref, vchip_ref)
+        put_halo(1, hcore_ref, hcorex_ref, first, vcore_ref)
+        put_halo(0, hchip_ref, hchipx_ref, 0, vchip_ref)
 
 
 def stage(first, orbs, weight, vcore, vchip):
@@ -311,7 +335,7 @@
 
 
 def propagate_body(
-    occ_ref, base_ref, v_ref, field_ref, edge_ref, acore_ref, achip_ref, acorex_ref, achipx_ref,
+    occ_ref, base_ref, v_ref, field_ref, edge_ref, acore_ref, achip_ref, achipx_ref,
     out_ref, norm_ref, a_ref, ping_ref, pong_ref, w_ref,
 ):
     core, half = core_index(), half_index()
@@ -319,10 +343,10 @@
     clear(pong_ref, WIDE)
     clear(out_ref, DEPTH + 2)
 
-    def put_field(j, fld_ref, edg_ref, i):
+    def put_field(j, fld_ref, edg_ref, i, k):
         total = v_ref[j]
         for comp in range(3):
-            value, edge = fld_ref[i, comp], edg_ref[i, comp]
+            value, edge = fld_ref[i, comp], edg_ref[k, comp]
             joined = jnp.where(
                 half == 0, jnp.concatenate([value, edge], axis=0), jnp.concatenate([edge, value], axis=0)
             )
@@ -332,22 +356,12 @@
 
     @pl.loop(0, DEPTH)
     def _(z):
-        put_field(z + MARGIN, field_ref, edge_ref, z)
-
-    def put_halo(above, fld_ref, edg_ref):
-        @pl.loop(0, MARGIN)
-        def _(i):
-            put_field(above * (DEPTH + MARGIN) + i, fld_ref, edg_ref, i)
-
-    @pl.when(core == 1)
-    def _():
-        put_halo(0, acore_ref, acorex_ref)
-        put_halo(1, achip_ref, achipx_ref)
-
-    @pl.when(core == 0)
-    def _():
-        put_halo(1, acore_ref, acorex_ref)
-        put_halo(0, achip_ref, achipx_ref)
+        put_field(z + MARGIN, field_ref, edge_ref, z, z + MARGIN * core)
+
+    @pl.loop(0, MARGIN)
+    def _(i):
+        put_field((1 - core) * (DEPTH + MARGIN) + i, acore_ref, edge_ref, i, (1 - core) * DEPTH + i)
+        put_field(core * (DEPTH + MARGIN) + i, achip_ref, achipx_ref, i, i)
 
     first = lax.axis_index("slab") * DEPTH - HALO
     sums = [jnp.zeros((8, NY), F32), jnp.zeros((8, NY), F32)]
@@ -401,7 +415,7 @@
         "propagate",
         propagate_body,
         [(DEPTH + 2, 4, XL, NY), (3, 8, NY), (DEPTH + 2 * MARGIN, 3, LOCAL, NY)],
-        [smem()] + [vmem()] * 8,
+        [smem()] + [vmem()] * 7,
         [
             pltpu.VMEM((WIDE, 4, XL, NY), F32),
             pltpu.VMEM((WIDE, 4, XL, NY), F32),
@@ -559,30 +573,36 @@
     return call("update", functools.partial(update_body, last), outs, [vmem()] * 4, flops=500000)(got, curl, e_rows, a_rows)
 
 
-def hand_back_body(wide_ref, out_ref):
+def hand_back_body(wide_ref, early_ref, late_ref):
     half = half_index()
     for z in range(DEPTH):
         for part in range(2):
-            out_ref[z, part] = own_rows(wide_ref[z + 1, 2 + part, PAD : PAD + LOCAL, :], half)
+            rows = own_rows(wide_ref[z + 1, 2 + part, PAD : PAD + LOCAL, :], half)
+            if z < EARLY:
+                early_ref[z, part] = rows
+            else:
+                late_ref[z - EARLY, part] = rows
 
 
 def hand_back(wide):
-    return call("hand_back", hand_back_body, [(DEPTH, 2, HALF, NY)], [vmem()])(wide)[0]
-
-
-def finish_body(scale_ref, wide_ref, theirs_ref, out_ref):
+    return call(
+        "hand_back", hand_back_body, [(EARLY, 2, HALF, NY), (DEPTH - EARLY, 2, HALF, NY)], [vmem()]
+    )(wide)
+
+
+def finish_body(scale_ref, wide_ref, early_ref, late_ref, out_ref):
     half = half_index()
     scale = scale_ref[0, 0:1, :]
     for z in range(DEPTH):
         for part in range(2):
             mine = own_rows(wide_ref[z + 1, part, PAD : PAD + LOCAL, :], half) * scale
-            theirs = theirs_ref[z, part] * scale
+            theirs = (early_ref[z, part] if z < EARLY else late_ref[z - EARLY, part]) * scale
             out_ref[part, pl.ds(z, HALF, stride=DEPTH), :] = jnp.where(half == 0, mine, theirs)
             out_ref[part, pl.ds(HALF * DEPTH + z, HALF, stride=DEPTH), :] = jnp.where(half == 0, theirs, mine)
 
 
-def finish(scale, wide, theirs):
-    return call("finish", finish_body, [(2, NX * DEPTH, NY)], [vmem()] * 3)(scale, wide, theirs)[0]
+def finish(scale, wide, early, late):
+    return call("finish", finish_body, [(2, NX * DEPTH, NY)], [vmem()] * 4)(scale, wide, early, late)[0]
 
 
 def everyone(copies):
@@ -590,34 +610,35 @@
 
 
 def per_device(orbitals, potential, occupation, e_field, a_field):
-    own, swap, weight, core, chip, corex, chipx, e_rows = prepare(orbitals, potential, e_field)
-    other = send(swap, HALVES)
-    vcore, vchip = send(core, CORE), send(chip, CHIP)
-    orbs = (own, other, vcore, vchip, send(corex, CORE_ACROSS), send(chipx, CHIP_ACROSS))
-    a_field, swap = lax.optimization_barrier((a_field, swap))
     copies, a_rows = spread(a_field)
     got = everyone(copies)
+    own, swap, weight, core, chip, chipx, e_rows = prepare(orbitals, potential, e_field)
+    vcore, vchip, chipx = send(core, CORE), send(chip, CHIP), send(chipx, CHIP_ACROSS)
+    other = send(swap, HALVES)
+    got, vcore, vchip = lax.optimization_barrier((got, vcore, vchip))
     scale = jnp.ones((2, 8, NY), F32)
     for step in range(STEPS):
         last = step == STEPS - 1
-        field, edge, acore, achip, acorex, achipx = assemble(got)
-        fields = (
-            field,
-            send(edge, HALVES),
-            send(acore, CORE),
-            send(achip, CHIP),
-            send(acorex, CORE_ACROSS),
-            send(achipx, CHIP_ACROSS),
-        )
+        field, edge, acore, achip, achipx = assemble(got)
+        acore = send(acore, CORE)
+        achip = send(achip, CHIP)
+        edge = corners(edge, acore)
+        edge = send(edge, HALVES)
+        if step == 0:
+            edge, other = lax.optimization_barrier((edge, other))
+        achipx = send(achipx, CHIP_ACROSS)
+        if step == 0:
+            orbs = (own, other, vcore, vchip, send(lend(other), CORE), chipx)
         base, v = stage(2 * HALO * step, orbs, weight, vcore, vchip)
-        wide, norm, field = propagate(occupation, base, v, fields)
+        wide, norm, field = propagate(occupation, base, v, (field, edge, acore, achip, achipx))
         norm = norm + send(norm, CORE)
         norms = (norm, send(norm, CHIP_SUM), send(norm, HALVES), send(norm, BOTH_SUM))
         flow = current(wide, field)
         if last:
-            theirs = hand_back(wide)
-            flow, theirs = lax.optimization_barrier((flow, theirs))
-            theirs = send(theirs, HALVES)
+            early, late = hand_back(wide)
+            early = send(early, HALVES)
+            flow, early, late = lax.optimization_barrier((flow, early, late))
+            late = send(late, HALVES)
         else:
             edge = send(edges(wide), HALVES)
             flow, edge = lax.optimization_barrier((flow, edge))
@@ -625,16 +646,17 @@
         flows = everyone(flow.reshape(GROUP, PACK, NY))
         curl = double_curl(field)
         if not last:
-            own, other, core, chip = rims(wide, edge)
-            flows, core, chip = lax.optimization_barrier((flows, core, chip))
+            own, other, core, chip, chipx = rims(wide, edge)
             core, chip = send(core, CORE), send(chip, CHIP)
+            flows, core, chip, chipx = lax.optimization_barrier((flows, core, chip, chipx))
+            chipx = send(chipx, CHIP)
             copies, a_rows, e_rows = update(last, flows, curl, e_rows, a_rows)
             got = everyone(copies)
-            got, core, chip = lax.optimization_barrier((got, core, chip))
-            orbs = (own, other, core, chip, core, chip)
+            got, chipx = lax.optimization_barrier((got, chipx))
+            orbs = (own, other, core, chip, core, chipx)
         else:
             e_new, a_new = update(last, flows, curl, e_rows, a_rows)
-            orbitals = finish(scale, wide, theirs)
+            orbitals = finish(scale, wide, early, late)
     return (
         orbitals.reshape(1, 2, NX, DEPTH, NY),
         e_new.reshape(3, ROWS, DEPTH, NY),

time: 171 us -> 158 us (0.924)
  starting transfers between devices: 75.6 us -> 65.5 us
  local copies, waits for them, and re-layouts: 15.4 us -> 13.4 us
    all_to_all x4, waiting for transfers between devices: 24.7 us -> 32.4 us  [everyone(): lax.all_to_all(copies, 'orb', 0, 0, tiled=True, axis_index_groups=GROUPS)]
    ppermute x27, starting transfers between devices: 51 us -> 43.6 us  [send(): return lax.ppermute(value, ALL, table)]
    ppermute x27, waiting for transfers between devices: 28 us -> 21.1 us  [send(): return lax.ppermute(value, ALL, table)]
    all_to_all x4, starting transfers between devices: 24.6 us -> 21.9 us  [everyone(): lax.all_to_all(copies, 'orb', 0, 0, tiled=True, axis_index_groups=GROUPS)]
    pallas_call x2, Pallas kernels: 3.19 us -> 0.78 us  [stage(): call('stage', functools.partial(stage_body, first), [(WIDE, 4, XL, NY), (...]
    unnamed x40 -> x62, local copies, waits for them, and re-layouts: 15.4 us -> 13.4 us
  transfers between devices with their start and end apart: 31 -> 31, of which waited for: 12 -> 14; matrix products, arithmetic and copies ran while one was open for 0% -> 0% of each run, Pallas kernels for 4% -> 5%
where the time goes in v4:
time: 158 us; the launch traced here: 157 us
  starting transfers between devices  65.5 us (41%)
  waiting for transfers between devices  53.5 us (34%)
  Pallas kernels  23 us (15%)
  local copies, waits for them, and re-layouts  13.4 us (8%)
  between operations  1.82 us (1%)
    ppermute x27, starting transfers between devices, send(): return lax.ppermute(value, ALL, table)  43.6 us
    all_to_all x4, waiting for transfers between devices, everyone(): lax.all_to_all(copies, 'orb', 0, 0, tiled=True, axis_index_groups=GROUPS)  32.4 us
    all_to_all x4, starting transfers between devices, everyone(): lax.all_to_all(copies, 'orb', 0, 0, tiled=True, axis_index_groups=GROUPS)  21.9 us
    ppermute x27, waiting for transfers between devices, send(): return lax.ppermute(value, ALL, table)  21.1 us
    unnamed x62, local copies, waits for them, and re-layouts  13.4 us
    pallas_call x2, Pallas kernels, propagate(): call('propagate', propagate_body, [(DEPTH + 2, 4, XL, NY), (3, 8, NY), (D...  11.6 us
  transfers between devices with their start and end apart: 31, of which 14 were waited for; matrix products, arithmetic and copies ran while one was open for 0% of the time, Pallas kernels for 5%

profile of v4, /device:TPU:0, one launch (start us, length us, event | category | flops | bytes accessed | tf_op | source)
XLA Modules:
  0.0 157.2 jit_solution(1906000926039616889)
XLA Ops:
  0.7 0.9 copy-done.27
  1.6 1.0 spread.1
  2.5 7.1 %all-to-all-start = ((f32[16,96,128]{2,1,0:T(8,128)}), f32[16,96,128]{2,1,0:T(8,128)S(1)}, u32[]{:S(2)}, u32[]{:S(2)}) async-start(f32[16,96,128]{2,1,0:T(8,128)} %get-tuple-element.65), calls=%async_computation | async-start | bytes 1572864 | tf_op jit(solution)/shard_map/all_to_all | solution.py:609
  9.7 0.8 copy-done.18
  10.5 1.3 prepare.1
  12.4 0.7 collective-permute-start.1
  13.1 4.0 %collective-permute-start.4 = (f32[8,2,72,128]{3,2,1,0:T(8,128)}, f32[8,2,72,128]{3,2,1,0:T(8,128)S(1)}, u32[]{:S(2)}, u32[]{:S(2)}) collective-permute-start(f32[8,2,72,128]{3,2,1,0:T(8,128)} %get-tuple-element.71), channel_id=1, source_target_pairs={{0,64},{1,65},{2,66},{3,67},{4,68},{5,69},{6,70},{7,71},{8,72},{9,... | collective-permute-start | bytes 1769480 | tf_op jit(solution)/shard_map/ppermute | solution.py:70
  17.1 6.9 %all-to-all-done = f32[16,96,128]{2,1,0:T(8,128)S(1)} async-done(((f32[16,96,128]{2,1,0:T(8,128)}), f32[16,96,128]{2,1,0:T(8,128)S(1)}, u32[]{:S(2)}, u32[]{:S(2)}) %all-to-all-start) | async-done | bytes 786464 | tf_op jit(solution)/shard_map/all_to_all | solution.py:609
  24.2 3.8 %collective-permute-start.2 = (f32[4,3,64,128]{3,2,1,0:T(8,128)S(1)}, f32[4,3,64,128]{3,2,1,0:T(8,128)S(1)}, u32[]{:S(2)}, u32[]{:S(2)}) collective-permute-start(f32[4,3,64,128]{3,2,1,0:T(8,128)S(1)} %get-tuple-element.70), channel_id=1, source_target_pairs={{0,1},{1,0},{2,3},{3,2},{4,5},{5,4},{6,7},{7,6},{8,9},{9,8},{10,11... | collective-permute-start | bytes 1179656 | tf_op jit(solution)/shard_map/ppermute | solution.py:70
  28.0 1.3 collective-permute-done.2.core_ref.acore_ref
  29.3 4.9 %collective-permute-start.3 = (f32[12,3,8,128]{3,2,1,0:T(8,128)S(1)}, f32[12,3,8,128]{3,2,1,0:T(8,128)S(1)}, u32[]{:S(2)}, u32[]{:S(2)}) collective-permute-start(f32[12,3,8,128]{3,2,1,0:T(8,128)S(1)} %corners.2), channel_id=1, source_target_pairs={{0,64},{1,65},{2,66},{3,67},{4,68},{5,69},{6,70},{7,71},{8,72},{9,... | collective-permute-start | bytes 442376 | tf_op jit(solution)/shard_map/ppermute | solution.py:70
  34.2 0.7 collective-permute-start.7
  34.9 0.7 collective-permute-start.6
  35.6 3.4 %collective-permute-done.3.edge_ref = f32[12,3,8,128]{3,2,1,0:T(8,128)S(1)} collective-permute-done((f32[12,3,8,128]{3,2,1,0:T(8,128)S(1)}, f32[12,3,8,128]{3,2,1,0:T(8,128)S(1)}, u32[]{:S(2)}, u32[]{:S(2)}) %collective-permute-start.3) | collective-permute-done | bytes 147488 | tf_op jit(solution)/shard_map/ppermute | solution.py:70
  39.0 1.1 collective-permute-start.5
  40.1 0.7 collective-permute-start.8
  41.9 5.8 %propagate.2 = (f32[10,4,88,128]{3,2,1,0:T(8,128)S(1)}, f32[3,8,128]{2,1,0:T(8,128)S(1)}, f32[16,3,72,128]{3,2,1,0:T(8,128)S(1)}) custom-call(f32[1]{0:T(128)S(6)} %copy.8.occ_ref, f32[18,4,88,128]{3,2,1,0:T(8,128)S(1)} %get-tuple-element.77.base_ref, f32[16,72,128]{2,1,0:T(8,128)S(1)} %get-tuple-element.78.v_ref, ...), custom_call_target="tpu_custom_call" | custom-call | flops 60000000 | bytes 7168000 | tf_op jit(solution)/shard_map/propagate/pallas_call | solution.py:414
  47.7 2.9 %collective-permute-start.13 = (f32[8,4,8,128]{3,2,1,0:T(8,128)S(1)}, f32[8,4,8,128]{3,2,1,0:T(8,128)S(1)}, u32[]{:S(2)}, u32[]{:S(2)}) collective-permute-start(f32[8,4,8,128]{3,2,1,0:T(8,128)S(1)} %edges.1), channel_id=1, source_target_pairs={{0,64},{1,65},{2,66},{3,67},{4,68},{5,69},{6,70},{7,71},{8,72},{9,... | collective-permute-start | bytes 393224 | tf_op jit(solution)/shard_map/ppermute | solution.py:70
  50.6 3.5 %collective-permute-start.9 = (f32[3,8,128]{2,1,0:T(8,128)S(1)}, f32[3,8,128]{2,1,0:T(8,128)S(1)}, u32[]{:S(2)}, u32[]{:S(2)}) collective-permute-start(f32[3,8,128]{2,1,0:T(8,128)S(1)} %get-tuple-element.83), channel_id=1, source_target_pairs={{0,1},{1,0},{2,3},{3,2},{4,5},{5,4},{6,7},{7,6},{8,9},{9,8},{10,11... | collective-permute-start | bytes 36872 | tf_op jit(solution)/shard_map/ppermute | solution.py:70
  54.1 0.8 collective-permute-done.9
  55.0 1.7 %collective-permute-start.10 = (f32[3,8,128]{2,1,0:T(8,128)S(1)}, f32[3,8,128]{2,1,0:T(8,128)S(1)}, u32[]{:S(2)}, u32[]{:S(2)}) collective-permute-start(f32[3,8,128]{2,1,0:T(8,128)S(1)} %add.6.n_ref), channel_id=1, source_target_pairs={{0,2},{1,3},{2,0},{3,1},{4,6},{5,7},{6,4},{7,5},{8,10},{9,11},{10,... | collective-permute-start | bytes 36872 | tf_op jit(solution)/shard_map/ppermute | solution.py:70
  56.7 1.9 %collective-permute-start.11 = (f32[3,8,128]{2,1,0:T(8,128)S(1)}, f32[3,8,128]{2,1,0:T(8,128)S(1)}, u32[]{:S(2)}, u32[]{:S(2)}) collective-permute-start(f32[3,8,128]{2,1,0:T(8,128)S(1)} %add.6.n_ref), channel_id=1, source_target_pairs={{0,64},{1,65},{2,66},{3,67},{4,68},{5,69},{6,70},{7,71},{8,72},{9,... | collective-permute-start | bytes 36872 | tf_op jit(solution)/shard_map/ppermute | solution.py:70
  58.6 1.1 collective-permute-start.12
  59.7 1.0 current.2.flow_ref
  60.7 1.1 rims.1
  61.7 0.7 copy-done.30
  62.5 1.0 collective-permute-done.12.nboth_ref
  63.8 0.8 copy-done.5
  64.7 7.3 %all-to-all-start.1 = ((f32[16,96,128]{2,1,0:T(8,128)}), f32[16,96,128]{2,1,0:T(8,128)}, u32[]{:S(2)}, u32[]{:S(2)}) async-start(f32[16,96,128]{2,1,0:T(8,128)} %bitcast.14), calls=%async_computation.1 | async-start | bytes 1572864 | tf_op jit(solution)/shard_map/all_to_all | solution.py:609
  71.9 0.7 collective-permute-start.15
  73.4 0.7 copy-done.12
  74.1 11.8 %all-to-all-done.1.got_ref = f32[16,96,128]{2,1,0:T(8,128)} async-done(((f32[16,96,128]{2,1,0:T(8,128)}), f32[16,96,128]{2,1,0:T(8,128)}, u32[]{:S(2)}, u32[]{:S(2)}) %all-to-all-start.1) | async-done | bytes 786464 | tf_op jit(solution)/shard_map/all_to_all | solution.py:609
  85.9 0.8 copy-done.17
  86.7 0.8 copy-done.20
  87.5 0.8 copy-done.22
  88.3 1.3 update.2
  89.7 0.9 copy-done.6
  91.2 3.6 %all-to-all-start.2 = ((f32[16,96,128]{2,1,0:T(8,128)}), f32[16,96,128]{2,1,0:T(8,128)S(1)}, u32[]{:S(2)}, u32[]{:S(2)}) async-start(f32[16,96,128]{2,1,0:T(8,128)} %copy-done.6), calls=%async_computation.2 | async-start | bytes 1572864 | tf_op jit(solution)/shard_map/all_to_all | solution.py:609
  94.8 0.9 collective-permute-start.16
  95.7 0.7 copy-done.14
  96.4 11.5 %all-to-all-done.2 = f32[16,96,128]{2,1,0:T(8,128)S(1)} async-done(((f32[16,96,128]{2,1,0:T(8,128)}), f32[16,96,128]{2,1,0:T(8,128)S(1)}, u32[]{:S(2)}, u32[]{:S(2)}) %all-to-all-start.2) | async-done | bytes 786464 | tf_op jit(solution)/shard_map/all_to_all | solution.py:609
  108.1 0.7 collective-permute-start.19
  108.8 1.0 collective-permute-done.17.core_ref.acore_ref
  109.9 3.0 %collective-permute-start.18 = (f32[12,3,8,128]{3,2,1,0:T(8,128)S(1)}, f32[12,3,8,128]{3,2,1,0:T(8,128)S(1)}, u32[]{:S(2)}, u32[]{:S(2)}) collective-permute-start(f32[12,3,8,128]{3,2,1,0:T(8,128)S(1)} %corners.3), channel_id=1, source_target_pairs={{0,64},{1,65},{2,66},{3,67},{4,68},{5,69},{6,70},{7,71},{8,72},{9,... | collective-permute-start | bytes 442376 | tf_op jit(solution)/shard_map/ppermute | solution.py:70
  113.6 1.0 copy-done.13
  114.6 1.0 copy-done.15
  116.0 2.2 %collective-permute-done.18.edge_ref = f32[12,3,8,128]{3,2,1,0:T(8,128)S(1)} collective-permute-done((f32[12,3,8,128]{3,2,1,0:T(8,128)S(1)}, f32[12,3,8,128]{3,2,1,0:T(8,128)S(1)}, u32[]{:S(2)}, u32[]{:S(2)}) %collective-permute-start.18) | collective-permute-done | bytes 147488 | tf_op jit(solution)/shard_map/ppermute | solution.py:70
  118.2 5.8 %propagate.3 = (f32[10,4,88,128]{3,2,1,0:T(8,128)S(1)}, f32[3,8,128]{2,1,0:T(8,128)S(1)}, f32[16,3,72,128]{3,2,1,0:T(8,128)S(1)}) custom-call(f32[1]{0:T(128)S(6)} %copy.8.occ_ref, f32[18,4,88,128]{3,2,1,0:T(8,128)S(1)} %get-tuple-element.103.base_ref, f32[16,72,128]{2,1,0:T(8,128)S(1)} %get-tuple-element.104.v_ref, ...), custom_call_target="tpu_custom_call" | custom-call | flops 60000000 | bytes 7168000 | tf_op jit(solution)/shard_map/propagate/pallas_call | solution.py:414
  124.0 3.2 %collective-permute-start.25 = (f32[3,2,64,128]{3,2,1,0:T(8,128)S(1)}, f32[3,2,64,128]{3,2,1,0:T(8,128)S(1)}, u32[]{:S(2)}, u32[]{:S(2)}) collective-permute-start(f32[3,2,64,128]{3,2,1,0:T(8,128)S(1)} %get-tuple-element.114), channel_id=1, source_target_pairs={{0,64},{1,65},{2,66},{3,67},{4,68},{5,69},{6,70},{7,71},{8,72},{9,... | collective-permute-start | bytes 589832 | tf_op jit(solution)/shard_map/ppermute | solution.py:70
  127.2 1.0 collective-permute-start.21
  128.3 0.8 collective-permute-done.21
  129.1 2.6 %collective-permute-start.22 = (f32[3,8,128]{2,1,0:T(8,128)S(1)}, f32[3,8,128]{2,1,0:T(8,128)S(1)}, u32[]{:S(2)}, u32[]{:S(2)}) collective-permute-start(f32[3,8,128]{2,1,0:T(8,128)S(1)} %add.7.n_ref), channel_id=1, source_target_pairs={{0,2},{1,3},{2,0},{3,1},{4,6},{5,7},{6,4},{7,5},{8,10},{9,11},{10,... | collective-permute-start | bytes 36872 | tf_op jit(solution)/shard_map/ppermute | solution.py:70
  131.7 1.6 %collective-permute-start.23 = (f32[3,8,128]{2,1,0:T(8,128)S(1)}, f32[3,8,128]{2,1,0:T(8,128)S(1)}, u32[]{:S(2)}, u32[]{:S(2)}) collective-permute-start(f32[3,8,128]{2,1,0:T(8,128)S(1)} %add.7.n_ref), channel_id=1, source_target_pairs={{0,64},{1,65},{2,66},{3,67},{4,68},{5,69},{6,70},{7,71},{8,72},{9,... | collective-permute-start | bytes 36872 | tf_op jit(solution)/shard_map/ppermute | solution.py:70
  133.4 1.0 collective-permute-start.24
  134.4 1.0 current.3.flow_ref
  135.4 1.6 %collective-permute-done.23.nhalf_ref = f32[3,8,128]{2,1,0:T(8,128)S(1)} collective-permute-done((f32[3,8,128]{2,1,0:T(8,128)S(1)}, f32[3,8,128]{2,1,0:T(8,128)S(1)}, u32[]{:S(2)}, u32[]{:S(2)}) %collective-permute-start.23) | collective-permute-done | bytes 12320 | tf_op jit(solution)/shard_map/ppermute | solution.py:70
  137.0 1.2 collective-permute-done.24.nboth_ref
  138.3 1.1 weigh.3
  139.4 3.9 %all-to-all-start.3 = ((f32[16,96,128]{2,1,0:T(8,128)}), f32[16,96,128]{2,1,0:T(8,128)S(1)}, u32[]{:S(2)}, u32[]{:S(2)}) async-start(f32[16,96,128]{2,1,0:T(8,128)} %bitcast.8), calls=%async_computation.3 | async-start | bytes 1572864 | tf_op jit(solution)/shard_map/all_to_all | solution.py:609
  143.8 1.5 copy-done.1
  145.5 7.5 %collective-permute-done.26.late_ref = f32[5,2,64,128]{3,2,1,0:T(8,128)S(1)} collective-permute-done((f32[5,2,64,128]{3,2,1,0:T(8,128)S(1)}, f32[5,2,64,128]{3,2,1,0:T(8,128)S(1)}, u32[]{:S(2)}, u32[]{:S(2)}) %collective-permute-start.26) | collective-permute-done | bytes 327712 | tf_op jit(solution)/shard_map/ppermute | solution.py:70
  153.0 1.3 finish.1
  154.3 2.2 %all-to-all-done.3.got_ref = f32[16,96,128]{2,1,0:T(8,128)S(1)} async-done(((f32[16,96,128]{2,1,0:T(8,128)}), f32[16,96,128]{2,1,0:T(8,128)S(1)}, u32[]{:S(2)}, u32[]{:S(2)}) %all-to-all-start.3) | async-done | bytes 786464 | tf_op jit(solution)/shard_map/all_to_all | solution.py:609
  156.5 0.7 update.3
  (86 shorter events, 5.0 us)
Async XLA Ops:
  0.6 9.0 %copy-start.4 = (f32[1,2,128,8,128]{4,3,2,1,0:T(8,128)S(1)}, f32[1,2,128,8,128]{4,3,2,1,0:T(8,128)}, u32[]{:S(2)}) copy-start(f32[1,2,128,8,128]{4,3,2,1,0:T(8,128)} %param.5) | copy-start | bytes 3145732
  0.6 9.0 %copy-start.11 = (f32[128,8,128]{2,1,0:T(8,128)S(1)}, f32[128,8,128]{2,1,0:T(8,128)}, u32[]{:S(2)}) copy-start(f32[128,8,128]{2,1,0:T(8,128)} %param.6) | copy-start | bytes 1572868
  0.7 0.9 copy-start.27
  2.5 7.1 %copy-start.19 = (f32[96,128]{1,0:T(8,128)}, f32[96,128]{1,0:T(8,128)S(1)}, u32[]{:S(2)}) copy-start(f32[96,128]{1,0:T(8,128)S(1)} %get-tuple-element.99.a_ref) | copy-start | bytes 147460
  2.5 21.5 %all-to-all-start = ((f32[16,96,128]{2,1,0:T(8,128)}), f32[16,96,128]{2,1,0:T(8,128)S(1)}, u32[]{:S(2)}, u32[]{:S(2)}) async-start(f32[16,96,128]{2,1,0:T(8,128)} %get-tuple-element.65), calls=%async_computation | async-start | bytes 1572864 | tf_op jit(solution)/shard_map/all_to_all | solution.py:609
  9.7 0.8 copy-start.18
  11.8 0.6 copy-start.21
  12.4 4.7 %copy-start.28 = (f32[10,72,128]{2,1,0:T(8,128)}, f32[10,72,128]{2,1,0:T(8,128)S(1)}, u32[]{:S(2)}) copy-start(f32[10,72,128]{2,1,0:T(8,128)S(1)} %get-tuple-element.75) | copy-start | bytes 1105924
  12.4 29.4 %copy-start.2 = (f32[8,72,128]{2,1,0:T(8,128)}, f32[8,72,128]{2,1,0:T(8,128)S(1)}, u32[]{:S(2)}) copy-start(f32[8,72,128]{2,1,0:T(8,128)S(1)} %get-tuple-element.76.weight_ref) | copy-start | bytes 884740
  12.4 4.7 %collective-permute-start = (f32[14,72,128]{2,1,0:T(8,128)S(1)}, f32[14,72,128]{2,1,0:T(8,128)S(1)}, u32[]{:S(2)}, u32[]{:S(2)}) collective-permute-start(f32[14,72,128]{2,1,0:T(8,128)S(1)} %get-tuple-element.66), channel_id=1, source_target_pairs={{0,1},{1,0},{2,3},{3,2},{4,5},{5,4},{6,7},{7,6},{8,9},{9,8},{10,11... | collective-permute-start | bytes 1548296 | tf_op jit(solution)/shard_map/ppermute | solution.py:70
  12.4 4.7 %collective-permute-start.1 = (f32[14,72,128]{2,1,0:T(8,128)S(1)}, f32[14,72,128]{2,1,0:T(8,128)S(1)}, u32[]{:S(2)}, u32[]{:S(2)}) collective-permute-start(f32[14,72,128]{2,1,0:T(8,128)S(1)} %get-tuple-element.67), channel_id=1, source_target_pairs={{1,2},{2,1},{5,6},{6,5},{9,10},{10,9},{13,14},{14,13},{17,18},{18,... | collective-permute-start | bytes 1548296 | tf_op jit(solution)/shard_map/ppermute | solution.py:70
  13.1 22.5 %collective-permute-start.4 = (f32[8,2,72,128]{3,2,1,0:T(8,128)}, f32[8,2,72,128]{3,2,1,0:T(8,128)S(1)}, u32[]{:S(2)}, u32[]{:S(2)}) collective-permute-start(f32[8,2,72,128]{3,2,1,0:T(8,128)} %get-tuple-element.71), channel_id=1, source_target_pairs={{0,64},{1,65},{2,66},{3,67},{4,68},{5,69},{6,70},{7,71},{8,72},{9,... | collective-permute-start | bytes 1769480 | tf_op jit(solution)/shard_map/ppermute | solution.py:70
  24.2 5.1 %collective-permute-start.2 = (f32[4,3,64,128]{3,2,1,0:T(8,128)S(1)}, f32[4,3,64,128]{3,2,1,0:T(8,128)S(1)}, u32[]{:S(2)}, u32[]{:S(2)}) collective-permute-start(f32[4,3,64,128]{3,2,1,0:T(8,128)S(1)} %get-tuple-element.70), channel_id=1, source_target_pairs={{0,1},{1,0},{2,3},{3,2},{4,5},{5,4},{6,7},{7,6},{8,9},{9,8},{10,11... | collective-permute-start | bytes 1179656 | tf_op jit(solution)/shard_map/ppermute | solution.py:70
  29.3 9.6 %collective-permute-start.3 = (f32[12,3,8,128]{3,2,1,0:T(8,128)S(1)}, f32[12,3,8,128]{3,2,1,0:T(8,128)S(1)}, u32[]{:S(2)}, u32[]{:S(2)}) collective-permute-start(f32[12,3,8,128]{3,2,1,0:T(8,128)S(1)} %corners.2), channel_id=1, source_target_pairs={{0,64},{1,65},{2,66},{3,67},{4,68},{5,69},{6,70},{7,71},{8,72},{9,... | collective-permute-start | bytes 442376 | tf_op jit(solution)/shard_map/ppermute | solution.py:70
  34.2 7.6 %collective-permute-start.7 = (f32[4,3,64,128]{3,2,1,0:T(8,128)S(1)}, f32[4,3,64,128]{3,2,1,0:T(8,128)S(1)}, u32[]{:S(2)}, u32[]{:S(2)}) collective-permute-start(f32[4,3,64,128]{3,2,1,0:T(8,128)S(1)} %get-tuple-element.81), channel_id=1, source_target_pairs={{1,2},{2,1},{5,6},{6,5},{9,10},{10,9},{13,14},{14,13},{17,18},{18,... | collective-permute-start | bytes 1179656 | tf_op jit(solution)/shard_map/ppermute | solution.py:70
  34.9 6.5 %collective-permute-start.6 = (f32[10,72,128]{2,1,0:T(8,128)}, f32[10,72,128]{2,1,0:T(8,128)S(1)}, u32[]{:S(2)}, u32[]{:S(2)}) collective-permute-start(f32[10,72,128]{2,1,0:T(8,128)} %copy-done.28), channel_id=1, source_target_pairs={{1,66},{2,65},{5,70},{6,69},{9,74},{10,73},{13,78},{14,77},{17,82}... | collective-permute-start | bytes 1105928 | tf_op jit(solution)/shard_map/ppermute | solution.py:70
  39.0 2.4 %collective-permute-start.5 = (f32[10,72,128]{2,1,0:T(8,128)S(1)}, f32[10,72,128]{2,1,0:T(8,128)S(1)}, u32[]{:S(2)}, u32[]{:S(2)}) collective-permute-start(f32[10,72,128]{2,1,0:T(8,128)S(1)} %lend.1), channel_id=1, source_target_pairs={{0,1},{1,0},{2,3},{3,2},{4,5},{5,4},{6,7},{7,6},{8,9},{9,8},{10,11... | collective-permute-start | bytes 1105928 | tf_op jit(solution)/shard_map/ppermute | solution.py:70
  40.1 1.8 %collective-permute-start.8 = (f32[4,3,8,128]{3,2,1,0:T(8,128)S(1)}, f32[4,3,8,128]{3,2,1,0:T(8,128)S(1)}, u32[]{:S(2)}, u32[]{:S(2)}) collective-permute-start(f32[4,3,8,128]{3,2,1,0:T(8,128)S(1)} %get-tuple-element.82), channel_id=1, source_target_pairs={{1,66},{2,65},{5,70},{6,69},{9,74},{10,73},{13,78},{14,77},{17,82}... | collective-permute-start | bytes 147464 | tf_op jit(solution)/shard_map/ppermute | solution.py:70
  47.7 12.9 %collective-permute-start.13 = (f32[8,4,8,128]{3,2,1,0:T(8,128)S(1)}, f32[8,4,8,128]{3,2,1,0:T(8,128)S(1)}, u32[]{:S(2)}, u32[]{:S(2)}) collective-permute-start(f32[8,4,8,128]{3,2,1,0:T(8,128)S(1)} %edges.1), channel_id=1, source_target_pairs={{0,64},{1,65},{2,66},{3,67},{4,68},{5,69},{6,70},{7,71},{8,72},{9,... | collective-permute-start | bytes 393224 | tf_op jit(solution)/shard_map/ppermute | solution.py:70
  50.6 4.3 %collective-permute-start.9 = (f32[3,8,128]{2,1,0:T(8,128)S(1)}, f32[3,8,128]{2,1,0:T(8,128)S(1)}, u32[]{:S(2)}, u32[]{:S(2)}) collective-permute-start(f32[3,8,128]{2,1,0:T(8,128)S(1)} %get-tuple-element.83), channel_id=1, source_target_pairs={{0,1},{1,0},{2,3},{3,2},{4,5},{5,4},{6,7},{7,6},{8,9},{9,8},{10,11... | collective-permute-start | bytes 36872 | tf_op jit(solution)/shard_map/ppermute | solution.py:70
  55.0 7.5 %collective-permute-start.10 = (f32[3,8,128]{2,1,0:T(8,128)S(1)}, f32[3,8,128]{2,1,0:T(8,128)S(1)}, u32[]{:S(2)}, u32[]{:S(2)}) collective-permute-start(f32[3,8,128]{2,1,0:T(8,128)S(1)} %add.6.n_ref), channel_id=1, source_target_pairs={{0,2},{1,3},{2,0},{3,1},{4,6},{5,7},{6,4},{7,5},{8,10},{9,11},{10,... | collective-permute-start | bytes 36872 | tf_op jit(solution)/shard_map/ppermute | solution.py:70
  56.7 5.8 %collective-permute-start.11 = (f32[3,8,128]{2,1,0:T(8,128)S(1)}, f32[3,8,128]{2,1,0:T(8,128)S(1)}, u32[]{:S(2)}, u32[]{:S(2)}) collective-permute-start(f32[3,8,128]{2,1,0:T(8,128)S(1)} %add.6.n_ref), channel_id=1, source_target_pairs={{0,64},{1,65},{2,66},{3,67},{4,68},{5,69},{6,70},{7,71},{8,72},{9,... | collective-permute-start | bytes 36872 | tf_op jit(solution)/shard_map/ppermute | solution.py:70
  58.6 4.9 %collective-permute-start.12 = (f32[3,8,128]{2,1,0:T(8,128)S(1)}, f32[3,8,128]{2,1,0:T(8,128)S(1)}, u32[]{:S(2)}, u32[]{:S(2)}) collective-permute-start(f32[3,8,128]{2,1,0:T(8,128)S(1)} %add.6.n_ref), channel_id=1, source_target_pairs={{0,66},{1,67},{2,64},{3,65},{4,70},{5,71},{6,68},{7,69},{8,74},{9,... | collective-permute-start | bytes 36872 | tf_op jit(solution)/shard_map/ppermute | solution.py:70
  61.7 0.7 copy-start.30
  62.5 1.3 copy-start.7
  62.5 1.3 copy-start.9
  62.5 1.3 copy-start.29
  62.5 11.7 %collective-permute-start.14 = (f32[20,72,128]{2,1,0:T(8,128)}, f32[20,72,128]{2,1,0:T(8,128)S(1)}, u32[]{:S(2)}, u32[]{:S(2)}) collective-permute-start(f32[20,72,128]{2,1,0:T(8,128)} %get-tuple-element.92), channel_id=1, source_target_pairs={{0,1},{1,0},{2,3},{3,2},{4,5},{5,4},{6,7},{7,6},{8,9},{9,8},{10,11... | collective-permute-start | bytes 2211848 | tf_op jit(solution)/shard_map/ppermute | solution.py:70
  63.8 0.9 copy-start.5
  64.7 21.3 %all-to-all-start.1 = ((f32[16,96,128]{2,1,0:T(8,128)}), f32[16,96,128]{2,1,0:T(8,128)}, u32[]{:S(2)}, u32[]{:S(2)}) async-start(f32[16,96,128]{2,1,0:T(8,128)} %bitcast.14), calls=%async_computation.1 | async-start | bytes 1572864 | tf_op jit(solution)/shard_map/all_to_all | solution.py:609
  71.9 1.5 collective-permute-start.15
  72.8 0.6 copy-start.16
  73.4 0.7 copy-start.12
  85.9 0.8 copy-start.17
  86.7 0.8 copy-start.20
  87.5 0.8 copy-start.22
  88.3 25.3 %copy-start.3 = (f32[8,72,128]{2,1,0:T(8,128)S(1)}, f32[8,72,128]{2,1,0:T(8,128)}, u32[]{:S(2)}) copy-start(f32[8,72,128]{2,1,0:T(8,128)} %copy-done.2) | copy-start | bytes 884740
  88.3 25.3 %copy-start.8 = (f32[8,2,72,128]{3,2,1,0:T(8,128)S(1)}, f32[8,2,72,128]{3,2,1,0:T(8,128)}, u32[]{:S(2)}) copy-start(f32[8,2,72,128]{3,2,1,0:T(8,128)} %copy-done.7) | copy-start | bytes 1769476
  89.7 0.9 copy-start.6
  90.5 0.6 copy-start.23
  91.2 16.7 %copy-start.25 = (f32[96,128]{1,0:T(8,128)}, f32[96,128]{1,0:T(8,128)S(1)}, u32[]{:S(2)}) copy-start(f32[96,128]{1,0:T(8,128)S(1)} %get-tuple-element.121.e_ref) | copy-start | bytes 147460
  91.2 16.7 %all-to-all-start.2 = ((f32[16,96,128]{2,1,0:T(8,128)}), f32[16,96,128]{2,1,0:T(8,128)S(1)}, u32[]{:S(2)}, u32[]{:S(2)}) async-start(f32[16,96,128]{2,1,0:T(8,128)} %copy-done.6), calls=%async_computation.2 | async-start | bytes 1572864 | tf_op jit(solution)/shard_map/all_to_all | solution.py:609
  94.8 0.9 collective-permute-start.16
  95.7 0.7 copy-start.14
  107.9 5.7 %copy-start.10 = (f32[8,2,72,128]{3,2,1,0:T(8,128)S(1)}, f32[8,2,72,128]{3,2,1,0:T(8,128)}, u32[]{:S(2)}) copy-start(f32[8,2,72,128]{3,2,1,0:T(8,128)} %copy-done.9) | copy-start | bytes 1769476
  108.1 1.8 %collective-permute-start.17 = (f32[4,3,64,128]{3,2,1,0:T(8,128)S(1)}, f32[4,3,64,128]{3,2,1,0:T(8,128)S(1)}, u32[]{:S(2)}, u32[]{:S(2)}) collective-permute-start(f32[4,3,64,128]{3,2,1,0:T(8,128)S(1)} %get-tuple-element.108), channel_id=1, source_target_pairs={{0,1},{1,0},{2,3},{3,2},{4,5},{5,4},{6,7},{7,6},{8,9},{9,8},{10,11... | collective-permute-start | bytes 1179656 | tf_op jit(solution)/shard_map/ppermute | solution.py:70
  108.1 7.8 %collective-permute-start.19 = (f32[4,3,64,128]{3,2,1,0:T(8,128)S(1)}, f32[4,3,64,128]{3,2,1,0:T(8,128)S(1)}, u32[]{:S(2)}, u32[]{:S(2)}) collective-permute-start(f32[4,3,64,128]{3,2,1,0:T(8,128)S(1)} %get-tuple-element.109), channel_id=1, source_target_pairs={{1,2},{2,1},{5,6},{6,5},{9,10},{10,9},{13,14},{14,13},{17,18},{18,... | collective-permute-start | bytes 1179656 | tf_op jit(solution)/shard_map/ppermute | solution.py:70
  109.9 8.3 %collective-permute-start.18 = (f32[12,3,8,128]{3,2,1,0:T(8,128)S(1)}, f32[12,3,8,128]{3,2,1,0:T(8,128)S(1)}, u32[]{:S(2)}, u32[]{:S(2)}) collective-permute-start(f32[12,3,8,128]{3,2,1,0:T(8,128)S(1)} %corners.3), channel_id=1, source_target_pairs={{0,64},{1,65},{2,66},{3,67},{4,68},{5,69},{6,70},{7,71},{8,72},{9,... | collective-permute-start | bytes 442376 | tf_op jit(solution)/shard_map/ppermute | solution.py:70
  112.9 3.1 %collective-permute-start.20 = (f32[4,3,8,128]{3,2,1,0:T(8,128)S(1)}, f32[4,3,8,128]{3,2,1,0:T(8,128)S(1)}, u32[]{:S(2)}, u32[]{:S(2)}) collective-permute-start(f32[4,3,8,128]{3,2,1,0:T(8,128)S(1)} %get-tuple-element.110), channel_id=1, source_target_pairs={{1,66},{2,65},{5,70},{6,69},{9,74},{10,73},{13,78},{14,77},{17,82}... | collective-permute-start | bytes 147464 | tf_op jit(solution)/shard_map/ppermute | solution.py:70
  113.6 1.0 copy-start.13
  114.6 1.0 copy-start.15
  124.0 11.4 %copy-start = (f32[16,3,72,128]{3,2,1,0:T(8,128)}, f32[16,3,72,128]{3,2,1,0:T(8,128)S(1)}, u32[]{:S(2)}) copy-start(f32[16,3,72,128]{3,2,1,0:T(8,128)S(1)} %get-tuple-element.113.field_ref) | copy-start | bytes 5308420
  124.0 11.3 %collective-permute-start.25 = (f32[3,2,64,128]{3,2,1,0:T(8,128)S(1)}, f32[3,2,64,128]{3,2,1,0:T(8,128)S(1)}, u32[]{:S(2)}, u32[]{:S(2)}) collective-permute-start(f32[3,2,64,128]{3,2,1,0:T(8,128)S(1)} %get-tuple-element.114), channel_id=1, source_target_pairs={{0,64},{1,65},{2,66},{3,67},{4,68},{5,69},{6,70},{7,71},{8,72},{9,... | collective-permute-start | bytes 589832 | tf_op jit(solution)/shard_map/ppermute | solution.py:70
  127.2 1.9 %collective-permute-start.21 = (f32[3,8,128]{2,1,0:T(8,128)S(1)}, f32[3,8,128]{2,1,0:T(8,128)S(1)}, u32[]{:S(2)}, u32[]{:S(2)}) collective-permute-start(f32[3,8,128]{2,1,0:T(8,128)S(1)} %get-tuple-element.111), channel_id=1, source_target_pairs={{0,1},{1,0},{2,3},{3,2},{4,5},{5,4},{6,7},{7,6},{8,9},{9,8},{10,11... | collective-permute-start | bytes 36872 | tf_op jit(solution)/shard_map/ppermute | solution.py:70
  129.1 6.3 %collective-permute-start.22 = (f32[3,8,128]{2,1,0:T(8,128)S(1)}, f32[3,8,128]{2,1,0:T(8,128)S(1)}, u32[]{:S(2)}, u32[]{:S(2)}) collective-permute-start(f32[3,8,128]{2,1,0:T(8,128)S(1)} %add.7.n_ref), channel_id=1, source_target_pairs={{0,2},{1,3},{2,0},{3,1},{4,6},{5,7},{6,4},{7,5},{8,10},{9,11},{10,... | collective-permute-start | bytes 36872 | tf_op jit(solution)/shard_map/ppermute | solution.py:70
  131.7 5.3 %collective-permute-start.23 = (f32[3,8,128]{2,1,0:T(8,128)S(1)}, f32[3,8,128]{2,1,0:T(8,128)S(1)}, u32[]{:S(2)}, u32[]{:S(2)}) collective-permute-start(f32[3,8,128]{2,1,0:T(8,128)S(1)} %add.7.n_ref), channel_id=1, source_target_pairs={{0,64},{1,65},{2,66},{3,67},{4,68},{5,69},{6,70},{7,71},{8,72},{9,... | collective-permute-start | bytes 36872 | tf_op jit(solution)/shard_map/ppermute | solution.py:70
  133.4 4.9 %collective-permute-start.24 = (f32[3,8,128]{2,1,0:T(8,128)S(1)}, f32[3,8,128]{2,1,0:T(8,128)S(1)}, u32[]{:S(2)}, u32[]{:S(2)}) collective-permute-start(f32[3,8,128]{2,1,0:T(8,128)S(1)} %add.7.n_ref), channel_id=1, source_target_pairs={{0,66},{1,67},{2,64},{3,65},{4,70},{5,71},{6,68},{7,69},{8,74},{9,... | collective-permute-start | bytes 36872 | tf_op jit(solution)/shard_map/ppermute | solution.py:70
  139.4 17.1 %all-to-all-start.3 = ((f32[16,96,128]{2,1,0:T(8,128)}), f32[16,96,128]{2,1,0:T(8,128)S(1)}, u32[]{:S(2)}, u32[]{:S(2)}) async-start(f32[16,96,128]{2,1,0:T(8,128)} %bitcast.8), calls=%async_computation.3 | async-start | bytes 1572864 | tf_op jit(solution)/shard_map/all_to_all | solution.py:609
  143.3 9.7 %collective-permute-start.26 = (f32[5,2,64,128]{3,2,1,0:T(8,128)S(1)}, f32[5,2,64,128]{3,2,1,0:T(8,128)S(1)}, u32[]{:S(2)}, u32[]{:S(2)}) collective-permute-start(f32[5,2,64,128]{3,2,1,0:T(8,128)S(1)} %get-tuple-element.119), channel_id=1, source_target_pairs={{0,64},{1,65},{2,66},{3,67},{4,68},{5,69},{6,70},{7,71},{8,72},{9,... | collective-permute-start | bytes 983048 | tf_op jit(solution)/shard_map/ppermute | solution.py:70
  143.8 1.5 copy-start.1
  145.4 11.1 %copy-start.24 = (f32[96,128]{1,0:T(8,128)S(1)}, f32[96,128]{1,0:T(8,128)}, u32[]{:S(2)}) copy-start(f32[96,128]{1,0:T(8,128)} %copy-done.23) | copy-start | bytes 147460
  145.4 11.0 %copy-start.26 = (f32[96,128]{1,0:T(8,128)S(1)}, f32[96,128]{1,0:T(8,128)}, u32[]{:S(2)}) copy-start(f32[96,128]{1,0:T(8,128)} %copy-done.25) | copy-start | bytes 147460

commit v5 on v4

--- a/solution.py
+++ b/solution.py
@@ -128,10 +128,11 @@
 
 
 def prepare_body(
-    orb_ref, pot_ref, e_ref, own_ref, swap_ref, weight_ref, core_ref, chip_ref, chipx_ref, e_rows_ref
+    orb_ref, pot_ref, a_ref, e_ref, own_ref, swap_ref, weight_ref, core_ref, chip_ref, chipx_ref, rows_ref
 ):
     core, half = core_index(), half_index()
-    to_rows(e_ref, e_rows_ref)
+    to_rows(a_ref, rows_ref.at[0])
+    to_rows(e_ref, rows_ref.at[1])
     for z in range(DEPTH):
         for part in range(2):
             own_ref[z, part], swap_ref[z, part] = split_rows(orb_ref[part, pl.ds(z, NX, stride=DEPTH), :], half)
@@ -148,7 +149,7 @@
         chip_ref[2 * HALO + i] = weight_ref[core * (DEPTH - MARGIN) + i]
 
 
-def prepare(orbitals, potential, e_field):
+def prepare(orbitals, potential, a_field, e_field):
     planes = 2 * HALO + MARGIN
     return call(
         "prepare",
@@ -157,12 +158,13 @@
         + [(DEPTH, LOCAL, NY)]
         + [(planes, LOCAL, NY)] * 2
         + [(2 * HALO, LOCAL, NY)]
-        + [(PACK, NY)],
-        [vmem()] * 3,
+        + [(2, PACK, NY)],
+        [vmem()] * 4,
         limit=12,
     )(
         orbitals.reshape(2, NX * DEPTH, NY),
         potential.reshape(NX * DEPTH, NY),
+        a_field.reshape(3, ROWS * DEPTH, NY),
         e_field.reshape(3, ROWS * DEPTH, NY),
     )
 
@@ -215,17 +217,17 @@
     )(wide, edge)
 
 
-def spread_body(a_ref, copies_ref, a_rows_ref):
-    to_rows(a_ref, a_rows_ref)
-    value = a_rows_ref[...]
+def spread_body(a_ref, copies_ref, rows_ref):
+    to_rows(a_ref, rows_ref)
+    value = rows_ref[...]
     for i in range(GROUP):
         copies_ref[i] = value
 
 
 def spread(a_field):
-    return call("spread", spread_body, [(GROUP, PACK, NY), (PACK, NY)], [vmem()])(
+    return call("spread", spread_body, [(GROUP, PACK, NY)], [vmem()], [pltpu.VMEM((PACK, NY), F32)])(
         a_field.reshape(3, ROWS * DEPTH, NY)
-    )
+    )[0]
 
 
 def assemble_body(got_ref, field_ref, edge_ref, core_ref, chip_ref, chipx_ref):
@@ -240,7 +242,7 @@
             odd = jnp.where(low, pltpu.roll(first, 4, 1), second)
             for z, value in ((2 * pair, even), (2 * pair + 1, odd)):
                 field_ref[z, comp] = value.reshape(HALF, NY)
-                edge_ref[z, comp] = jnp.where(half == 0, value[GROUP // 2 - 1], value[0])
+                edge_ref[z, comp] = jnp.where(half == 0, pltpu.roll(value[GROUP // 2 - 1], 4, 0), value[0])[0:ROWS]
     for i in range(MARGIN):
         to_core = (1 - core) * (DEPTH - MARGIN) + i
         to_chip = core * (DEPTH - MARGIN) + i
@@ -254,9 +256,9 @@
     return call(
         "assemble",
         assemble_body,
-        [(DEPTH, 3, HALF, NY), (DEPTH, 3, 8, NY)]
+        [(DEPTH, 3, HALF, NY), (DEPTH, 3, ROWS, NY)]
         + [(MARGIN, 3, HALF, NY)] * 2
-        + [(MARGIN, 3, 8, NY)],
+        + [(MARGIN, 3, ROWS, NY)],
         [vmem()],
     )(got.reshape(GROUP // 2, 2, PACK, NY))
 
@@ -268,12 +270,12 @@
             out_ref[z + MARGIN * core, comp] = edge_ref[z, comp]
         for i in range(MARGIN):
             out_ref[(1 - core) * DEPTH + i, comp] = jnp.where(
-                half == 0, core_ref[i, comp, HALF - 8 : HALF, :], core_ref[i, comp, 0:8, :]
+                half == 0, core_ref[i, comp, HALF - ROWS : HALF, :], core_ref[i, comp, 0:ROWS, :]
             )
 
 
 def corners(edge, acore):
-    return call("corners", corners_body, [(DEPTH + MARGIN, 3, 8, NY)], [vmem()] * 2)(edge, acore)[0]
+    return call("corners", corners_body, [(DEPTH + MARGIN, 3, ROWS, NY)], [vmem()] * 2)(edge, acore)[0]
 
 
 def clear(ref, count):
@@ -343,10 +345,13 @@
     clear(pong_ref, WIDE)
     clear(out_ref, DEPTH + 2)
 
+    near = half_rows((8, NY)) == (half == 0)
+
     def put_field(j, fld_ref, edg_ref, i, k):
         total = v_ref[j]
         for comp in range(3):
             value, edge = fld_ref[i, comp], edg_ref[k, comp]
+            edge = jnp.where(near, jnp.concatenate([edge, edge], axis=0), 0.0)
             joined = jnp.where(
                 half == 0, jnp.concatenate([value, edge], axis=0), jnp.concatenate([edge, value], axis=0)
             )
@@ -496,7 +501,7 @@
     )(prior, *norms, flow)
 
 
-def curl_body(field_ref, out_ref):
+def curl_body(field_ref, rows_ref, out_ref):
     owner = lax.axis_index("orb")
     place = lax.rem(owner, GROUP)
     tile = place // 2 + half_index()
@@ -538,19 +543,22 @@
         out_y = (lane_shifts(inner_y)[0] - inner_y) - (x_plus(ay) + x_minus(ay) + ayp + aym - 4.0 * ay)
         out_z = (up_inner_z - inner_z) - (x_plus(az) + x_minus(az) + az_up + az_dn - 4.0 * az)
         for comp, value in enumerate((out_x, out_y, out_z)):
-            out_ref[pl.ds((comp * DEPTH + z) * ROWS, ROWS), :] = pltpu.roll(value, 7, 0)[0:ROWS]
-
-
-def double_curl(field):
-    return call("double_curl", curl_body, [(PACK, NY)], [vmem()], flops=1000000)(field)[0]
-
-
-def update_body(last, got_ref, curl_ref, e_ref, a_ref, *outs):
+            out_ref[1, pl.ds((comp * DEPTH + z) * ROWS, ROWS), :] = pltpu.roll(value, 7, 0)[0:ROWS]
+    e_part = rows_ref[1] + WAVE_STEP * out_ref[1]
+    out_ref[1] = e_part
+    out_ref[0] = rows_ref[0] - WAVE_STEP * e_part
+
+
+def double_curl(field, rows):
+    return call("double_curl", curl_body, [(2, PACK, NY)], [vmem()] * 2, flops=1000000)(field, rows)[0]
+
+
+def update_body(last, got_ref, part_ref, *outs):
     total = got_ref[0]
     for i in range(1, GROUP):
         total = total + got_ref[i]
-    e_new = e_ref[...] + WAVE_STEP * (curl_ref[...] - total)
-    a_new = a_ref[...] - WAVE_STEP * e_new
+    e_new = part_ref[1] - WAVE_STEP * total
+    a_new = part_ref[0] + WAVE_STEP * WAVE_STEP * total
     if last:
         for ref, value in zip(outs, (e_new, a_new)):
             for comp in range(3):
@@ -558,19 +566,19 @@
                     start = (comp * DEPTH + z) * ROWS
                     ref[comp, pl.ds(z, ROWS, stride=DEPTH), :] = value[start : start + ROWS]
     else:
-        copies_ref, a_out_ref, e_out_ref = outs
-        a_out_ref[...] = a_new
-        e_out_ref[...] = e_new
+        copies_ref, rows_ref = outs
+        rows_ref[0] = a_new
+        rows_ref[1] = e_new
         for i in range(GROUP):
             copies_ref[i] = a_new
 
 
-def update(last, got, curl, e_rows, a_rows):
+def update(last, got, part):
     if last:
         outs = [(3, ROWS * DEPTH, NY)] * 2
     else:
-        outs = [(GROUP, PACK, NY), (PACK, NY), (PACK, NY)]
-    return call("update", functools.partial(update_body, last), outs, [vmem()] * 4, flops=500000)(got, curl, e_rows, a_rows)
+        outs = [(GROUP, PACK, NY), (2, PACK, NY)]
+    return call("update", functools.partial(update_body, last), outs, [vmem()] * 2, flops=500000)(got, part)
 
 
 def hand_back_body(wide_ref, early_ref, late_ref):
@@ -610,12 +618,11 @@
 
 
 def per_device(orbitals, potential, occupation, e_field, a_field):
-    copies, a_rows = spread(a_field)
-    got = everyone(copies)
-    own, swap, weight, core, chip, chipx, e_rows = prepare(orbitals, potential, e_field)
+    got = everyone(spread(a_field))
+    own, swap, weight, core, chip, chipx, rows = prepare(orbitals, potential, a_field, e_field)
     vcore, vchip, chipx = send(core, CORE), send(chip, CHIP), send(chipx, CHIP_ACROSS)
     other = send(swap, HALVES)
-    got, vcore, vchip = lax.optimization_barrier((got, vcore, vchip))
+    got, vcore = lax.optimization_barrier((got, vcore))
     scale = jnp.ones((2, 8, NY), F32)
     for step in range(STEPS):
         last = step == STEPS - 1
@@ -631,31 +638,31 @@
             orbs = (own, other, vcore, vchip, send(lend(other), CORE), chipx)
         base, v = stage(2 * HALO * step, orbs, weight, vcore, vchip)
         wide, norm, field = propagate(occupation, base, v, (field, edge, acore, achip, achipx))
-        norm = norm + send(norm, CORE)
+        norm, late_wide = lax.optimization_barrier((norm + send(norm, CORE), wide))
         norms = (norm, send(norm, CHIP_SUM), send(norm, HALVES), send(norm, BOTH_SUM))
         flow = current(wide, field)
         if last:
-            early, late = hand_back(wide)
+            early, late = hand_back(late_wide)
             early = send(early, HALVES)
             flow, early, late = lax.optimization_barrier((flow, early, late))
             late = send(late, HALVES)
         else:
-            edge = send(edges(wide), HALVES)
+            edge = send(edges(late_wide), HALVES)
             flow, edge = lax.optimization_barrier((flow, edge))
         flow, scale = weigh(scale, norms, flow)
         flows = everyone(flow.reshape(GROUP, PACK, NY))
-        curl = double_curl(field)
+        part = double_curl(field, rows)
         if not last:
             own, other, core, chip, chipx = rims(wide, edge)
             core, chip = send(core, CORE), send(chip, CHIP)
             flows, core, chip, chipx = lax.optimization_barrier((flows, core, chip, chipx))
             chipx = send(chipx, CHIP)
-            copies, a_rows, e_rows = update(last, flows, curl, e_rows, a_rows)
+            copies, rows = update(last, flows, part)
             got = everyone(copies)
             got, chipx = lax.optimization_barrier((got, chipx))
             orbs = (own, other, core, chip, core, chipx)
         else:
-            e_new, a_new = update(last, flows, curl, e_rows, a_rows)
+            e_new, a_new = update(last, flows, part)
             orbitals = finish(scale, wide, early, late)
     return (
         orbitals.reshape(1, 2, NX, DEPTH, NY),

time: 158 us -> 153 us (0.968)
  waiting for transfers between devices: 53.5 us -> 49.6 us
    ppermute x27, waiting for transfers between devices: 21.1 us -> 16.1 us  [send(): return lax.ppermute(value, ALL, table)]
    unnamed x62 -> x58, local copies, waits for them, and re-layouts: 13.4 us -> 13 us
where the time goes in v5:
time: 153 us; the launch traced here: 152 us
  starting transfers between devices  65 us (42%)
  waiting for transfers between devices  49.6 us (32%)
  Pallas kernels  23.1 us (15%)
  local copies, waits for them, and re-layouts  13 us (8%)
  between operations  1.82 us (1%)
    ppermute x27, starting transfers between devices, send(): return lax.ppermute(value, ALL, table)  44.6 us
    all_to_all x4, waiting for transfers between devices, everyone(): lax.all_to_all(copies, 'orb', 0, 0, tiled=True, axis_index_groups=GROUPS)  33.5 us
    all_to_all x4, starting transfers between devices, everyone(): lax.all_to_all(copies, 'orb', 0, 0, tiled=True, axis_index_groups=GROUPS)  20.3 us
    ppermute x27, waiting for transfers between devices, send(): return lax.ppermute(value, ALL, table)  16.1 us
    unnamed x58, local copies, waits for them, and re-layouts  13 us
    pallas_call x2, Pallas kernels, propagate(): call('propagate', propagate_body, [(DEPTH + 2, 4, XL, NY), (3, 8, NY), (D...  11.6 us
  transfers between devices with their start and end apart: 31, of which 14 were waited for; matrix products, arithmetic and copies ran while one was open for 0% of the time, Pallas kernels for 5%

profile of v5, /device:TPU:0, one launch (start us, length us, event | category | flops | bytes accessed | tf_op | source)
XLA Modules:
  0.0 152.5 jit_solution(4618719605768741529)
XLA Ops:
  0.7 0.9 copy-done.18
  1.6 1.0 spread.1
  2.5 7.1 %all-to-all-start = ((f32[16,96,128]{2,1,0:T(8,128)}), f32[16,96,128]{2,1,0:T(8,128)S(1)}, u32[]{:S(2)}, u32[]{:S(2)}) async-start(f32[16,96,128]{2,1,0:T(8,128)} %spread.1), calls=%async_computation | async-start | bytes 1572864 | tf_op jit(solution)/shard_map/all_to_all | solution.py:617
  9.7 1.3 prepare.1
  11.0 0.6 copy-done.20
  11.7 4.0 %collective-permute-start.3 = (f32[8,2,72,128]{3,2,1,0:T(8,128)}, f32[8,2,72,128]{3,2,1,0:T(8,128)S(1)}, u32[]{:S(2)}, u32[]{:S(2)}) collective-permute-start(f32[8,2,72,128]{3,2,1,0:T(8,128)} %get-tuple-element.69), channel_id=1, source_target_pairs={{0,64},{1,65},{2,66},{3,67},{4,68},{5,69},{6,70},{7,71},{8,72},{9,... | collective-permute-start | bytes 1769480 | tf_op jit(solution)/shard_map/ppermute | solution.py:70
  15.7 8.4 %all-to-all-done = f32[16,96,128]{2,1,0:T(8,128)S(1)} async-done(((f32[16,96,128]{2,1,0:T(8,128)}), f32[16,96,128]{2,1,0:T(8,128)S(1)}, u32[]{:S(2)}, u32[]{:S(2)}) %all-to-all-start) | async-done | bytes 786464 | tf_op jit(solution)/shard_map/all_to_all | solution.py:617
  24.3 0.7 collective-permute-start.4
  25.0 1.0 collective-permute-done.1.core_ref.acore_ref
  26.0 4.0 %collective-permute-start.2 = (f32[12,3,4,128]{3,2,1,0:T(4,128)S(1)}, f32[12,3,4,128]{3,2,1,0:T(4,128)S(1)}, u32[]{:S(2)}, u32[]{:S(2)}) collective-permute-start(f32[12,3,4,128]{3,2,1,0:T(4,128)S(1)} %corners.2), channel_id=1, source_target_pairs={{0,64},{1,65},{2,66},{3,67},{4,68},{5,69},{6,70},{7,71},{8,72},{9,... | collective-permute-start | bytes 221192 | tf_op jit(solution)/shard_map/ppermute | solution.py:70
  30.0 0.7 collective-permute-start.7
  30.6 0.7 collective-permute-start.6
  31.3 1.3 collective-permute-done.2.edge_ref
  32.7 6.4 %collective-permute-start.5 = (f32[10,72,128]{2,1,0:T(8,128)S(1)}, f32[10,72,128]{2,1,0:T(8,128)S(1)}, u32[]{:S(2)}, u32[]{:S(2)}) collective-permute-start(f32[10,72,128]{2,1,0:T(8,128)S(1)} %lend.1), channel_id=1, source_target_pairs={{0,1},{1,0},{2,3},{3,2},{4,5},{5,4},{6,7},{7,6},{8,9},{9,8},{10,11... | collective-permute-start | bytes 1105928 | tf_op jit(solution)/shard_map/ppermute | solution.py:70
  39.1 0.7 collective-permute-start.8
  40.9 5.8 %propagate.2 = (f32[10,4,88,128]{3,2,1,0:T(8,128)S(1)}, f32[3,8,128]{2,1,0:T(8,128)S(1)}, f32[16,3,72,128]{3,2,1,0:T(8,128)S(1)}) custom-call(f32[1]{0:T(128)S(6)} %copy.8.occ_ref, f32[18,4,88,128]{3,2,1,0:T(8,128)S(1)} %get-tuple-element.75.base_ref, f32[16,72,128]{2,1,0:T(8,128)S(1)} %get-tuple-element.76.v_ref, ...), custom_call_target="tpu_custom_call" | custom-call | flops 60000000 | bytes 7168000 | tf_op jit(solution)/shard_map/propagate/pallas_call | solution.py:419
  46.7 4.6 %collective-permute-start.9 = (f32[3,8,128]{2,1,0:T(8,128)S(1)}, f32[3,8,128]{2,1,0:T(8,128)S(1)}, u32[]{:S(2)}, u32[]{:S(2)}) collective-permute-start(f32[3,8,128]{2,1,0:T(8,128)S(1)} %get-tuple-element.81), channel_id=1, source_target_pairs={{0,1},{1,0},{2,3},{3,2},{4,5},{5,4},{6,7},{7,6},{8,9},{9,8},{10,11... | collective-permute-start | bytes 36872 | tf_op jit(solution)/shard_map/ppermute | solution.py:70
  51.3 0.8 collective-permute-done.9
  52.3 2.5 %collective-permute-start.10 = (f32[3,8,128]{2,1,0:T(8,128)S(1)}, f32[3,8,128]{2,1,0:T(8,128)S(1)}, u32[]{:S(2)}, u32[]{:S(2)}) collective-permute-start(f32[3,8,128]{2,1,0:T(8,128)S(1)} %add.6.n_ref), channel_id=1, source_target_pairs={{0,2},{1,3},{2,0},{3,1},{4,6},{5,7},{6,4},{7,5},{8,10},{9,11},{10,... | collective-permute-start | bytes 36872 | tf_op jit(solution)/shard_map/ppermute | solution.py:70
  54.8 1.4 collective-permute-start.11
  56.2 1.3 collective-permute-start.12
  57.5 1.0 current.2.flow_ref
  58.5 1.4 collective-permute-done.13.edge_ref
  59.8 1.0 rims.1
  60.9 0.7 copy-done.28
  62.8 0.6 copy-done.5
  63.3 6.0 %all-to-all-start.1 = ((f32[16,96,128]{2,1,0:T(8,128)}), f32[16,96,128]{2,1,0:T(8,128)}, u32[]{:S(2)}, u32[]{:S(2)}) async-start(f32[16,96,128]{2,1,0:T(8,128)} %bitcast.14), calls=%async_computation.1 | async-start | bytes 1572864 | tf_op jit(solution)/shard_map/all_to_all | solution.py:617
  69.3 0.7 collective-permute-start.15
  70.0 0.9 copy-done.21
  71.1 0.6 copy-done.12
  71.7 0.7 copy-done.14
  72.4 11.5 %all-to-all-done.1.got_ref = f32[16,96,128]{2,1,0:T(8,128)} async-done(((f32[16,96,128]{2,1,0:T(8,128)}), f32[16,96,128]{2,1,0:T(8,128)}, u32[]{:S(2)}, u32[]{:S(2)}) %all-to-all-start.1) | async-done | bytes 786464 | tf_op jit(solution)/shard_map/all_to_all | solution.py:617
  84.0 0.9 copy-done.13
  84.9 1.3 update.2
  86.2 0.9 copy-done.6
  87.1 3.6 %all-to-all-start.2 = ((f32[16,96,128]{2,1,0:T(8,128)}), f32[16,96,128]{2,1,0:T(8,128)S(1)}, u32[]{:S(2)}, u32[]{:S(2)}) async-start(f32[16,96,128]{2,1,0:T(8,128)} %copy-done.6), calls=%async_computation.2 | async-start | bytes 1572864 | tf_op jit(solution)/shard_map/all_to_all | solution.py:617
  90.7 0.9 collective-permute-start.16
  91.6 0.7 copy-done.16
  92.3 11.4 %all-to-all-done.2 = f32[16,96,128]{2,1,0:T(8,128)S(1)} async-done(((f32[16,96,128]{2,1,0:T(8,128)}), f32[16,96,128]{2,1,0:T(8,128)S(1)}, u32[]{:S(2)}, u32[]{:S(2)}) %all-to-all-start.2) | async-done | bytes 786464 | tf_op jit(solution)/shard_map/all_to_all | solution.py:617
  104.0 0.7 collective-permute-start.19
  104.7 1.0 collective-permute-done.17.core_ref.acore_ref
  105.7 3.5 %collective-permute-start.18 = (f32[12,3,4,128]{3,2,1,0:T(4,128)S(1)}, f32[12,3,4,128]{3,2,1,0:T(4,128)S(1)}, u32[]{:S(2)}, u32[]{:S(2)}) collective-permute-start(f32[12,3,4,128]{3,2,1,0:T(4,128)S(1)} %corners.3), channel_id=1, source_target_pairs={{0,64},{1,65},{2,66},{3,67},{4,68},{5,69},{6,70},{7,71},{8,72},{9,... | collective-permute-start | bytes 221192 | tf_op jit(solution)/shard_map/ppermute | solution.py:70
  109.2 0.7 collective-permute-start.20
  109.9 1.1 copy-done.10
  111.0 1.0 copy-done.15
  112.0 1.0 copy-done.17
  113.4 5.8 %propagate.3 = (f32[10,4,88,128]{3,2,1,0:T(8,128)S(1)}, f32[3,8,128]{2,1,0:T(8,128)S(1)}, f32[16,3,72,128]{3,2,1,0:T(8,128)S(1)}) custom-call(f32[1]{0:T(128)S(6)} %copy.8.occ_ref, f32[18,4,88,128]{3,2,1,0:T(8,128)S(1)} %get-tuple-element.102.base_ref, f32[16,72,128]{2,1,0:T(8,128)S(1)} %get-tuple-element.103.v_ref, ...), custom_call_target="tpu_custom_call" | custom-call | flops 60000000 | bytes 7168000 | tf_op jit(solution)/shard_map/propagate/pallas_call | solution.py:419
  119.2 3.4 %collective-permute-start.21 = (f32[3,8,128]{2,1,0:T(8,128)S(1)}, f32[3,8,128]{2,1,0:T(8,128)S(1)}, u32[]{:S(2)}, u32[]{:S(2)}) collective-permute-start(f32[3,8,128]{2,1,0:T(8,128)S(1)} %get-tuple-element.110), channel_id=1, source_target_pairs={{0,1},{1,0},{2,3},{3,2},{4,5},{5,4},{6,7},{7,6},{8,9},{9,8},{10,11... | collective-permute-start | bytes 36872 | tf_op jit(solution)/shard_map/ppermute | solution.py:70
  122.6 0.8 collective-permute-done.21
  123.5 1.9 %collective-permute-start.25 = (f32[3,2,64,128]{3,2,1,0:T(8,128)S(1)}, f32[3,2,64,128]{3,2,1,0:T(8,128)S(1)}, u32[]{:S(2)}, u32[]{:S(2)}) collective-permute-start(f32[3,2,64,128]{3,2,1,0:T(8,128)S(1)} %get-tuple-element.115), channel_id=1, source_target_pairs={{0,64},{1,65},{2,66},{3,67},{4,68},{5,69},{6,70},{7,71},{8,72},{9,... | collective-permute-start | bytes 589832 | tf_op jit(solution)/shard_map/ppermute | solution.py:70
  125.4 1.1 collective-permute-start.22
  126.5 2.2 %collective-permute-start.23 = (f32[3,8,128]{2,1,0:T(8,128)S(1)}, f32[3,8,128]{2,1,0:T(8,128)S(1)}, u32[]{:S(2)}, u32[]{:S(2)}) collective-permute-start(f32[3,8,128]{2,1,0:T(8,128)S(1)} %add.7.n_ref), channel_id=1, source_target_pairs={{0,64},{1,65},{2,66},{3,67},{4,68},{5,69},{6,70},{7,71},{8,72},{9,... | collective-permute-start | bytes 36872 | tf_op jit(solution)/shard_map/ppermute | solution.py:70
  128.7 1.4 collective-permute-start.24
  130.1 1.0 current.3.flow_ref
  131.1 1.5 collective-permute-done.25.early_ref
  132.8 0.8 collective-permute-done.24.nboth_ref
  133.6 1.1 weigh.3
  134.7 3.6 %all-to-all-start.3 = ((f32[16,96,128]{2,1,0:T(8,128)}), f32[16,96,128]{2,1,0:T(8,128)S(1)}, u32[]{:S(2)}, u32[]{:S(2)}) async-start(f32[16,96,128]{2,1,0:T(8,128)} %bitcast.8), calls=%async_computation.3 | async-start | bytes 1572864 | tf_op jit(solution)/shard_map/all_to_all | solution.py:617
  138.3 1.1 collective-permute-start.26
  139.4 1.5 copy-done.1
  141.1 7.2 %collective-permute-done.26.late_ref = f32[5,2,64,128]{3,2,1,0:T(8,128)S(1)} collective-permute-done((f32[5,2,64,128]{3,2,1,0:T(8,128)S(1)}, f32[5,2,64,128]{3,2,1,0:T(8,128)S(1)}, u32[]{:S(2)}, u32[]{:S(2)}) %collective-permute-start.26) | collective-permute-done | bytes 327712 | tf_op jit(solution)/shard_map/ppermute | solution.py:70
  148.3 1.3 finish.1
  149.6 2.2 %all-to-all-done.3.got_ref = f32[16,96,128]{2,1,0:T(8,128)S(1)} async-done(((f32[16,96,128]{2,1,0:T(8,128)}), f32[16,96,128]{2,1,0:T(8,128)S(1)}, u32[]{:S(2)}, u32[]{:S(2)}) %all-to-all-start.3) | async-done | bytes 786464 | tf_op jit(solution)/shard_map/all_to_all | solution.py:617
  151.8 0.7 update.3
  (82 shorter events, 3.2 us)
Async XLA Ops:
  0.6 9.0 %copy-start.4 = (f32[1,2,128,8,128]{4,3,2,1,0:T(8,128)S(1)}, f32[1,2,128,8,128]{4,3,2,1,0:T(8,128)}, u32[]{:S(2)}) copy-start(f32[1,2,128,8,128]{4,3,2,1,0:T(8,128)} %param.5) | copy-start | bytes 3145732
  0.6 9.0 %copy-start.11 = (f32[128,8,128]{2,1,0:T(8,128)S(1)}, f32[128,8,128]{2,1,0:T(8,128)}, u32[]{:S(2)}) copy-start(f32[128,8,128]{2,1,0:T(8,128)} %param.6) | copy-start | bytes 1572868
  0.7 0.9 copy-start.18
  1.6 8.1 %copy-start.19 = (f32[3,4,8,128]{3,2,1,0:T(8,128)S(1)}, f32[3,4,8,128]{3,2,1,0:T(8,128)}, u32[]{:S(2)}) copy-start(f32[3,4,8,128]{3,2,1,0:T(8,128)} %param.9) | copy-start | bytes 147460
  1.6 8.1 %copy-start.24 = (f32[3,4,8,128]{3,2,1,0:T(8,128)S(1)}, f32[3,4,8,128]{3,2,1,0:T(8,128)}, u32[]{:S(2)}) copy-start(f32[3,4,8,128]{3,2,1,0:T(8,128)} %param.8) | copy-start | bytes 147460
  2.5 21.5 %all-to-all-start = ((f32[16,96,128]{2,1,0:T(8,128)}), f32[16,96,128]{2,1,0:T(8,128)S(1)}, u32[]{:S(2)}, u32[]{:S(2)}) async-start(f32[16,96,128]{2,1,0:T(8,128)} %spread.1), calls=%async_computation | async-start | bytes 1572864 | tf_op jit(solution)/shard_map/all_to_all | solution.py:617
  11.0 0.6 copy-start.20
  11.7 4.0 %copy-start.25 = (f32[14,72,128]{2,1,0:T(8,128)}, f32[14,72,128]{2,1,0:T(8,128)S(1)}, u32[]{:S(2)}) copy-start(f32[14,72,128]{2,1,0:T(8,128)S(1)} %get-tuple-element.72) | copy-start | bytes 1548292
  11.7 4.0 %copy-start.26 = (f32[10,72,128]{2,1,0:T(8,128)}, f32[10,72,128]{2,1,0:T(8,128)S(1)}, u32[]{:S(2)}) copy-start(f32[10,72,128]{2,1,0:T(8,128)S(1)} %get-tuple-element.73) | copy-start | bytes 1105924
  11.7 29.2 %copy-start.2 = (f32[8,72,128]{2,1,0:T(8,128)}, f32[8,72,128]{2,1,0:T(8,128)S(1)}, u32[]{:S(2)}) copy-start(f32[8,72,128]{2,1,0:T(8,128)S(1)} %get-tuple-element.74.weight_ref) | copy-start | bytes 884740
  11.7 4.0 %collective-permute-start = (f32[14,72,128]{2,1,0:T(8,128)S(1)}, f32[14,72,128]{2,1,0:T(8,128)S(1)}, u32[]{:S(2)}, u32[]{:S(2)}) collective-permute-start(f32[14,72,128]{2,1,0:T(8,128)S(1)} %get-tuple-element.65), channel_id=1, source_target_pairs={{0,1},{1,0},{2,3},{3,2},{4,5},{5,4},{6,7},{7,6},{8,9},{9,8},{10,11... | collective-permute-start | bytes 1548296 | tf_op jit(solution)/shard_map/ppermute | solution.py:70
  11.7 19.6 %collective-permute-start.3 = (f32[8,2,72,128]{3,2,1,0:T(8,128)}, f32[8,2,72,128]{3,2,1,0:T(8,128)S(1)}, u32[]{:S(2)}, u32[]{:S(2)}) collective-permute-start(f32[8,2,72,128]{3,2,1,0:T(8,128)} %get-tuple-element.69), channel_id=1, source_target_pairs={{0,64},{1,65},{2,66},{3,67},{4,68},{5,69},{6,70},{7,71},{8,72},{9,... | collective-permute-start | bytes 1769480 | tf_op jit(solution)/shard_map/ppermute | solution.py:70
  24.2 1.8 %collective-permute-start.1 = (f32[4,3,64,128]{3,2,1,0:T(8,128)S(1)}, f32[4,3,64,128]{3,2,1,0:T(8,128)S(1)}, u32[]{:S(2)}, u32[]{:S(2)}) collective-permute-start(f32[4,3,64,128]{3,2,1,0:T(8,128)S(1)} %get-tuple-element.68), channel_id=1, source_target_pairs={{0,1},{1,0},{2,3},{3,2},{4,5},{5,4},{6,7},{7,6},{8,9},{9,8},{10,11... | collective-permute-start | bytes 1179656 | tf_op jit(solution)/shard_map/ppermute | solution.py:70
  24.3 16.1 %collective-permute-start.4 = (f32[14,72,128]{2,1,0:T(8,128)}, f32[14,72,128]{2,1,0:T(8,128)S(1)}, u32[]{:S(2)}, u32[]{:S(2)}) collective-permute-start(f32[14,72,128]{2,1,0:T(8,128)} %copy-done.25), channel_id=1, source_target_pairs={{1,2},{2,1},{5,6},{6,5},{9,10},{10,9},{13,14},{14,13},{17,18},{18,... | collective-permute-start | bytes 1548296 | tf_op jit(solution)/shard_map/ppermute | solution.py:70
  26.0 6.7 %collective-permute-start.2 = (f32[12,3,4,128]{3,2,1,0:T(4,128)S(1)}, f32[12,3,4,128]{3,2,1,0:T(4,128)S(1)}, u32[]{:S(2)}, u32[]{:S(2)}) collective-permute-start(f32[12,3,4,128]{3,2,1,0:T(4,128)S(1)} %corners.2), channel_id=1, source_target_pairs={{0,64},{1,65},{2,66},{3,67},{4,68},{5,69},{6,70},{7,71},{8,72},{9,... | collective-permute-start | bytes 221192 | tf_op jit(solution)/shard_map/ppermute | solution.py:70
  30.0 10.9 %collective-permute-start.7 = (f32[4,3,64,128]{3,2,1,0:T(8,128)S(1)}, f32[4,3,64,128]{3,2,1,0:T(8,128)S(1)}, u32[]{:S(2)}, u32[]{:S(2)}) collective-permute-start(f32[4,3,64,128]{3,2,1,0:T(8,128)S(1)} %get-tuple-element.79), channel_id=1, source_target_pairs={{1,2},{2,1},{5,6},{6,5},{9,10},{10,9},{13,14},{14,13},{17,18},{18,... | collective-permute-start | bytes 1179656 | tf_op jit(solution)/shard_map/ppermute | solution.py:70
  30.6 9.7 %collective-permute-start.6 = (f32[10,72,128]{2,1,0:T(8,128)}, f32[10,72,128]{2,1,0:T(8,128)S(1)}, u32[]{:S(2)}, u32[]{:S(2)}) collective-permute-start(f32[10,72,128]{2,1,0:T(8,128)} %copy-done.26), channel_id=1, source_target_pairs={{1,66},{2,65},{5,70},{6,69},{9,74},{10,73},{13,78},{14,77},{17,82}... | collective-permute-start | bytes 1105928 | tf_op jit(solution)/shard_map/ppermute | solution.py:70
  32.7 7.7 %collective-permute-start.5 = (f32[10,72,128]{2,1,0:T(8,128)S(1)}, f32[10,72,128]{2,1,0:T(8,128)S(1)}, u32[]{:S(2)}, u32[]{:S(2)}) collective-permute-start(f32[10,72,128]{2,1,0:T(8,128)S(1)} %lend.1), channel_id=1, source_target_pairs={{0,1},{1,0},{2,3},{3,2},{4,5},{5,4},{6,7},{7,6},{8,9},{9,8},{10,11... | collective-permute-start | bytes 1105928 | tf_op jit(solution)/shard_map/ppermute | solution.py:70
  39.1 1.8 %collective-permute-start.8 = (f32[4,3,4,128]{3,2,1,0:T(4,128)S(1)}, f32[4,3,4,128]{3,2,1,0:T(4,128)S(1)}, u32[]{:S(2)}, u32[]{:S(2)}) collective-permute-start(f32[4,3,4,128]{3,2,1,0:T(4,128)S(1)} %get-tuple-element.80), channel_id=1, source_target_pairs={{1,66},{2,65},{5,70},{6,69},{9,74},{10,73},{13,78},{14,77},{17,82}... | collective-permute-start | bytes 73736 | tf_op jit(solution)/shard_map/ppermute | solution.py:70
  46.7 5.5 %collective-permute-start.9 = (f32[3,8,128]{2,1,0:T(8,128)S(1)}, f32[3,8,128]{2,1,0:T(8,128)S(1)}, u32[]{:S(2)}, u32[]{:S(2)}) collective-permute-start(f32[3,8,128]{2,1,0:T(8,128)S(1)} %get-tuple-element.81), channel_id=1, source_target_pairs={{0,1},{1,0},{2,3},{3,2},{4,5},{5,4},{6,7},{7,6},{8,9},{9,8},{10,11... | collective-permute-start | bytes 36872 | tf_op jit(solution)/shard_map/ppermute | solution.py:70
  52.2 7.6 %collective-permute-start.13 = (f32[8,4,8,128]{3,2,1,0:T(8,128)S(1)}, f32[8,4,8,128]{3,2,1,0:T(8,128)S(1)}, u32[]{:S(2)}, u32[]{:S(2)}) collective-permute-start(f32[8,4,8,128]{3,2,1,0:T(8,128)S(1)} %edges.1), channel_id=1, source_target_pairs={{0,64},{1,65},{2,66},{3,67},{4,68},{5,69},{6,70},{7,71},{8,72},{9,... | collective-permute-start | bytes 393224 | tf_op jit(solution)/shard_map/ppermute | solution.py:70
  52.3 9.3 %collective-permute-start.10 = (f32[3,8,128]{2,1,0:T(8,128)S(1)}, f32[3,8,128]{2,1,0:T(8,128)S(1)}, u32[]{:S(2)}, u32[]{:S(2)}) collective-permute-start(f32[3,8,128]{2,1,0:T(8,128)S(1)} %add.6.n_ref), channel_id=1, source_target_pairs={{0,2},{1,3},{2,0},{3,1},{4,6},{5,7},{6,4},{7,5},{8,10},{9,11},{10,... | collective-permute-start | bytes 36872 | tf_op jit(solution)/shard_map/ppermute | solution.py:70
  54.8 6.8 %collective-permute-start.11 = (f32[3,8,128]{2,1,0:T(8,128)S(1)}, f32[3,8,128]{2,1,0:T(8,128)S(1)}, u32[]{:S(2)}, u32[]{:S(2)}) collective-permute-start(f32[3,8,128]{2,1,0:T(8,128)S(1)} %add.6.n_ref), channel_id=1, source_target_pairs={{0,64},{1,65},{2,66},{3,67},{4,68},{5,69},{6,70},{7,71},{8,72},{9,... | collective-permute-start | bytes 36872 | tf_op jit(solution)/shard_map/ppermute | solution.py:70
  56.2 5.5 %collective-permute-start.12 = (f32[3,8,128]{2,1,0:T(8,128)S(1)}, f32[3,8,128]{2,1,0:T(8,128)S(1)}, u32[]{:S(2)}, u32[]{:S(2)}) collective-permute-start(f32[3,8,128]{2,1,0:T(8,128)S(1)} %add.6.n_ref), channel_id=1, source_target_pairs={{0,66},{1,67},{2,64},{3,65},{4,70},{5,71},{6,68},{7,69},{8,74},{9,... | collective-permute-start | bytes 36872 | tf_op jit(solution)/shard_map/ppermute | solution.py:70
  60.9 0.7 copy-start.28
  61.6 0.8 copy-start.7
  61.6 1.0 copy-start.9
  61.6 1.1 copy-start.27
  61.6 10.8 %collective-permute-start.14 = (f32[20,72,128]{2,1,0:T(8,128)}, f32[20,72,128]{2,1,0:T(8,128)S(1)}, u32[]{:S(2)}, u32[]{:S(2)}) collective-permute-start(f32[20,72,128]{2,1,0:T(8,128)} %get-tuple-element.92), channel_id=1, source_target_pairs={{0,1},{1,0},{2,3},{3,2},{4,5},{5,4},{6,7},{7,6},{8,9},{9,8},{10,11... | collective-permute-start | bytes 2211848 | tf_op jit(solution)/shard_map/ppermute | solution.py:70
  62.4 0.9 copy-start.5
  63.3 20.6 %all-to-all-start.1 = ((f32[16,96,128]{2,1,0:T(8,128)}), f32[16,96,128]{2,1,0:T(8,128)}, u32[]{:S(2)}, u32[]{:S(2)}) async-start(f32[16,96,128]{2,1,0:T(8,128)} %bitcast.14), calls=%async_computation.1 | async-start | bytes 1572864 | tf_op jit(solution)/shard_map/all_to_all | solution.py:617
  69.3 2.4 %collective-permute-start.15 = (f32[10,72,128]{2,1,0:T(8,128)}, f32[10,72,128]{2,1,0:T(8,128)S(1)}, u32[]{:S(2)}, u32[]{:S(2)}) collective-permute-start(f32[10,72,128]{2,1,0:T(8,128)} %copy-done.28), channel_id=1, source_target_pairs={{1,2},{2,1},{5,6},{6,5},{9,10},{10,9},{13,14},{14,13},{17,18},{18,... | collective-permute-start | bytes 1105928 | tf_op jit(solution)/shard_map/ppermute | solution.py:70
  70.0 0.9 copy-start.21
  71.1 0.6 copy-start.12
  71.7 0.7 copy-start.14
  84.0 0.9 copy-start.13
  84.9 25.0 %copy-start.3 = (f32[8,72,128]{2,1,0:T(8,128)S(1)}, f32[8,72,128]{2,1,0:T(8,128)}, u32[]{:S(2)}) copy-start(f32[8,72,128]{2,1,0:T(8,128)} %copy-done.2) | copy-start | bytes 884740
  84.9 25.0 %copy-start.8 = (f32[8,2,72,128]{3,2,1,0:T(8,128)S(1)}, f32[8,2,72,128]{3,2,1,0:T(8,128)}, u32[]{:S(2)}) copy-start(f32[8,2,72,128]{3,2,1,0:T(8,128)} %copy-done.7) | copy-start | bytes 1769476
  86.2 0.9 copy-start.6
  87.1 26.3 %copy-start.22 = (f32[2,96,128]{2,1,0:T(8,128)}, f32[2,96,128]{2,1,0:T(8,128)S(1)}, u32[]{:S(2)}) copy-start(f32[2,96,128]{2,1,0:T(8,128)S(1)} %get-tuple-element.122.rows_ref) | copy-start | bytes 294916
  87.1 16.7 %all-to-all-start.2 = ((f32[16,96,128]{2,1,0:T(8,128)}), f32[16,96,128]{2,1,0:T(8,128)S(1)}, u32[]{:S(2)}, u32[]{:S(2)}) async-start(f32[16,96,128]{2,1,0:T(8,128)} %copy-done.6), calls=%async_computation.2 | async-start | bytes 1572864 | tf_op jit(solution)/shard_map/all_to_all | solution.py:617
  90.7 0.9 collective-permute-start.16
  91.6 0.7 copy-start.16
  103.9 1.8 %collective-permute-start.17 = (f32[4,3,64,128]{3,2,1,0:T(8,128)S(1)}, f32[4,3,64,128]{3,2,1,0:T(8,128)S(1)}, u32[]{:S(2)}, u32[]{:S(2)}) collective-permute-start(f32[4,3,64,128]{3,2,1,0:T(8,128)S(1)} %get-tuple-element.107), channel_id=1, source_target_pairs={{0,1},{1,0},{2,3},{3,2},{4,5},{5,4},{6,7},{7,6},{8,9},{9,8},{10,11... | collective-permute-start | bytes 1179656 | tf_op jit(solution)/shard_map/ppermute | solution.py:70
  104.0 9.4 %collective-permute-start.19 = (f32[4,3,64,128]{3,2,1,0:T(8,128)S(1)}, f32[4,3,64,128]{3,2,1,0:T(8,128)S(1)}, u32[]{:S(2)}, u32[]{:S(2)}) collective-permute-start(f32[4,3,64,128]{3,2,1,0:T(8,128)S(1)} %get-tuple-element.108), channel_id=1, source_target_pairs={{1,2},{2,1},{5,6},{6,5},{9,10},{10,9},{13,14},{14,13},{17,18},{18,... | collective-permute-start | bytes 1179656 | tf_op jit(solution)/shard_map/ppermute | solution.py:70
  105.7 7.7 %collective-permute-start.18 = (f32[12,3,4,128]{3,2,1,0:T(4,128)S(1)}, f32[12,3,4,128]{3,2,1,0:T(4,128)S(1)}, u32[]{:S(2)}, u32[]{:S(2)}) collective-permute-start(f32[12,3,4,128]{3,2,1,0:T(4,128)S(1)} %corners.3), channel_id=1, source_target_pairs={{0,64},{1,65},{2,66},{3,67},{4,68},{5,69},{6,70},{7,71},{8,72},{9,... | collective-permute-start | bytes 221192 | tf_op jit(solution)/shard_map/ppermute | solution.py:70
  109.2 4.1 %collective-permute-start.20 = (f32[4,3,4,128]{3,2,1,0:T(4,128)S(1)}, f32[4,3,4,128]{3,2,1,0:T(4,128)S(1)}, u32[]{:S(2)}, u32[]{:S(2)}) collective-permute-start(f32[4,3,4,128]{3,2,1,0:T(4,128)S(1)} %get-tuple-element.109), channel_id=1, source_target_pairs={{1,66},{2,65},{5,70},{6,69},{9,74},{10,73},{13,78},{14,77},{17,82}... | collective-permute-start | bytes 73736 | tf_op jit(solution)/shard_map/ppermute | solution.py:70
  109.9 1.1 copy-start.10
  111.0 1.0 copy-start.15
  112.0 1.0 copy-start.17
  119.2 11.9 %copy-start = (f32[16,3,72,128]{3,2,1,0:T(8,128)}, f32[16,3,72,128]{3,2,1,0:T(8,128)S(1)}, u32[]{:S(2)}) copy-start(f32[16,3,72,128]{3,2,1,0:T(8,128)S(1)} %get-tuple-element.113.field_ref) | copy-start | bytes 5308420
  119.2 4.3 %collective-permute-start.21 = (f32[3,8,128]{2,1,0:T(8,128)S(1)}, f32[3,8,128]{2,1,0:T(8,128)S(1)}, u32[]{:S(2)}, u32[]{:S(2)}) collective-permute-start(f32[3,8,128]{2,1,0:T(8,128)S(1)} %get-tuple-element.110), channel_id=1, source_target_pairs={{0,1},{1,0},{2,3},{3,2},{4,5},{5,4},{6,7},{7,6},{8,9},{9,8},{10,11... | collective-permute-start | bytes 36872 | tf_op jit(solution)/shard_map/ppermute | solution.py:70
  123.5 9.1 %collective-permute-start.25 = (f32[3,2,64,128]{3,2,1,0:T(8,128)S(1)}, f32[3,2,64,128]{3,2,1,0:T(8,128)S(1)}, u32[]{:S(2)}, u32[]{:S(2)}) collective-permute-start(f32[3,2,64,128]{3,2,1,0:T(8,128)S(1)} %get-tuple-element.115), channel_id=1, source_target_pairs={{0,64},{1,65},{2,66},{3,67},{4,68},{5,69},{6,70},{7,71},{8,72},{9,... | collective-permute-start | bytes 589832 | tf_op jit(solution)/shard_map/ppermute | solution.py:70
  125.4 7.2 %collective-permute-start.22 = (f32[3,8,128]{2,1,0:T(8,128)S(1)}, f32[3,8,128]{2,1,0:T(8,128)S(1)}, u32[]{:S(2)}, u32[]{:S(2)}) collective-permute-start(f32[3,8,128]{2,1,0:T(8,128)S(1)} %add.7.n_ref), channel_id=1, source_target_pairs={{0,2},{1,3},{2,0},{3,1},{4,6},{5,7},{6,4},{7,5},{8,10},{9,11},{10,... | collective-permute-start | bytes 36872 | tf_op jit(solution)/shard_map/ppermute | solution.py:70
  126.5 6.3 %collective-permute-start.23 = (f32[3,8,128]{2,1,0:T(8,128)S(1)}, f32[3,8,128]{2,1,0:T(8,128)S(1)}, u32[]{:S(2)}, u32[]{:S(2)}) collective-permute-start(f32[3,8,128]{2,1,0:T(8,128)S(1)} %add.7.n_ref), channel_id=1, source_target_pairs={{0,64},{1,65},{2,66},{3,67},{4,68},{5,69},{6,70},{7,71},{8,72},{9,... | collective-permute-start | bytes 36872 | tf_op jit(solution)/shard_map/ppermute | solution.py:70
  128.7 4.9 %collective-permute-start.24 = (f32[3,8,128]{2,1,0:T(8,128)S(1)}, f32[3,8,128]{2,1,0:T(8,128)S(1)}, u32[]{:S(2)}, u32[]{:S(2)}) collective-permute-start(f32[3,8,128]{2,1,0:T(8,128)S(1)} %add.7.n_ref), channel_id=1, source_target_pairs={{0,66},{1,67},{2,64},{3,65},{4,70},{5,71},{6,68},{7,69},{8,74},{9,... | collective-permute-start | bytes 36872 | tf_op jit(solution)/shard_map/ppermute | solution.py:70
  131.1 8.4 %copy-start.23 = (f32[2,96,128]{2,1,0:T(8,128)S(1)}, f32[2,96,128]{2,1,0:T(8,128)}, u32[]{:S(2)}) copy-start(f32[2,96,128]{2,1,0:T(8,128)} %copy-done.22) | copy-start | bytes 294916
  134.7 17.1 %all-to-all-start.3 = ((f32[16,96,128]{2,1,0:T(8,128)}), f32[16,96,128]{2,1,0:T(8,128)S(1)}, u32[]{:S(2)}, u32[]{:S(2)}) async-start(f32[16,96,128]{2,1,0:T(8,128)} %bitcast.8), calls=%async_computation.3 | async-start | bytes 1572864 | tf_op jit(solution)/shard_map/all_to_all | solution.py:617
  138.3 9.9 %collective-permute-start.26 = (f32[5,2,64,128]{3,2,1,0:T(8,128)S(1)}, f32[5,2,64,128]{3,2,1,0:T(8,128)S(1)}, u32[]{:S(2)}, u32[]{:S(2)}) collective-permute-start(f32[5,2,64,128]{3,2,1,0:T(8,128)S(1)} %get-tuple-element.120), channel_id=1, source_target_pairs={{0,64},{1,65},{2,66},{3,67},{4,68},{5,69},{6,70},{7,71},{8,72},{9,... | collective-permute-start | bytes 983048 | tf_op jit(solution)/shard_map/ppermute | solution.py:70
  139.4 1.5 copy-start.1

commit v6 on v5

--- a/solution.py
+++ b/solution.py
@@ -629,11 +629,10 @@
         field, edge, acore, achip, achipx = assemble(got)
         acore = send(acore, CORE)
         achip = send(achip, CHIP)
-        edge = corners(edge, acore)
-        edge = send(edge, HALVES)
+        edge = send(corners(edge, acore), HALVES)
+        achipx = send(achipx, CHIP_ACROSS)
         if step == 0:
-            edge, other = lax.optimization_barrier((edge, other))
-        achipx = send(achipx, CHIP_ACROSS)
+            edge, achipx, other = lax.optimization_barrier((edge, achipx, other))
         if step == 0:
             orbs = (own, other, vcore, vchip, send(lend(other), CORE), chipx)
         base, v = stage(2 * HALO * step, orbs, weight, vcore, vchip)
@@ -644,12 +643,13 @@
         if last:
             early, late = hand_back(late_wide)
             early = send(early, HALVES)
-            flow, early, late = lax.optimization_barrier((flow, early, late))
-            late = send(late, HALVES)
         else:
             edge = send(edges(late_wide), HALVES)
             flow, edge = lax.optimization_barrier((flow, edge))
         flow, scale = weigh(scale, norms, flow)
+        if last:
+            flow, early, late = lax.optimization_barrier((flow, early, late))
+            late = send(late, HALVES)
         flows = everyone(flow.reshape(GROUP, PACK, NY))
         part = double_curl(field, rows)
         if not last:

time: 153 us -> 154 us (level)
    all_to_all x4, starting transfers between devices: 20.3 us -> 18.6 us  [everyone(): lax.all_to_all(copies, 'orb', 0, 0, tiled=True, axis_index_groups=GROUPS)]
where the time goes in v6:
time: 154 us; the launch traced here: 153 us
  starting transfers between devices  64.3 us (42%)
  waiting for transfers between devices  51 us (33%)
  Pallas kernels  23 us (15%)
  local copies, waits for them, and re-layouts  13 us (8%)
  between operations  1.81 us (1%)
    ppermute x27, starting transfers between devices, send(): return lax.ppermute(value, ALL, table)  45.6 us
    all_to_all x4, waiting for transfers between devices, everyone(): lax.all_to_all(copies, 'orb', 0, 0, tiled=True, axis_index_groups=GROUPS)  34.2 us
    all_to_all x4, starting transfers between devices, everyone(): lax.all_to_all(copies, 'orb', 0, 0, tiled=True, axis_index_groups=GROUPS)  18.6 us
    ppermute x27, waiting for transfers between devices, send(): return lax.ppermute(value, ALL, table)  16.8 us
    unnamed x58, local copies, waits for them, and re-layouts  13 us
    pallas_call x2, Pallas kernels, propagate(): call('propagate', propagate_body, [(DEPTH + 2, 4, XL, NY), (3, 8, NY), (D...  11.6 us
  transfers between devices with their start and end apart: 31, of which 14 were waited for; matrix products, arithmetic and copies ran while one was open for 0% of the time, Pallas kernels for 5%

profile of v6, /device:TPU:0, one launch (start us, length us, event | category | flops | bytes accessed | tf_op | source)
XLA Modules:
  0.0 153.1 jit_solution(17210381435488934312)
XLA Ops:
  0.7 0.9 copy-done.18
  1.6 1.0 spread.1
  2.5 7.1 %all-to-all-start = ((f32[16,96,128]{2,1,0:T(8,128)}), f32[16,96,128]{2,1,0:T(8,128)S(1)}, u32[]{:S(2)}, u32[]{:S(2)}) async-start(f32[16,96,128]{2,1,0:T(8,128)} %spread.1), calls=%async_computation | async-start | bytes 1572864 | tf_op jit(solution)/shard_map/all_to_all | solution.py:617
  9.7 1.3 prepare.1
  11.0 0.6 copy-done.20
  11.7 4.0 %collective-permute-start.4 = (f32[8,2,72,128]{3,2,1,0:T(8,128)}, f32[8,2,72,128]{3,2,1,0:T(8,128)S(1)}, u32[]{:S(2)}, u32[]{:S(2)}) collective-permute-start(f32[8,2,72,128]{3,2,1,0:T(8,128)} %get-tuple-element.71), channel_id=1, source_target_pairs={{0,64},{1,65},{2,66},{3,67},{4,68},{5,69},{6,70},{7,71},{8,72},{9,... | collective-permute-start | bytes 1769480 | tf_op jit(solution)/shard_map/ppermute | solution.py:70
  15.7 8.4 %all-to-all-done = f32[16,96,128]{2,1,0:T(8,128)S(1)} async-done(((f32[16,96,128]{2,1,0:T(8,128)}), f32[16,96,128]{2,1,0:T(8,128)S(1)}, u32[]{:S(2)}, u32[]{:S(2)}) %all-to-all-start) | async-done | bytes 786464 | tf_op jit(solution)/shard_map/all_to_all | solution.py:617
  24.3 0.7 collective-permute-start.5
  25.0 1.0 collective-permute-done.1.core_ref.acore_ref
  26.0 4.0 %collective-permute-start.2 = (f32[12,3,4,128]{3,2,1,0:T(4,128)S(1)}, f32[12,3,4,128]{3,2,1,0:T(4,128)S(1)}, u32[]{:S(2)}, u32[]{:S(2)}) collective-permute-start(f32[12,3,4,128]{3,2,1,0:T(4,128)S(1)} %corners.2), channel_id=1, source_target_pairs={{0,64},{1,65},{2,66},{3,67},{4,68},{5,69},{6,70},{7,71},{8,72},{9,... | collective-permute-start | bytes 221192 | tf_op jit(solution)/shard_map/ppermute | solution.py:70
  30.0 0.7 collective-permute-start.3
  30.6 0.7 collective-permute-start.8
  31.3 0.7 collective-permute-start.7
  32.0 0.7 collective-permute-done.2.edge_ref
  32.7 7.8 %collective-permute-start.6 = (f32[10,72,128]{2,1,0:T(8,128)S(1)}, f32[10,72,128]{2,1,0:T(8,128)S(1)}, u32[]{:S(2)}, u32[]{:S(2)}) collective-permute-start(f32[10,72,128]{2,1,0:T(8,128)S(1)} %lend.1), channel_id=1, source_target_pairs={{0,1},{1,0},{2,3},{3,2},{4,5},{5,4},{6,7},{7,6},{8,9},{9,8},{10,11... | collective-permute-start | bytes 1105928 | tf_op jit(solution)/shard_map/ppermute | solution.py:70
  41.2 0.6 collective-permute-done.6.hcorex_ref
  42.2 5.8 %propagate.2 = (f32[10,4,88,128]{3,2,1,0:T(8,128)S(1)}, f32[3,8,128]{2,1,0:T(8,128)S(1)}, f32[16,3,72,128]{3,2,1,0:T(8,128)S(1)}) custom-call(f32[1]{0:T(128)S(6)} %copy.8.occ_ref, f32[18,4,88,128]{3,2,1,0:T(8,128)S(1)} %get-tuple-element.77.base_ref, f32[16,72,128]{2,1,0:T(8,128)S(1)} %get-tuple-element.78.v_ref, ...), custom_call_target="tpu_custom_call" | custom-call | flops 60000000 | bytes 7168000 | tf_op jit(solution)/shard_map/propagate/pallas_call | solution.py:419
  48.1 4.2 %collective-permute-start.9 = (f32[3,8,128]{2,1,0:T(8,128)S(1)}, f32[3,8,128]{2,1,0:T(8,128)S(1)}, u32[]{:S(2)}, u32[]{:S(2)}) collective-permute-start(f32[3,8,128]{2,1,0:T(8,128)S(1)} %get-tuple-element.83), channel_id=1, source_target_pairs={{0,1},{1,0},{2,3},{3,2},{4,5},{5,4},{6,7},{7,6},{8,9},{9,8},{10,11... | collective-permute-start | bytes 36872 | tf_op jit(solution)/shard_map/ppermute | solution.py:70
  52.2 0.8 collective-permute-done.9
  53.1 3.1 %collective-permute-start.13 = (f32[8,4,8,128]{3,2,1,0:T(8,128)S(1)}, f32[8,4,8,128]{3,2,1,0:T(8,128)S(1)}, u32[]{:S(2)}, u32[]{:S(2)}) collective-permute-start(f32[8,4,8,128]{3,2,1,0:T(8,128)S(1)} %edges.1), channel_id=1, source_target_pairs={{0,64},{1,65},{2,66},{3,67},{4,68},{5,69},{6,70},{7,71},{8,72},{9,... | collective-permute-start | bytes 393224 | tf_op jit(solution)/shard_map/ppermute | solution.py:70
  56.2 0.8 collective-permute-start.10
  57.1 1.5 collective-permute-start.11
  58.5 2.4 %collective-permute-start.12 = (f32[3,8,128]{2,1,0:T(8,128)S(1)}, f32[3,8,128]{2,1,0:T(8,128)S(1)}, u32[]{:S(2)}, u32[]{:S(2)}) collective-permute-start(f32[3,8,128]{2,1,0:T(8,128)S(1)} %add.6.n_ref), channel_id=1, source_target_pairs={{0,66},{1,67},{2,64},{3,65},{4,70},{5,71},{6,68},{7,69},{8,74},{9,... | collective-permute-start | bytes 36872 | tf_op jit(solution)/shard_map/ppermute | solution.py:70
  60.9 1.0 current.2.flow_ref
  61.9 1.0 rims.1
  62.9 0.7 copy-done.28
  65.4 4.3 %all-to-all-start.1 = ((f32[16,96,128]{2,1,0:T(8,128)}), f32[16,96,128]{2,1,0:T(8,128)}, u32[]{:S(2)}, u32[]{:S(2)}) async-start(f32[16,96,128]{2,1,0:T(8,128)} %bitcast.14), calls=%async_computation.1 | async-start | bytes 1572864 | tf_op jit(solution)/shard_map/all_to_all | solution.py:617
  69.7 0.7 collective-permute-start.15
  70.4 0.9 copy-done.21
  72.0 0.7 copy-done.14
  72.8 11.9 %all-to-all-done.1.got_ref = f32[16,96,128]{2,1,0:T(8,128)} async-done(((f32[16,96,128]{2,1,0:T(8,128)}), f32[16,96,128]{2,1,0:T(8,128)}, u32[]{:S(2)}, u32[]{:S(2)}) %all-to-all-start.1) | async-done | bytes 786464 | tf_op jit(solution)/shard_map/all_to_all | solution.py:617
  84.7 0.9 copy-done.13
  85.6 1.3 update.2
  86.9 0.9 copy-done.6
  87.8 3.6 %all-to-all-start.2 = ((f32[16,96,128]{2,1,0:T(8,128)}), f32[16,96,128]{2,1,0:T(8,128)S(1)}, u32[]{:S(2)}, u32[]{:S(2)}) async-start(f32[16,96,128]{2,1,0:T(8,128)} %copy-done.6), calls=%async_computation.2 | async-start | bytes 1572864 | tf_op jit(solution)/shard_map/all_to_all | solution.py:617
  91.4 0.9 collective-permute-start.16
  92.3 0.7 copy-done.16
  93.0 11.7 %all-to-all-done.2 = f32[16,96,128]{2,1,0:T(8,128)S(1)} async-done(((f32[16,96,128]{2,1,0:T(8,128)}), f32[16,96,128]{2,1,0:T(8,128)S(1)}, u32[]{:S(2)}, u32[]{:S(2)}) %all-to-all-start.2) | async-done | bytes 786464 | tf_op jit(solution)/shard_map/all_to_all | solution.py:617
  105.0 0.7 collective-permute-start.19
  105.7 1.0 collective-permute-done.17.core_ref.acore_ref
  106.7 1.9 %collective-permute-start.18 = (f32[12,3,4,128]{3,2,1,0:T(4,128)S(1)}, f32[12,3,4,128]{3,2,1,0:T(4,128)S(1)}, u32[]{:S(2)}, u32[]{:S(2)}) collective-permute-start(f32[12,3,4,128]{3,2,1,0:T(4,128)S(1)} %corners.3), channel_id=1, source_target_pairs={{0,64},{1,65},{2,66},{3,67},{4,68},{5,69},{6,70},{7,71},{8,72},{9,... | collective-permute-start | bytes 221192 | tf_op jit(solution)/shard_map/ppermute | solution.py:70
  108.7 0.7 collective-permute-start.20
  109.3 1.1 copy-done.10
  110.4 1.0 copy-done.15
  111.4 1.0 copy-done.17
  112.8 0.6 collective-permute-done.18.edge_ref
  113.4 5.8 %propagate.3 = (f32[10,4,88,128]{3,2,1,0:T(8,128)S(1)}, f32[3,8,128]{2,1,0:T(8,128)S(1)}, f32[16,3,72,128]{3,2,1,0:T(8,128)S(1)}) custom-call(f32[1]{0:T(128)S(6)} %copy.8.occ_ref, f32[18,4,88,128]{3,2,1,0:T(8,128)S(1)} %get-tuple-element.104.base_ref, f32[16,72,128]{2,1,0:T(8,128)S(1)} %get-tuple-element.105.v_ref, ...), custom_call_target="tpu_custom_call" | custom-call | flops 60000000 | bytes 7168000 | tf_op jit(solution)/shard_map/propagate/pallas_call | solution.py:419
  119.2 4.0 %collective-permute-start.21 = (f32[3,8,128]{2,1,0:T(8,128)S(1)}, f32[3,8,128]{2,1,0:T(8,128)S(1)}, u32[]{:S(2)}, u32[]{:S(2)}) collective-permute-start(f32[3,8,128]{2,1,0:T(8,128)S(1)} %get-tuple-element.112), channel_id=1, source_target_pairs={{0,1},{1,0},{2,3},{3,2},{4,5},{5,4},{6,7},{7,6},{8,9},{9,8},{10,11... | collective-permute-start | bytes 36872 | tf_op jit(solution)/shard_map/ppermute | solution.py:70
  123.2 0.8 collective-permute-done.21
  124.1 0.7 collective-permute-start.25
  124.9 2.0 %collective-permute-start.22 = (f32[3,8,128]{2,1,0:T(8,128)S(1)}, f32[3,8,128]{2,1,0:T(8,128)S(1)}, u32[]{:S(2)}, u32[]{:S(2)}) collective-permute-start(f32[3,8,128]{2,1,0:T(8,128)S(1)} %add.7.n_ref), channel_id=1, source_target_pairs={{0,2},{1,3},{2,0},{3,1},{4,6},{5,7},{6,4},{7,5},{8,10},{9,11},{10,... | collective-permute-start | bytes 36872 | tf_op jit(solution)/shard_map/ppermute | solution.py:70
  126.8 1.3 collective-permute-start.23
  128.1 1.4 collective-permute-start.24
  129.6 1.0 current.3.flow_ref
  130.5 1.6 %collective-permute-done.22.nchip_ref = f32[3,8,128]{2,1,0:T(8,128)S(1)} collective-permute-done((f32[3,8,128]{2,1,0:T(8,128)S(1)}, f32[3,8,128]{2,1,0:T(8,128)S(1)}, u32[]{:S(2)}, u32[]{:S(2)}) %collective-permute-start.22) | collective-permute-done | bytes 12320 | tf_op jit(solution)/shard_map/ppermute | solution.py:70
  132.2 1.2 collective-permute-done.23.nhalf_ref
  133.4 1.1 weigh.3
  134.5 3.6 %all-to-all-start.3 = ((f32[16,96,128]{2,1,0:T(8,128)}), f32[16,96,128]{2,1,0:T(8,128)S(1)}, u32[]{:S(2)}, u32[]{:S(2)}) async-start(f32[16,96,128]{2,1,0:T(8,128)} %bitcast.8), calls=%async_computation.3 | async-start | bytes 1572864 | tf_op jit(solution)/shard_map/all_to_all | solution.py:617
  138.2 0.8 collective-permute-start.26
  139.0 1.5 copy-done.1
  140.6 8.3 %collective-permute-done.26.late_ref = f32[5,2,64,128]{3,2,1,0:T(8,128)S(1)} collective-permute-done((f32[5,2,64,128]{3,2,1,0:T(8,128)S(1)}, f32[5,2,64,128]{3,2,1,0:T(8,128)S(1)}, u32[]{:S(2)}, u32[]{:S(2)}) %collective-permute-start.26) | collective-permute-done | bytes 327712 | tf_op jit(solution)/shard_map/ppermute | solution.py:70
  148.9 1.3 finish.1
  150.2 2.2 %all-to-all-done.3.got_ref = f32[16,96,128]{2,1,0:T(8,128)S(1)} async-done(((f32[16,96,128]{2,1,0:T(8,128)}), f32[16,96,128]{2,1,0:T(8,128)S(1)}, u32[]{:S(2)}, u32[]{:S(2)}) %all-to-all-start.3) | async-done | bytes 786464 | tf_op jit(solution)/shard_map/all_to_all | solution.py:617
  152.4 0.7 update.3
  (82 shorter events, 4.1 us)
Async XLA Ops:
  0.6 9.0 %copy-start.4 = (f32[1,2,128,8,128]{4,3,2,1,0:T(8,128)S(1)}, f32[1,2,128,8,128]{4,3,2,1,0:T(8,128)}, u32[]{:S(2)}) copy-start(f32[1,2,128,8,128]{4,3,2,1,0:T(8,128)} %param.5) | copy-start | bytes 3145732
  0.6 9.0 %copy-start.11 = (f32[128,8,128]{2,1,0:T(8,128)S(1)}, f32[128,8,128]{2,1,0:T(8,128)}, u32[]{:S(2)}) copy-start(f32[128,8,128]{2,1,0:T(8,128)} %param.6) | copy-start | bytes 1572868
  0.7 0.9 copy-start.18
  1.6 8.1 %copy-start.19 = (f32[3,4,8,128]{3,2,1,0:T(8,128)S(1)}, f32[3,4,8,128]{3,2,1,0:T(8,128)}, u32[]{:S(2)}) copy-start(f32[3,4,8,128]{3,2,1,0:T(8,128)} %param.9) | copy-start | bytes 147460
  1.6 8.1 %copy-start.24 = (f32[3,4,8,128]{3,2,1,0:T(8,128)S(1)}, f32[3,4,8,128]{3,2,1,0:T(8,128)}, u32[]{:S(2)}) copy-start(f32[3,4,8,128]{3,2,1,0:T(8,128)} %param.8) | copy-start | bytes 147460
  2.5 21.5 %all-to-all-start = ((f32[16,96,128]{2,1,0:T(8,128)}), f32[16,96,128]{2,1,0:T(8,128)S(1)}, u32[]{:S(2)}, u32[]{:S(2)}) async-start(f32[16,96,128]{2,1,0:T(8,128)} %spread.1), calls=%async_computation | async-start | bytes 1572864 | tf_op jit(solution)/shard_map/all_to_all | solution.py:617
  11.0 0.6 copy-start.20
  11.7 4.0 %copy-start.25 = (f32[14,72,128]{2,1,0:T(8,128)}, f32[14,72,128]{2,1,0:T(8,128)S(1)}, u32[]{:S(2)}) copy-start(f32[14,72,128]{2,1,0:T(8,128)S(1)} %get-tuple-element.74) | copy-start | bytes 1548292
  11.7 4.0 %copy-start.26 = (f32[10,72,128]{2,1,0:T(8,128)}, f32[10,72,128]{2,1,0:T(8,128)S(1)}, u32[]{:S(2)}) copy-start(f32[10,72,128]{2,1,0:T(8,128)S(1)} %get-tuple-element.75) | copy-start | bytes 1105924
  11.7 30.5 %copy-start.2 = (f32[8,72,128]{2,1,0:T(8,128)}, f32[8,72,128]{2,1,0:T(8,128)S(1)}, u32[]{:S(2)}) copy-start(f32[8,72,128]{2,1,0:T(8,128)S(1)} %get-tuple-element.76.weight_ref) | copy-start | bytes 884740
  11.7 4.0 %collective-permute-start = (f32[14,72,128]{2,1,0:T(8,128)S(1)}, f32[14,72,128]{2,1,0:T(8,128)S(1)}, u32[]{:S(2)}, u32[]{:S(2)}) collective-permute-start(f32[14,72,128]{2,1,0:T(8,128)S(1)} %get-tuple-element.66), channel_id=1, source_target_pairs={{0,1},{1,0},{2,3},{3,2},{4,5},{5,4},{6,7},{7,6},{8,9},{9,8},{10,11... | collective-permute-start | bytes 1548296 | tf_op jit(solution)/shard_map/ppermute | solution.py:70
  11.7 19.6 %collective-permute-start.4 = (f32[8,2,72,128]{3,2,1,0:T(8,128)}, f32[8,2,72,128]{3,2,1,0:T(8,128)S(1)}, u32[]{:S(2)}, u32[]{:S(2)}) collective-permute-start(f32[8,2,72,128]{3,2,1,0:T(8,128)} %get-tuple-element.71), channel_id=1, source_target_pairs={{0,64},{1,65},{2,66},{3,67},{4,68},{5,69},{6,70},{7,71},{8,72},{9,... | collective-permute-start | bytes 1769480 | tf_op jit(solution)/shard_map/ppermute | solution.py:70
  24.2 1.8 %collective-permute-start.1 = (f32[4,3,64,128]{3,2,1,0:T(8,128)S(1)}, f32[4,3,64,128]{3,2,1,0:T(8,128)S(1)}, u32[]{:S(2)}, u32[]{:S(2)}) collective-permute-start(f32[4,3,64,128]{3,2,1,0:T(8,128)S(1)} %get-tuple-element.69), channel_id=1, source_target_pairs={{0,1},{1,0},{2,3},{3,2},{4,5},{5,4},{6,7},{7,6},{8,9},{9,8},{10,11... | collective-permute-start | bytes 1179656 | tf_op jit(solution)/shard_map/ppermute | solution.py:70
  24.3 16.9 %collective-permute-start.5 = (f32[14,72,128]{2,1,0:T(8,128)}, f32[14,72,128]{2,1,0:T(8,128)S(1)}, u32[]{:S(2)}, u32[]{:S(2)}) collective-permute-start(f32[14,72,128]{2,1,0:T(8,128)} %copy-done.25), channel_id=1, source_target_pairs={{1,2},{2,1},{5,6},{6,5},{9,10},{10,9},{13,14},{14,13},{17,18},{18,... | collective-permute-start | bytes 1548296 | tf_op jit(solution)/shard_map/ppermute | solution.py:70
  26.0 6.7 %collective-permute-start.2 = (f32[12,3,4,128]{3,2,1,0:T(4,128)S(1)}, f32[12,3,4,128]{3,2,1,0:T(4,128)S(1)}, u32[]{:S(2)}, u32[]{:S(2)}) collective-permute-start(f32[12,3,4,128]{3,2,1,0:T(4,128)S(1)} %corners.2), channel_id=1, source_target_pairs={{0,64},{1,65},{2,66},{3,67},{4,68},{5,69},{6,70},{7,71},{8,72},{9,... | collective-permute-start | bytes 221192 | tf_op jit(solution)/shard_map/ppermute | solution.py:70
  30.0 2.1 %collective-permute-start.3 = (f32[4,3,4,128]{3,2,1,0:T(4,128)S(1)}, f32[4,3,4,128]{3,2,1,0:T(4,128)S(1)}, u32[]{:S(2)}, u32[]{:S(2)}) collective-permute-start(f32[4,3,4,128]{3,2,1,0:T(4,128)S(1)} %get-tuple-element.70), channel_id=1, source_target_pairs={{1,66},{2,65},{5,70},{6,69},{9,74},{10,73},{13,78},{14,77},{17,82}... | collective-permute-start | bytes 73736 | tf_op jit(solution)/shard_map/ppermute | solution.py:70
  30.6 11.6 %collective-permute-start.8 = (f32[4,3,64,128]{3,2,1,0:T(8,128)S(1)}, f32[4,3,64,128]{3,2,1,0:T(8,128)S(1)}, u32[]{:S(2)}, u32[]{:S(2)}) collective-permute-start(f32[4,3,64,128]{3,2,1,0:T(8,128)S(1)} %get-tuple-element.81), channel_id=1, source_target_pairs={{1,2},{2,1},{5,6},{6,5},{9,10},{10,9},{13,14},{14,13},{17,18},{18,... | collective-permute-start | bytes 1179656 | tf_op jit(solution)/shard_map/ppermute | solution.py:70
  31.3 9.8 %collective-permute-start.7 = (f32[10,72,128]{2,1,0:T(8,128)}, f32[10,72,128]{2,1,0:T(8,128)S(1)}, u32[]{:S(2)}, u32[]{:S(2)}) collective-permute-start(f32[10,72,128]{2,1,0:T(8,128)} %copy-done.26), channel_id=1, source_target_pairs={{1,66},{2,65},{5,70},{6,69},{9,74},{10,73},{13,78},{14,77},{17,82}... | collective-permute-start | bytes 1105928 | tf_op jit(solution)/shard_map/ppermute | solution.py:70
  32.7 9.1 %collective-permute-start.6 = (f32[10,72,128]{2,1,0:T(8,128)S(1)}, f32[10,72,128]{2,1,0:T(8,128)S(1)}, u32[]{:S(2)}, u32[]{:S(2)}) collective-permute-start(f32[10,72,128]{2,1,0:T(8,128)S(1)} %lend.1), channel_id=1, source_target_pairs={{0,1},{1,0},{2,3},{3,2},{4,5},{5,4},{6,7},{7,6},{8,9},{9,8},{10,11... | collective-permute-start | bytes 1105928 | tf_op jit(solution)/shard_map/ppermute | solution.py:70
  48.1 5.0 %collective-permute-start.9 = (f32[3,8,128]{2,1,0:T(8,128)S(1)}, f32[3,8,128]{2,1,0:T(8,128)S(1)}, u32[]{:S(2)}, u32[]{:S(2)}) collective-permute-start(f32[3,8,128]{2,1,0:T(8,128)S(1)} %get-tuple-element.83), channel_id=1, source_target_pairs={{0,1},{1,0},{2,3},{3,2},{4,5},{5,4},{6,7},{7,6},{8,9},{9,8},{10,11... | collective-permute-start | bytes 36872 | tf_op jit(solution)/shard_map/ppermute | solution.py:70
  53.1 8.8 %collective-permute-start.13 = (f32[8,4,8,128]{3,2,1,0:T(8,128)S(1)}, f32[8,4,8,128]{3,2,1,0:T(8,128)S(1)}, u32[]{:S(2)}, u32[]{:S(2)}) collective-permute-start(f32[8,4,8,128]{3,2,1,0:T(8,128)S(1)} %edges.1), channel_id=1, source_target_pairs={{0,64},{1,65},{2,66},{3,67},{4,68},{5,69},{6,70},{7,71},{8,72},{9,... | collective-permute-start | bytes 393224 | tf_op jit(solution)/shard_map/ppermute | solution.py:70
  56.2 7.5 %collective-permute-start.10 = (f32[3,8,128]{2,1,0:T(8,128)S(1)}, f32[3,8,128]{2,1,0:T(8,128)S(1)}, u32[]{:S(2)}, u32[]{:S(2)}) collective-permute-start(f32[3,8,128]{2,1,0:T(8,128)S(1)} %add.6.n_ref), channel_id=1, source_target_pairs={{0,2},{1,3},{2,0},{3,1},{4,6},{5,7},{6,4},{7,5},{8,10},{9,11},{10,... | collective-permute-start | bytes 36872 | tf_op jit(solution)/shard_map/ppermute | solution.py:70
  57.1 6.6 %collective-permute-start.11 = (f32[3,8,128]{2,1,0:T(8,128)S(1)}, f32[3,8,128]{2,1,0:T(8,128)S(1)}, u32[]{:S(2)}, u32[]{:S(2)}) collective-permute-start(f32[3,8,128]{2,1,0:T(8,128)S(1)} %add.6.n_ref), channel_id=1, source_target_pairs={{0,64},{1,65},{2,66},{3,67},{4,68},{5,69},{6,70},{7,71},{8,72},{9,... | collective-permute-start | bytes 36872 | tf_op jit(solution)/shard_map/ppermute | solution.py:70
  58.5 5.2 %collective-permute-start.12 = (f32[3,8,128]{2,1,0:T(8,128)S(1)}, f32[3,8,128]{2,1,0:T(8,128)S(1)}, u32[]{:S(2)}, u32[]{:S(2)}) collective-permute-start(f32[3,8,128]{2,1,0:T(8,128)S(1)} %add.6.n_ref), channel_id=1, source_target_pairs={{0,66},{1,67},{2,64},{3,65},{4,70},{5,71},{6,68},{7,69},{8,74},{9,... | collective-permute-start | bytes 36872 | tf_op jit(solution)/shard_map/ppermute | solution.py:70
  62.9 0.7 copy-start.28
  63.7 0.8 copy-start.7
  63.7 1.0 copy-start.9
  63.7 1.1 copy-start.27
  63.7 9.1 %collective-permute-start.14 = (f32[20,72,128]{2,1,0:T(8,128)}, f32[20,72,128]{2,1,0:T(8,128)S(1)}, u32[]{:S(2)}, u32[]{:S(2)}) collective-permute-start(f32[20,72,128]{2,1,0:T(8,128)} %get-tuple-element.94), channel_id=1, source_target_pairs={{0,1},{1,0},{2,3},{3,2},{4,5},{5,4},{6,7},{7,6},{8,9},{9,8},{10,11... | collective-permute-start | bytes 2211848 | tf_op jit(solution)/shard_map/ppermute | solution.py:70
  64.5 0.9 copy-start.5
  65.4 19.3 %all-to-all-start.1 = ((f32[16,96,128]{2,1,0:T(8,128)}), f32[16,96,128]{2,1,0:T(8,128)}, u32[]{:S(2)}, u32[]{:S(2)}) async-start(f32[16,96,128]{2,1,0:T(8,128)} %bitcast.14), calls=%async_computation.1 | async-start | bytes 1572864 | tf_op jit(solution)/shard_map/all_to_all | solution.py:617
  69.7 2.4 %collective-permute-start.15 = (f32[10,72,128]{2,1,0:T(8,128)}, f32[10,72,128]{2,1,0:T(8,128)S(1)}, u32[]{:S(2)}, u32[]{:S(2)}) collective-permute-start(f32[10,72,128]{2,1,0:T(8,128)} %copy-done.28), channel_id=1, source_target_pairs={{1,2},{2,1},{5,6},{6,5},{9,10},{10,9},{13,14},{14,13},{17,18},{18,... | collective-permute-start | bytes 1105928 | tf_op jit(solution)/shard_map/ppermute | solution.py:70
  70.4 0.9 copy-start.21
  71.4 0.6 copy-start.12
  72.0 0.7 copy-start.14
  84.7 0.9 copy-start.13
  85.6 23.7 %copy-start.3 = (f32[8,72,128]{2,1,0:T(8,128)S(1)}, f32[8,72,128]{2,1,0:T(8,128)}, u32[]{:S(2)}) copy-start(f32[8,72,128]{2,1,0:T(8,128)} %copy-done.2) | copy-start | bytes 884740
  85.6 23.7 %copy-start.8 = (f32[8,2,72,128]{3,2,1,0:T(8,128)S(1)}, f32[8,2,72,128]{3,2,1,0:T(8,128)}, u32[]{:S(2)}) copy-start(f32[8,2,72,128]{3,2,1,0:T(8,128)} %copy-done.7) | copy-start | bytes 1769476
  86.9 0.9 copy-start.6
  87.8 25.0 %copy-start.22 = (f32[2,96,128]{2,1,0:T(8,128)}, f32[2,96,128]{2,1,0:T(8,128)S(1)}, u32[]{:S(2)}) copy-start(f32[2,96,128]{2,1,0:T(8,128)S(1)} %get-tuple-element.124.rows_ref) | copy-start | bytes 294916
  87.8 17.0 %all-to-all-start.2 = ((f32[16,96,128]{2,1,0:T(8,128)}), f32[16,96,128]{2,1,0:T(8,128)S(1)}, u32[]{:S(2)}, u32[]{:S(2)}) async-start(f32[16,96,128]{2,1,0:T(8,128)} %copy-done.6), calls=%async_computation.2 | async-start | bytes 1572864 | tf_op jit(solution)/shard_map/all_to_all | solution.py:617
  91.4 0.9 collective-permute-start.16
  92.3 0.7 copy-start.16
  104.9 1.8 %collective-permute-start.17 = (f32[4,3,64,128]{3,2,1,0:T(8,128)S(1)}, f32[4,3,64,128]{3,2,1,0:T(8,128)S(1)}, u32[]{:S(2)}, u32[]{:S(2)}) collective-permute-start(f32[4,3,64,128]{3,2,1,0:T(8,128)S(1)} %get-tuple-element.109), channel_id=1, source_target_pairs={{0,1},{1,0},{2,3},{3,2},{4,5},{5,4},{6,7},{7,6},{8,9},{9,8},{10,11... | collective-permute-start | bytes 1179656 | tf_op jit(solution)/shard_map/ppermute | solution.py:70
  105.0 7.8 %collective-permute-start.19 = (f32[4,3,64,128]{3,2,1,0:T(8,128)S(1)}, f32[4,3,64,128]{3,2,1,0:T(8,128)S(1)}, u32[]{:S(2)}, u32[]{:S(2)}) collective-permute-start(f32[4,3,64,128]{3,2,1,0:T(8,128)S(1)} %get-tuple-element.110), channel_id=1, source_target_pairs={{1,2},{2,1},{5,6},{6,5},{9,10},{10,9},{13,14},{14,13},{17,18},{18,... | collective-permute-start | bytes 1179656 | tf_op jit(solution)/shard_map/ppermute | solution.py:70
  106.7 6.7 %collective-permute-start.18 = (f32[12,3,4,128]{3,2,1,0:T(4,128)S(1)}, f32[12,3,4,128]{3,2,1,0:T(4,128)S(1)}, u32[]{:S(2)}, u32[]{:S(2)}) collective-permute-start(f32[12,3,4,128]{3,2,1,0:T(4,128)S(1)} %corners.3), channel_id=1, source_target_pairs={{0,64},{1,65},{2,66},{3,67},{4,68},{5,69},{6,70},{7,71},{8,72},{9,... | collective-permute-start | bytes 221192 | tf_op jit(solution)/shard_map/ppermute | solution.py:70
  108.7 4.1 %collective-permute-start.20 = (f32[4,3,4,128]{3,2,1,0:T(4,128)S(1)}, f32[4,3,4,128]{3,2,1,0:T(4,128)S(1)}, u32[]{:S(2)}, u32[]{:S(2)}) collective-permute-start(f32[4,3,4,128]{3,2,1,0:T(4,128)S(1)} %get-tuple-element.111), channel_id=1, source_target_pairs={{1,66},{2,65},{5,70},{6,69},{9,74},{10,73},{13,78},{14,77},{17,82}... | collective-permute-start | bytes 73736 | tf_op jit(solution)/shard_map/ppermute | solution.py:70
  109.3 1.1 copy-start.10
  110.4 1.0 copy-start.15
  111.4 1.0 copy-start.17
  119.2 11.3 %copy-start = (f32[16,3,72,128]{3,2,1,0:T(8,128)}, f32[16,3,72,128]{3,2,1,0:T(8,128)S(1)}, u32[]{:S(2)}) copy-start(f32[16,3,72,128]{3,2,1,0:T(8,128)S(1)} %get-tuple-element.115.field_ref) | copy-start | bytes 5308420
  119.2 4.8 %collective-permute-start.21 = (f32[3,8,128]{2,1,0:T(8,128)S(1)}, f32[3,8,128]{2,1,0:T(8,128)S(1)}, u32[]{:S(2)}, u32[]{:S(2)}) collective-permute-start(f32[3,8,128]{2,1,0:T(8,128)S(1)} %get-tuple-element.112), channel_id=1, source_target_pairs={{0,1},{1,0},{2,3},{3,2},{4,5},{5,4},{6,7},{7,6},{8,9},{9,8},{10,11... | collective-permute-start | bytes 36872 | tf_op jit(solution)/shard_map/ppermute | solution.py:70
  124.1 10.4 %collective-permute-start.25 = (f32[3,2,64,128]{3,2,1,0:T(8,128)S(1)}, f32[3,2,64,128]{3,2,1,0:T(8,128)S(1)}, u32[]{:S(2)}, u32[]{:S(2)}) collective-permute-start(f32[3,2,64,128]{3,2,1,0:T(8,128)S(1)} %get-tuple-element.119), channel_id=1, source_target_pairs={{0,64},{1,65},{2,66},{3,67},{4,68},{5,69},{6,70},{7,71},{8,72},{9,... | collective-permute-start | bytes 589832 | tf_op jit(solution)/shard_map/ppermute | solution.py:70
  124.9 7.3 %collective-permute-start.22 = (f32[3,8,128]{2,1,0:T(8,128)S(1)}, f32[3,8,128]{2,1,0:T(8,128)S(1)}, u32[]{:S(2)}, u32[]{:S(2)}) collective-permute-start(f32[3,8,128]{2,1,0:T(8,128)S(1)} %add.7.n_ref), channel_id=1, source_target_pairs={{0,2},{1,3},{2,0},{3,1},{4,6},{5,7},{6,4},{7,5},{8,10},{9,11},{10,... | collective-permute-start | bytes 36872 | tf_op jit(solution)/shard_map/ppermute | solution.py:70
  126.8 6.6 %collective-permute-start.23 = (f32[3,8,128]{2,1,0:T(8,128)S(1)}, f32[3,8,128]{2,1,0:T(8,128)S(1)}, u32[]{:S(2)}, u32[]{:S(2)}) collective-permute-start(f32[3,8,128]{2,1,0:T(8,128)S(1)} %add.7.n_ref), channel_id=1, source_target_pairs={{0,64},{1,65},{2,66},{3,67},{4,68},{5,69},{6,70},{7,71},{8,72},{9,... | collective-permute-start | bytes 36872 | tf_op jit(solution)/shard_map/ppermute | solution.py:70
  128.1 5.3 %collective-permute-start.24 = (f32[3,8,128]{2,1,0:T(8,128)S(1)}, f32[3,8,128]{2,1,0:T(8,128)S(1)}, u32[]{:S(2)}, u32[]{:S(2)}) collective-permute-start(f32[3,8,128]{2,1,0:T(8,128)S(1)} %add.7.n_ref), channel_id=1, source_target_pairs={{0,66},{1,67},{2,64},{3,65},{4,70},{5,71},{6,68},{7,69},{8,74},{9,... | collective-permute-start | bytes 36872 | tf_op jit(solution)/shard_map/ppermute | solution.py:70
  130.5 8.5 %copy-start.23 = (f32[2,96,128]{2,1,0:T(8,128)S(1)}, f32[2,96,128]{2,1,0:T(8,128)}, u32[]{:S(2)}) copy-start(f32[2,96,128]{2,1,0:T(8,128)} %copy-done.22) | copy-start | bytes 294916
  134.5 17.9 %all-to-all-start.3 = ((f32[16,96,128]{2,1,0:T(8,128)}), f32[16,96,128]{2,1,0:T(8,128)S(1)}, u32[]{:S(2)}, u32[]{:S(2)}) async-start(f32[16,96,128]{2,1,0:T(8,128)} %bitcast.8), calls=%async_computation.3 | async-start | bytes 1572864 | tf_op jit(solution)/shard_map/all_to_all | solution.py:617
  138.2 10.7 %collective-permute-start.26 = (f32[5,2,64,128]{3,2,1,0:T(8,128)S(1)}, f32[5,2,64,128]{3,2,1,0:T(8,128)S(1)}, u32[]{:S(2)}, u32[]{:S(2)}) collective-permute-start(f32[5,2,64,128]{3,2,1,0:T(8,128)S(1)} %get-tuple-element.122), channel_id=1, source_target_pairs={{0,64},{1,65},{2,66},{3,67},{4,68},{5,69},{6,70},{7,71},{8,72},{9,... | collective-permute-start | bytes 983048 | tf_op jit(solution)/shard_map/ppermute | solution.py:70
  139.0 1.5 copy-start.1

commit v7 on v5

--- a/solution.py
+++ b/solution.py
@@ -644,12 +644,13 @@
         if last:
             early, late = hand_back(late_wide)
             early = send(early, HALVES)
-            flow, early, late = lax.optimization_barrier((flow, early, late))
-            late = send(late, HALVES)
         else:
             edge = send(edges(late_wide), HALVES)
             flow, edge = lax.optimization_barrier((flow, edge))
         flow, scale = weigh(scale, norms, flow)
+        if last:
+            flow, early, late = lax.optimization_barrier((flow, early, late))
+            late = send(late, HALVES)
         flows = everyone(flow.reshape(GROUP, PACK, NY))
         part = double_curl(field, rows)
         if not last:

time: 153 us -> 153 us (level)
  no operation moved by 1% of the time
where the time goes in v7:
time: 153 us; the launch traced here: 152 us
  starting transfers between devices  65 us (42%)
  waiting for transfers between devices  49.6 us (32%)
  Pallas kernels  23.1 us (15%)
  local copies, waits for them, and re-layouts  13 us (8%)
  between operations  1.82 us (1%)
    ppermute x27, starting transfers between devices, send(): return lax.ppermute(value, ALL, table)  44.6 us
    all_to_all x4, waiting for transfers between devices, everyone(): lax.all_to_all(copies, 'orb', 0, 0, tiled=True, axis_index_groups=GROUPS)  33.5 us
    all_to_all x4, starting transfers between devices, everyone(): lax.all_to_all(copies, 'orb', 0, 0, tiled=True, axis_index_groups=GROUPS)  20.3 us
    ppermute x27, waiting for transfers between devices, send(): return lax.ppermute(value, ALL, table)  16.1 us
    unnamed x58, local copies, waits for them, and re-layouts  13 us
    pallas_call x2, Pallas kernels, propagate(): call('propagate', propagate_body, [(DEPTH + 2, 4, XL, NY), (3, 8, NY), (D...  11.6 us
  transfers between devices with their start and end apart: 31, of which 14 were waited for; matrix products, arithmetic and copies ran while one was open for 0% of the time, Pallas kernels for 5%

profile of v7, /device:TPU:0, one launch (start us, length us, event | category | flops | bytes accessed | tf_op | source)
XLA Modules:
  0.0 152.5 jit_solution(7437200270071223595)
XLA Ops:
  0.7 0.9 copy-done.18
  1.6 1.0 spread.1
  2.5 7.1 %all-to-all-start = ((f32[16,96,128]{2,1,0:T(8,128)}), f32[16,96,128]{2,1,0:T(8,128)S(1)}, u32[]{:S(2)}, u32[]{:S(2)}) async-start(f32[16,96,128]{2,1,0:T(8,128)} %spread.1), calls=%async_computation | async-start | bytes 1572864 | tf_op jit(solution)/shard_map/all_to_all | solution.py:617
  9.7 1.3 prepare.1
  11.0 0.6 copy-done.20
  11.7 4.0 %collective-permute-start.3 = (f32[8,2,72,128]{3,2,1,0:T(8,128)}, f32[8,2,72,128]{3,2,1,0:T(8,128)S(1)}, u32[]{:S(2)}, u32[]{:S(2)}) collective-permute-start(f32[8,2,72,128]{3,2,1,0:T(8,128)} %get-tuple-element.69), channel_id=1, source_target_pairs={{0,64},{1,65},{2,66},{3,67},{4,68},{5,69},{6,70},{7,71},{8,72},{9,... | collective-permute-start | bytes 1769480 | tf_op jit(solution)/shard_map/ppermute | solution.py:70
  15.7 8.4 %all-to-all-done = f32[16,96,128]{2,1,0:T(8,128)S(1)} async-done(((f32[16,96,128]{2,1,0:T(8,128)}), f32[16,96,128]{2,1,0:T(8,128)S(1)}, u32[]{:S(2)}, u32[]{:S(2)}) %all-to-all-start) | async-done | bytes 786464 | tf_op jit(solution)/shard_map/all_to_all | solution.py:617
  24.3 0.7 collective-permute-start.4
  25.0 1.0 collective-permute-done.1.core_ref.acore_ref
  26.0 4.0 %collective-permute-start.2 = (f32[12,3,4,128]{3,2,1,0:T(4,128)S(1)}, f32[12,3,4,128]{3,2,1,0:T(4,128)S(1)}, u32[]{:S(2)}, u32[]{:S(2)}) collective-permute-start(f32[12,3,4,128]{3,2,1,0:T(4,128)S(1)} %corners.2), channel_id=1, source_target_pairs={{0,64},{1,65},{2,66},{3,67},{4,68},{5,69},{6,70},{7,71},{8,72},{9,... | collective-permute-start | bytes 221192 | tf_op jit(solution)/shard_map/ppermute | solution.py:70
  30.0 0.7 collective-permute-start.7
  30.6 0.7 collective-permute-start.6
  31.3 1.3 collective-permute-done.2.edge_ref
  32.7 6.4 %collective-permute-start.5 = (f32[10,72,128]{2,1,0:T(8,128)S(1)}, f32[10,72,128]{2,1,0:T(8,128)S(1)}, u32[]{:S(2)}, u32[]{:S(2)}) collective-permute-start(f32[10,72,128]{2,1,0:T(8,128)S(1)} %lend.1), channel_id=1, source_target_pairs={{0,1},{1,0},{2,3},{3,2},{4,5},{5,4},{6,7},{7,6},{8,9},{9,8},{10,11... | collective-permute-start | bytes 1105928 | tf_op jit(solution)/shard_map/ppermute | solution.py:70
  39.1 0.7 collective-permute-start.8
  40.9 5.8 %propagate.2 = (f32[10,4,88,128]{3,2,1,0:T(8,128)S(1)}, f32[3,8,128]{2,1,0:T(8,128)S(1)}, f32[16,3,72,128]{3,2,1,0:T(8,128)S(1)}) custom-call(f32[1]{0:T(128)S(6)} %copy.8.occ_ref, f32[18,4,88,128]{3,2,1,0:T(8,128)S(1)} %get-tuple-element.75.base_ref, f32[16,72,128]{2,1,0:T(8,128)S(1)} %get-tuple-element.76.v_ref, ...), custom_call_target="tpu_custom_call" | custom-call | flops 60000000 | bytes 7168000 | tf_op jit(solution)/shard_map/propagate/pallas_call | solution.py:419
  46.7 4.6 %collective-permute-start.9 = (f32[3,8,128]{2,1,0:T(8,128)S(1)}, f32[3,8,128]{2,1,0:T(8,128)S(1)}, u32[]{:S(2)}, u32[]{:S(2)}) collective-permute-start(f32[3,8,128]{2,1,0:T(8,128)S(1)} %get-tuple-element.81), channel_id=1, source_target_pairs={{0,1},{1,0},{2,3},{3,2},{4,5},{5,4},{6,7},{7,6},{8,9},{9,8},{10,11... | collective-permute-start | bytes 36872 | tf_op jit(solution)/shard_map/ppermute | solution.py:70
  51.3 0.8 collective-permute-done.9
  52.3 2.5 %collective-permute-start.10 = (f32[3,8,128]{2,1,0:T(8,128)S(1)}, f32[3,8,128]{2,1,0:T(8,128)S(1)}, u32[]{:S(2)}, u32[]{:S(2)}) collective-permute-start(f32[3,8,128]{2,1,0:T(8,128)S(1)} %add.6.n_ref), channel_id=1, source_target_pairs={{0,2},{1,3},{2,0},{3,1},{4,6},{5,7},{6,4},{7,5},{8,10},{9,11},{10,... | collective-permute-start | bytes 36872 | tf_op jit(solution)/shard_map/ppermute | solution.py:70
  54.8 1.4 collective-permute-start.11
  56.2 1.3 collective-permute-start.12
  57.5 1.0 current.2.flow_ref
  58.5 1.4 collective-permute-done.13.edge_ref
  59.8 1.0 rims.1
  60.9 0.7 copy-done.28
  63.3 6.0 %all-to-all-start.1 = ((f32[16,96,128]{2,1,0:T(8,128)}), f32[16,96,128]{2,1,0:T(8,128)}, u32[]{:S(2)}, u32[]{:S(2)}) async-start(f32[16,96,128]{2,1,0:T(8,128)} %bitcast.14), calls=%async_computation.1 | async-start | bytes 1572864 | tf_op jit(solution)/shard_map/all_to_all | solution.py:617
  69.3 0.7 collective-permute-start.15
  70.0 0.9 copy-done.21
  71.1 0.6 copy-done.12
  71.7 0.7 copy-done.14
  72.4 11.5 %all-to-all-done.1.got_ref = f32[16,96,128]{2,1,0:T(8,128)} async-done(((f32[16,96,128]{2,1,0:T(8,128)}), f32[16,96,128]{2,1,0:T(8,128)}, u32[]{:S(2)}, u32[]{:S(2)}) %all-to-all-start.1) | async-done | bytes 786464 | tf_op jit(solution)/shard_map/all_to_all | solution.py:617
  84.0 0.9 copy-done.13
  84.9 1.3 update.2
  86.2 0.9 copy-done.6
  87.1 3.6 %all-to-all-start.2 = ((f32[16,96,128]{2,1,0:T(8,128)}), f32[16,96,128]{2,1,0:T(8,128)S(1)}, u32[]{:S(2)}, u32[]{:S(2)}) async-start(f32[16,96,128]{2,1,0:T(8,128)} %copy-done.6), calls=%async_computation.2 | async-start | bytes 1572864 | tf_op jit(solution)/shard_map/all_to_all | solution.py:617
  90.7 0.9 collective-permute-start.16
  91.6 0.7 copy-done.16
  92.3 11.4 %all-to-all-done.2 = f32[16,96,128]{2,1,0:T(8,128)S(1)} async-done(((f32[16,96,128]{2,1,0:T(8,128)}), f32[16,96,128]{2,1,0:T(8,128)S(1)}, u32[]{:S(2)}, u32[]{:S(2)}) %all-to-all-start.2) | async-done | bytes 786464 | tf_op jit(solution)/shard_map/all_to_all | solution.py:617
  104.0 0.7 collective-permute-start.19
  104.7 1.0 collective-permute-done.17.core_ref.acore_ref
  105.7 3.5 %collective-permute-start.18 = (f32[12,3,4,128]{3,2,1,0:T(4,128)S(1)}, f32[12,3,4,128]{3,2,1,0:T(4,128)S(1)}, u32[]{:S(2)}, u32[]{:S(2)}) collective-permute-start(f32[12,3,4,128]{3,2,1,0:T(4,128)S(1)} %corners.3), channel_id=1, source_target_pairs={{0,64},{1,65},{2,66},{3,67},{4,68},{5,69},{6,70},{7,71},{8,72},{9,... | collective-permute-start | bytes 221192 | tf_op jit(solution)/shard_map/ppermute | solution.py:70
  109.2 0.7 collective-permute-start.20
  109.9 1.1 copy-done.10
  111.0 1.0 copy-done.15
  112.0 1.0 copy-done.17
  113.4 5.8 %propagate.3 = (f32[10,4,88,128]{3,2,1,0:T(8,128)S(1)}, f32[3,8,128]{2,1,0:T(8,128)S(1)}, f32[16,3,72,128]{3,2,1,0:T(8,128)S(1)}) custom-call(f32[1]{0:T(128)S(6)} %copy.8.occ_ref, f32[18,4,88,128]{3,2,1,0:T(8,128)S(1)} %get-tuple-element.102.base_ref, f32[16,72,128]{2,1,0:T(8,128)S(1)} %get-tuple-element.103.v_ref, ...), custom_call_target="tpu_custom_call" | custom-call | flops 60000000 | bytes 7168000 | tf_op jit(solution)/shard_map/propagate/pallas_call | solution.py:419
  119.2 3.4 %collective-permute-start.21 = (f32[3,8,128]{2,1,0:T(8,128)S(1)}, f32[3,8,128]{2,1,0:T(8,128)S(1)}, u32[]{:S(2)}, u32[]{:S(2)}) collective-permute-start(f32[3,8,128]{2,1,0:T(8,128)S(1)} %get-tuple-element.110), channel_id=1, source_target_pairs={{0,1},{1,0},{2,3},{3,2},{4,5},{5,4},{6,7},{7,6},{8,9},{9,8},{10,11... | collective-permute-start | bytes 36872 | tf_op jit(solution)/shard_map/ppermute | solution.py:70
  122.6 0.8 collective-permute-done.21
  123.5 1.9 %collective-permute-start.25 = (f32[3,2,64,128]{3,2,1,0:T(8,128)S(1)}, f32[3,2,64,128]{3,2,1,0:T(8,128)S(1)}, u32[]{:S(2)}, u32[]{:S(2)}) collective-permute-start(f32[3,2,64,128]{3,2,1,0:T(8,128)S(1)} %get-tuple-element.117), channel_id=1, source_target_pairs={{0,64},{1,65},{2,66},{3,67},{4,68},{5,69},{6,70},{7,71},{8,72},{9,... | collective-permute-start | bytes 589832 | tf_op jit(solution)/shard_map/ppermute | solution.py:70
  125.4 1.1 collective-permute-start.22
  126.5 2.2 %collective-permute-start.23 = (f32[3,8,128]{2,1,0:T(8,128)S(1)}, f32[3,8,128]{2,1,0:T(8,128)S(1)}, u32[]{:S(2)}, u32[]{:S(2)}) collective-permute-start(f32[3,8,128]{2,1,0:T(8,128)S(1)} %add.7.n_ref), channel_id=1, source_target_pairs={{0,64},{1,65},{2,66},{3,67},{4,68},{5,69},{6,70},{7,71},{8,72},{9,... | collective-permute-start | bytes 36872 | tf_op jit(solution)/shard_map/ppermute | solution.py:70
  128.7 1.4 collective-permute-start.24
  130.1 1.0 current.3.flow_ref
  131.1 0.7 collective-permute-done.22.nchip_ref
  131.8 0.9 collective-permute-done.23.nhalf_ref
  132.8 0.8 collective-permute-done.24.nboth_ref
  133.6 1.1 weigh.3
  134.7 3.6 %all-to-all-start.3 = ((f32[16,96,128]{2,1,0:T(8,128)}), f32[16,96,128]{2,1,0:T(8,128)S(1)}, u32[]{:S(2)}, u32[]{:S(2)}) async-start(f32[16,96,128]{2,1,0:T(8,128)} %bitcast.8), calls=%async_computation.3 | async-start | bytes 1572864 | tf_op jit(solution)/shard_map/all_to_all | solution.py:617
  138.3 1.1 collective-permute-start.26
  139.5 1.5 copy-done.1
  141.1 7.2 %collective-permute-done.26.late_ref = f32[5,2,64,128]{3,2,1,0:T(8,128)S(1)} collective-permute-done((f32[5,2,64,128]{3,2,1,0:T(8,128)S(1)}, f32[5,2,64,128]{3,2,1,0:T(8,128)S(1)}, u32[]{:S(2)}, u32[]{:S(2)}) %collective-permute-start.26) | collective-permute-done | bytes 327712 | tf_op jit(solution)/shard_map/ppermute | solution.py:70
  148.3 1.3 finish.1
  149.6 2.2 %all-to-all-done.3.got_ref = f32[16,96,128]{2,1,0:T(8,128)S(1)} async-done(((f32[16,96,128]{2,1,0:T(8,128)}), f32[16,96,128]{2,1,0:T(8,128)S(1)}, u32[]{:S(2)}, u32[]{:S(2)}) %all-to-all-start.3) | async-done | bytes 786464 | tf_op jit(solution)/shard_map/all_to_all | solution.py:617
  151.8 0.7 update.3
  (82 shorter events, 3.5 us)
Async XLA Ops:
  0.6 9.0 %copy-start.4 = (f32[1,2,128,8,128]{4,3,2,1,0:T(8,128)S(1)}, f32[1,2,128,8,128]{4,3,2,1,0:T(8,128)}, u32[]{:S(2)}) copy-start(f32[1,2,128,8,128]{4,3,2,1,0:T(8,128)} %param.5) | copy-start | bytes 3145732
  0.6 9.0 %copy-start.11 = (f32[128,8,128]{2,1,0:T(8,128)S(1)}, f32[128,8,128]{2,1,0:T(8,128)}, u32[]{:S(2)}) copy-start(f32[128,8,128]{2,1,0:T(8,128)} %param.6) | copy-start | bytes 1572868
  0.7 0.9 copy-start.18
  1.6 8.1 %copy-start.19 = (f32[3,4,8,128]{3,2,1,0:T(8,128)S(1)}, f32[3,4,8,128]{3,2,1,0:T(8,128)}, u32[]{:S(2)}) copy-start(f32[3,4,8,128]{3,2,1,0:T(8,128)} %param.9) | copy-start | bytes 147460
  1.6 8.1 %copy-start.24 = (f32[3,4,8,128]{3,2,1,0:T(8,128)S(1)}, f32[3,4,8,128]{3,2,1,0:T(8,128)}, u32[]{:S(2)}) copy-start(f32[3,4,8,128]{3,2,1,0:T(8,128)} %param.8) | copy-start | bytes 147460
  2.5 21.5 %all-to-all-start = ((f32[16,96,128]{2,1,0:T(8,128)}), f32[16,96,128]{2,1,0:T(8,128)S(1)}, u32[]{:S(2)}, u32[]{:S(2)}) async-start(f32[16,96,128]{2,1,0:T(8,128)} %spread.1), calls=%async_computation | async-start | bytes 1572864 | tf_op jit(solution)/shard_map/all_to_all | solution.py:617
  11.0 0.6 copy-start.20
  11.7 4.0 %copy-start.25 = (f32[14,72,128]{2,1,0:T(8,128)}, f32[14,72,128]{2,1,0:T(8,128)S(1)}, u32[]{:S(2)}) copy-start(f32[14,72,128]{2,1,0:T(8,128)S(1)} %get-tuple-element.72) | copy-start | bytes 1548292
  11.7 4.0 %copy-start.26 = (f32[10,72,128]{2,1,0:T(8,128)}, f32[10,72,128]{2,1,0:T(8,128)S(1)}, u32[]{:S(2)}) copy-start(f32[10,72,128]{2,1,0:T(8,128)S(1)} %get-tuple-element.73) | copy-start | bytes 1105924
  11.7 29.2 %copy-start.2 = (f32[8,72,128]{2,1,0:T(8,128)}, f32[8,72,128]{2,1,0:T(8,128)S(1)}, u32[]{:S(2)}) copy-start(f32[8,72,128]{2,1,0:T(8,128)S(1)} %get-tuple-element.74.weight_ref) | copy-start | bytes 884740
  11.7 4.0 %collective-permute-start = (f32[14,72,128]{2,1,0:T(8,128)S(1)}, f32[14,72,128]{2,1,0:T(8,128)S(1)}, u32[]{:S(2)}, u32[]{:S(2)}) collective-permute-start(f32[14,72,128]{2,1,0:T(8,128)S(1)} %get-tuple-element.65), channel_id=1, source_target_pairs={{0,1},{1,0},{2,3},{3,2},{4,5},{5,4},{6,7},{7,6},{8,9},{9,8},{10,11... | collective-permute-start | bytes 1548296 | tf_op jit(solution)/shard_map/ppermute | solution.py:70
  11.7 19.6 %collective-permute-start.3 = (f32[8,2,72,128]{3,2,1,0:T(8,128)}, f32[8,2,72,128]{3,2,1,0:T(8,128)S(1)}, u32[]{:S(2)}, u32[]{:S(2)}) collective-permute-start(f32[8,2,72,128]{3,2,1,0:T(8,128)} %get-tuple-element.69), channel_id=1, source_target_pairs={{0,64},{1,65},{2,66},{3,67},{4,68},{5,69},{6,70},{7,71},{8,72},{9,... | collective-permute-start | bytes 1769480 | tf_op jit(solution)/shard_map/ppermute | solution.py:70
  24.2 1.8 %collective-permute-start.1 = (f32[4,3,64,128]{3,2,1,0:T(8,128)S(1)}, f32[4,3,64,128]{3,2,1,0:T(8,128)S(1)}, u32[]{:S(2)}, u32[]{:S(2)}) collective-permute-start(f32[4,3,64,128]{3,2,1,0:T(8,128)S(1)} %get-tuple-element.68), channel_id=1, source_target_pairs={{0,1},{1,0},{2,3},{3,2},{4,5},{5,4},{6,7},{7,6},{8,9},{9,8},{10,11... | collective-permute-start | bytes 1179656 | tf_op jit(solution)/shard_map/ppermute | solution.py:70
  24.3 16.1 %collective-permute-start.4 = (f32[14,72,128]{2,1,0:T(8,128)}, f32[14,72,128]{2,1,0:T(8,128)S(1)}, u32[]{:S(2)}, u32[]{:S(2)}) collective-permute-start(f32[14,72,128]{2,1,0:T(8,128)} %copy-done.25), channel_id=1, source_target_pairs={{1,2},{2,1},{5,6},{6,5},{9,10},{10,9},{13,14},{14,13},{17,18},{18,... | collective-permute-start | bytes 1548296 | tf_op jit(solution)/shard_map/ppermute | solution.py:70
  26.0 6.7 %collective-permute-start.2 = (f32[12,3,4,128]{3,2,1,0:T(4,128)S(1)}, f32[12,3,4,128]{3,2,1,0:T(4,128)S(1)}, u32[]{:S(2)}, u32[]{:S(2)}) collective-permute-start(f32[12,3,4,128]{3,2,1,0:T(4,128)S(1)} %corners.2), channel_id=1, source_target_pairs={{0,64},{1,65},{2,66},{3,67},{4,68},{5,69},{6,70},{7,71},{8,72},{9,... | collective-permute-start | bytes 221192 | tf_op jit(solution)/shard_map/ppermute | solution.py:70
  30.0 10.9 %collective-permute-start.7 = (f32[4,3,64,128]{3,2,1,0:T(8,128)S(1)}, f32[4,3,64,128]{3,2,1,0:T(8,128)S(1)}, u32[]{:S(2)}, u32[]{:S(2)}) collective-permute-start(f32[4,3,64,128]{3,2,1,0:T(8,128)S(1)} %get-tuple-element.79), channel_id=1, source_target_pairs={{1,2},{2,1},{5,6},{6,5},{9,10},{10,9},{13,14},{14,13},{17,18},{18,... | collective-permute-start | bytes 1179656 | tf_op jit(solution)/shard_map/ppermute | solution.py:70
  30.6 9.7 %collective-permute-start.6 = (f32[10,72,128]{2,1,0:T(8,128)}, f32[10,72,128]{2,1,0:T(8,128)S(1)}, u32[]{:S(2)}, u32[]{:S(2)}) collective-permute-start(f32[10,72,128]{2,1,0:T(8,128)} %copy-done.26), channel_id=1, source_target_pairs={{1,66},{2,65},{5,70},{6,69},{9,74},{10,73},{13,78},{14,77},{17,82}... | collective-permute-start | bytes 1105928 | tf_op jit(solution)/shard_map/ppermute | solution.py:70
  32.7 7.7 %collective-permute-start.5 = (f32[10,72,128]{2,1,0:T(8,128)S(1)}, f32[10,72,128]{2,1,0:T(8,128)S(1)}, u32[]{:S(2)}, u32[]{:S(2)}) collective-permute-start(f32[10,72,128]{2,1,0:T(8,128)S(1)} %lend.1), channel_id=1, source_target_pairs={{0,1},{1,0},{2,3},{3,2},{4,5},{5,4},{6,7},{7,6},{8,9},{9,8},{10,11... | collective-permute-start | bytes 1105928 | tf_op jit(solution)/shard_map/ppermute | solution.py:70
  39.1 1.8 %collective-permute-start.8 = (f32[4,3,4,128]{3,2,1,0:T(4,128)S(1)}, f32[4,3,4,128]{3,2,1,0:T(4,128)S(1)}, u32[]{:S(2)}, u32[]{:S(2)}) collective-permute-start(f32[4,3,4,128]{3,2,1,0:T(4,128)S(1)} %get-tuple-element.80), channel_id=1, source_target_pairs={{1,66},{2,65},{5,70},{6,69},{9,74},{10,73},{13,78},{14,77},{17,82}... | collective-permute-start | bytes 73736 | tf_op jit(solution)/shard_map/ppermute | solution.py:70
  46.7 5.5 %collective-permute-start.9 = (f32[3,8,128]{2,1,0:T(8,128)S(1)}, f32[3,8,128]{2,1,0:T(8,128)S(1)}, u32[]{:S(2)}, u32[]{:S(2)}) collective-permute-start(f32[3,8,128]{2,1,0:T(8,128)S(1)} %get-tuple-element.81), channel_id=1, source_target_pairs={{0,1},{1,0},{2,3},{3,2},{4,5},{5,4},{6,7},{7,6},{8,9},{9,8},{10,11... | collective-permute-start | bytes 36872 | tf_op jit(solution)/shard_map/ppermute | solution.py:70
  52.2 7.6 %collective-permute-start.13 = (f32[8,4,8,128]{3,2,1,0:T(8,128)S(1)}, f32[8,4,8,128]{3,2,1,0:T(8,128)S(1)}, u32[]{:S(2)}, u32[]{:S(2)}) collective-permute-start(f32[8,4,8,128]{3,2,1,0:T(8,128)S(1)} %edges.1), channel_id=1, source_target_pairs={{0,64},{1,65},{2,66},{3,67},{4,68},{5,69},{6,70},{7,71},{8,72},{9,... | collective-permute-start | bytes 393224 | tf_op jit(solution)/shard_map/ppermute | solution.py:70
  52.3 9.3 %collective-permute-start.10 = (f32[3,8,128]{2,1,0:T(8,128)S(1)}, f32[3,8,128]{2,1,0:T(8,128)S(1)}, u32[]{:S(2)}, u32[]{:S(2)}) collective-permute-start(f32[3,8,128]{2,1,0:T(8,128)S(1)} %add.6.n_ref), channel_id=1, source_target_pairs={{0,2},{1,3},{2,0},{3,1},{4,6},{5,7},{6,4},{7,5},{8,10},{9,11},{10,... | collective-permute-start | bytes 36872 | tf_op jit(solution)/shard_map/ppermute | solution.py:70
  54.8 6.8 %collective-permute-start.11 = (f32[3,8,128]{2,1,0:T(8,128)S(1)}, f32[3,8,128]{2,1,0:T(8,128)S(1)}, u32[]{:S(2)}, u32[]{:S(2)}) collective-permute-start(f32[3,8,128]{2,1,0:T(8,128)S(1)} %add.6.n_ref), channel_id=1, source_target_pairs={{0,64},{1,65},{2,66},{3,67},{4,68},{5,69},{6,70},{7,71},{8,72},{9,... | collective-permute-start | bytes 36872 | tf_op jit(solution)/shard_map/ppermute | solution.py:70
  56.2 5.5 %collective-permute-start.12 = (f32[3,8,128]{2,1,0:T(8,128)S(1)}, f32[3,8,128]{2,1,0:T(8,128)S(1)}, u32[]{:S(2)}, u32[]{:S(2)}) collective-permute-start(f32[3,8,128]{2,1,0:T(8,128)S(1)} %add.6.n_ref), channel_id=1, source_target_pairs={{0,66},{1,67},{2,64},{3,65},{4,70},{5,71},{6,68},{7,69},{8,74},{9,... | collective-permute-start | bytes 36872 | tf_op jit(solution)/shard_map/ppermute | solution.py:70
  60.9 0.7 copy-start.28
  61.6 0.8 copy-start.7
  61.6 1.0 copy-start.9
  61.6 1.1 copy-start.27
  61.6 10.8 %collective-permute-start.14 = (f32[20,72,128]{2,1,0:T(8,128)}, f32[20,72,128]{2,1,0:T(8,128)S(1)}, u32[]{:S(2)}, u32[]{:S(2)}) collective-permute-start(f32[20,72,128]{2,1,0:T(8,128)} %get-tuple-element.92), channel_id=1, source_target_pairs={{0,1},{1,0},{2,3},{3,2},{4,5},{5,4},{6,7},{7,6},{8,9},{9,8},{10,11... | collective-permute-start | bytes 2211848 | tf_op jit(solution)/shard_map/ppermute | solution.py:70
  62.4 0.9 copy-start.5
  63.3 20.6 %all-to-all-start.1 = ((f32[16,96,128]{2,1,0:T(8,128)}), f32[16,96,128]{2,1,0:T(8,128)}, u32[]{:S(2)}, u32[]{:S(2)}) async-start(f32[16,96,128]{2,1,0:T(8,128)} %bitcast.14), calls=%async_computation.1 | async-start | bytes 1572864 | tf_op jit(solution)/shard_map/all_to_all | solution.py:617
  69.3 2.4 %collective-permute-start.15 = (f32[10,72,128]{2,1,0:T(8,128)}, f32[10,72,128]{2,1,0:T(8,128)S(1)}, u32[]{:S(2)}, u32[]{:S(2)}) collective-permute-start(f32[10,72,128]{2,1,0:T(8,128)} %copy-done.28), channel_id=1, source_target_pairs={{1,2},{2,1},{5,6},{6,5},{9,10},{10,9},{13,14},{14,13},{17,18},{18,... | collective-permute-start | bytes 1105928 | tf_op jit(solution)/shard_map/ppermute | solution.py:70
  70.0 0.9 copy-start.21
  71.1 0.6 copy-start.12
  71.7 0.7 copy-start.14
  84.0 0.9 copy-start.13
  84.9 25.0 %copy-start.3 = (f32[8,72,128]{2,1,0:T(8,128)S(1)}, f32[8,72,128]{2,1,0:T(8,128)}, u32[]{:S(2)}) copy-start(f32[8,72,128]{2,1,0:T(8,128)} %copy-done.2) | copy-start | bytes 884740
  84.9 25.0 %copy-start.8 = (f32[8,2,72,128]{3,2,1,0:T(8,128)S(1)}, f32[8,2,72,128]{3,2,1,0:T(8,128)}, u32[]{:S(2)}) copy-start(f32[8,2,72,128]{3,2,1,0:T(8,128)} %copy-done.7) | copy-start | bytes 1769476
  86.2 0.9 copy-start.6
  87.1 26.3 %copy-start.22 = (f32[2,96,128]{2,1,0:T(8,128)}, f32[2,96,128]{2,1,0:T(8,128)S(1)}, u32[]{:S(2)}) copy-start(f32[2,96,128]{2,1,0:T(8,128)S(1)} %get-tuple-element.122.rows_ref) | copy-start | bytes 294916
  87.1 16.7 %all-to-all-start.2 = ((f32[16,96,128]{2,1,0:T(8,128)}), f32[16,96,128]{2,1,0:T(8,128)S(1)}, u32[]{:S(2)}, u32[]{:S(2)}) async-start(f32[16,96,128]{2,1,0:T(8,128)} %copy-done.6), calls=%async_computation.2 | async-start | bytes 1572864 | tf_op jit(solution)/shard_map/all_to_all | solution.py:617
  90.7 0.9 collective-permute-start.16
  91.6 0.7 copy-start.16
  103.9 1.8 %collective-permute-start.17 = (f32[4,3,64,128]{3,2,1,0:T(8,128)S(1)}, f32[4,3,64,128]{3,2,1,0:T(8,128)S(1)}, u32[]{:S(2)}, u32[]{:S(2)}) collective-permute-start(f32[4,3,64,128]{3,2,1,0:T(8,128)S(1)} %get-tuple-element.107), channel_id=1, source_target_pairs={{0,1},{1,0},{2,3},{3,2},{4,5},{5,4},{6,7},{7,6},{8,9},{9,8},{10,11... | collective-permute-start | bytes 1179656 | tf_op jit(solution)/shard_map/ppermute | solution.py:70
  104.0 9.4 %collective-permute-start.19 = (f32[4,3,64,128]{3,2,1,0:T(8,128)S(1)}, f32[4,3,64,128]{3,2,1,0:T(8,128)S(1)}, u32[]{:S(2)}, u32[]{:S(2)}) collective-permute-start(f32[4,3,64,128]{3,2,1,0:T(8,128)S(1)} %get-tuple-element.108), channel_id=1, source_target_pairs={{1,2},{2,1},{5,6},{6,5},{9,10},{10,9},{13,14},{14,13},{17,18},{18,... | collective-permute-start | bytes 1179656 | tf_op jit(solution)/shard_map/ppermute | solution.py:70
  105.7 7.7 %collective-permute-start.18 = (f32[12,3,4,128]{3,2,1,0:T(4,128)S(1)}, f32[12,3,4,128]{3,2,1,0:T(4,128)S(1)}, u32[]{:S(2)}, u32[]{:S(2)}) collective-permute-start(f32[12,3,4,128]{3,2,1,0:T(4,128)S(1)} %corners.3), channel_id=1, source_target_pairs={{0,64},{1,65},{2,66},{3,67},{4,68},{5,69},{6,70},{7,71},{8,72},{9,... | collective-permute-start | bytes 221192 | tf_op jit(solution)/shard_map/ppermute | solution.py:70
  109.2 4.1 %collective-permute-start.20 = (f32[4,3,4,128]{3,2,1,0:T(4,128)S(1)}, f32[4,3,4,128]{3,2,1,0:T(4,128)S(1)}, u32[]{:S(2)}, u32[]{:S(2)}) collective-permute-start(f32[4,3,4,128]{3,2,1,0:T(4,128)S(1)} %get-tuple-element.109), channel_id=1, source_target_pairs={{1,66},{2,65},{5,70},{6,69},{9,74},{10,73},{13,78},{14,77},{17,82}... | collective-permute-start | bytes 73736 | tf_op jit(solution)/shard_map/ppermute | solution.py:70
  109.9 1.1 copy-start.10
  111.0 1.0 copy-start.15
  112.0 1.0 copy-start.17
  119.2 11.9 %copy-start = (f32[16,3,72,128]{3,2,1,0:T(8,128)}, f32[16,3,72,128]{3,2,1,0:T(8,128)S(1)}, u32[]{:S(2)}) copy-start(f32[16,3,72,128]{3,2,1,0:T(8,128)S(1)} %get-tuple-element.113.field_ref) | copy-start | bytes 5308420
  119.2 4.3 %collective-permute-start.21 = (f32[3,8,128]{2,1,0:T(8,128)S(1)}, f32[3,8,128]{2,1,0:T(8,128)S(1)}, u32[]{:S(2)}, u32[]{:S(2)}) collective-permute-start(f32[3,8,128]{2,1,0:T(8,128)S(1)} %get-tuple-element.110), channel_id=1, source_target_pairs={{0,1},{1,0},{2,3},{3,2},{4,5},{5,4},{6,7},{7,6},{8,9},{9,8},{10,11... | collective-permute-start | bytes 36872 | tf_op jit(solution)/shard_map/ppermute | solution.py:70
  123.5 11.2 %collective-permute-start.25 = (f32[3,2,64,128]{3,2,1,0:T(8,128)S(1)}, f32[3,2,64,128]{3,2,1,0:T(8,128)S(1)}, u32[]{:S(2)}, u32[]{:S(2)}) collective-permute-start(f32[3,2,64,128]{3,2,1,0:T(8,128)S(1)} %get-tuple-element.117), channel_id=1, source_target_pairs={{0,64},{1,65},{2,66},{3,67},{4,68},{5,69},{6,70},{7,71},{8,72},{9,... | collective-permute-start | bytes 589832 | tf_op jit(solution)/shard_map/ppermute | solution.py:70
  125.4 6.4 %collective-permute-start.22 = (f32[3,8,128]{2,1,0:T(8,128)S(1)}, f32[3,8,128]{2,1,0:T(8,128)S(1)}, u32[]{:S(2)}, u32[]{:S(2)}) collective-permute-start(f32[3,8,128]{2,1,0:T(8,128)S(1)} %add.7.n_ref), channel_id=1, source_target_pairs={{0,2},{1,3},{2,0},{3,1},{4,6},{5,7},{6,4},{7,5},{8,10},{9,11},{10,... | collective-permute-start | bytes 36872 | tf_op jit(solution)/shard_map/ppermute | solution.py:70
  126.5 6.3 %collective-permute-start.23 = (f32[3,8,128]{2,1,0:T(8,128)S(1)}, f32[3,8,128]{2,1,0:T(8,128)S(1)}, u32[]{:S(2)}, u32[]{:S(2)}) collective-permute-start(f32[3,8,128]{2,1,0:T(8,128)S(1)} %add.7.n_ref), channel_id=1, source_target_pairs={{0,64},{1,65},{2,66},{3,67},{4,68},{5,69},{6,70},{7,71},{8,72},{9,... | collective-permute-start | bytes 36872 | tf_op jit(solution)/shard_map/ppermute | solution.py:70
  128.7 4.9 %collective-permute-start.24 = (f32[3,8,128]{2,1,0:T(8,128)S(1)}, f32[3,8,128]{2,1,0:T(8,128)S(1)}, u32[]{:S(2)}, u32[]{:S(2)}) collective-permute-start(f32[3,8,128]{2,1,0:T(8,128)S(1)} %add.7.n_ref), channel_id=1, source_target_pairs={{0,66},{1,67},{2,64},{3,65},{4,70},{5,71},{6,68},{7,69},{8,74},{9,... | collective-permute-start | bytes 36872 | tf_op jit(solution)/shard_map/ppermute | solution.py:70
  131.1 8.4 %copy-start.23 = (f32[2,96,128]{2,1,0:T(8,128)S(1)}, f32[2,96,128]{2,1,0:T(8,128)}, u32[]{:S(2)}) copy-start(f32[2,96,128]{2,1,0:T(8,128)} %copy-done.22) | copy-start | bytes 294916
  134.7 17.1 %all-to-all-start.3 = ((f32[16,96,128]{2,1,0:T(8,128)}), f32[16,96,128]{2,1,0:T(8,128)S(1)}, u32[]{:S(2)}, u32[]{:S(2)}) async-start(f32[16,96,128]{2,1,0:T(8,128)} %bitcast.8), calls=%async_computation.3 | async-start | bytes 1572864 | tf_op jit(solution)/shard_map/all_to_all | solution.py:617
  138.3 9.9 %collective-permute-start.26 = (f32[5,2,64,128]{3,2,1,0:T(8,128)S(1)}, f32[5,2,64,128]{3,2,1,0:T(8,128)S(1)}, u32[]{:S(2)}, u32[]{:S(2)}) collective-permute-start(f32[5,2,64,128]{3,2,1,0:T(8,128)S(1)} %get-tuple-element.120), channel_id=1, source_target_pairs={{0,64},{1,65},{2,66},{3,67},{4,68},{5,69},{6,70},{7,71},{8,72},{9,... | collective-permute-start | bytes 983048 | tf_op jit(solution)/shard_map/ppermute | solution.py:70
  139.4 1.5 copy-start.1
